TPU v7x, 32 devices: a whole 2x2x4 slice. The times are simulated.
32 devices in a mesh: tr: 16 (over z, y, x), ct: 2 (over core).
Axes of the slice: x: 2, y: 2, z: 4, core: 2. Of those that a mesh axis runs over, the one named last changes fastest.
Arguments:
- amplitudes: bfloat16 [8, 1024, 2, 1024], P(None, 'tr', None, 'ct'), may hold values from -6 to 6
- cycle_integrals: bfloat16 [2, 1024, 1, 1024], P(None, 'ct', None, 'tr'), may hold values from -0.125 to 0.125
- pair_live: int32 [8, 16], replicated, may hold values 0 or 1
Outputs:
- permuted: bfloat16 [8, 1024, 1, 1024], P('ct', 'tr')
All inputs are finite; a program needn't handle non-finite values.
Results may differ from a plain program's by a relative error of at most 0.017.
Values may be sent and summed in bfloat16 or wider, within the bound.
No kernel may reach another device: no remote copies, remote signals or barrier semaphores. Data moves between devices by JAX's collectives and lax.ppermute only.
A program may use at most 64 MiB of HBM per device.

v0:
```python
import jax
import jax.numpy as jnp
from jax import lax
from jax.sharding import PartitionSpec as P


def per_device(amplitudes, cycle_integrals, pair_live):
    tile_size = amplitudes.shape[1]
    block_cols = amplitudes.shape[3]
    occ_k = amplitudes.shape[2]
    row_index = lax.axis_index("tr")
    col_index = lax.axis_index("ct")
    row_live = lax.dynamic_slice_in_dim(pair_live, row_index, 1, 1).astype(jnp.bfloat16)
    col_full = jnp.repeat(pair_live[:occ_k], tile_size, axis=1)
    col_live = lax.dynamic_slice_in_dim(col_full, col_index * block_cols, block_cols, 1).astype(
        jnp.bfloat16
    )
    masked = amplitudes * row_live[:, :, None, None] * col_live[None, None, :, :]
    partial_value = jnp.einsum(
        "iakc,kcjb->iajb",
        masked,
        lax.all_gather(cycle_integrals, "tr", axis=3, tiled=True),
        preferred_element_type=jnp.float32,
    )
    moved_parts = lax.all_to_all(
        partial_value.astype(jnp.bfloat16), "tr", split_axis=3, concat_axis=1, tiled=True
    )
    moved = lax.psum_scatter(
        moved_parts.astype(jnp.float32).astype(jnp.bfloat16), "ct", scatter_dimension=0, tiled=True
    )
    return jnp.transpose(moved, (0, 3, 2, 1))


def solution(mesh):
    return jax.shard_map(
        per_device,
        mesh=mesh,
        in_specs=(P(None, "tr", None, "ct"), P(None, "ct", None, "tr"), P()),
        out_specs=P("ct", "tr", None, None),
        check_vma=False,
    )
```

profile of v0, /device:TPU:0, one launch (start us, length us, event | category | flops | bytes accessed | tf_op | source)
XLA Modules:
  0.0 138.4 jit_solution(5978201409989466977)
XLA Ops:
  6.5 0.0 all-gather.2.cloned.1.call-start
  6.5 1.7 %copy.7 = bf16[2,512,1,64]{1,0,2,3:T(2,128)(2,1)} copy(bf16[2,512,1,64]{1,3,2,0:T(8,128)(2,1)} %param.4) | data formatting | bytes 262144 | tf_op args[1]
  8.2 0.0 all-gather.2.cloned.1.call-update
  8.3 0.0 reduce-scatter.2.cloned.1.call-start
  8.3 0.7 slice.3
  9.0 0.9 fusion.8
  9.9 0.1 broadcast_in_dim.2
  9.9 0.1 reshape.10
  10.0 3.3 %multiply_multiply_fusion = bf16[8,64,2,512]{3,2,1,0:T(2,128)(2,1)} fusion(bf16[8,64,2,512]{3,2,1,0:T(2,128)(2,1)} %param.3, bf16[8]{0:T(256)(128)(2,1)S(1)} %fusion.8, bf16[2,512]{1,0:T(2,128)(2,1)S(1)} %dynamic-slice_convert_fusion), kind=kLoop, calls=%fused_computation.5 | loop fusion | flops 1048576 | bytes 2099216 | tf_op jit(solution)/shard_map/mul | solution.py:18
  13.3 60.2 %all-gather.2.cloned.1.call-done = bf16[2,512,1,1024]{1,0,2,3:T(2,128)(2,1)} async-done(((bf16[2,512,1,64]{1,0,2,3:T(2,128)(2,1)}), bf16[2,512,1,1024]{1,0,2,3:T(2,128)(2,1)}) %all-gather.2.cloned.1.call-update) | async-done | bytes 2097168 | tf_op jit(solution)/shard_map/all_gather | solution.py:22
  73.6 4.7 %copy.8 = bf16[2,512,1,1024]{3,1,0,2:T(8,128)(2,1)S(1)} copy(bf16[2,512,1,1024]{1,0,2,3:T(2,128)(2,1)} %all-gather.2.cloned.1.call-done) | data formatting | bytes 4194304 | tf_op jit(solution)/shard_map/all_gather | solution.py:22
  78.3 2.5 %fusion.4 = bf16[8,64,1,1024]{3,1,0,2:T(8,128)(2,1)S(1)} fusion(bf16[2,512,1,1024]{3,1,0,2:T(8,128)(2,1)S(1)} %copy.8, bf16[8,64,2,512]{3,2,1,0:T(2,128)(2,1)} %multiply_multiply_fusion), kind=kOutput, calls=%fused_computation.3 | convolution fusion | flops 1074266112 | bytes 4194304 | tf_op jit(solution)/shard_map/iakc,kcjb->iajb/dot_general | solution.py:19
  80.8 1.7 %copy.10 = bf16[8,64,1,1024]{1,0,2,3:T(8,128)(2,1)S(1)} copy(bf16[8,64,1,1024]{3,1,0,2:T(8,128)(2,1)S(1)} %fusion.4) | data formatting | bytes 2097152 | tf_op jit(solution)/shard_map/convert_element_type | solution.py:26
  82.5 1.5 %reshape.15 = bf16[16,2,16384]{2,1,0:T(2,128)(2,1)S(1)} reshape(bf16[1024,1,8,64]{3,2,1,0:T(8,128)(2,1)S(1)} %bitcast.25) | data formatting | bytes 2097152
  83.9 30.0 %all_to_all.18 = bf16[16,2,16384]{2,1,0:T(2,128)(2,1)} all-to-all(bf16[16,2,16384]{2,1,0:T(2,128)(2,1)S(1)} %reshape.15), channel_id=1, replica_groups=mesh['tr'=16,'ct'=2] {'tr'}, dimensions={0} | all-to-all | bytes 2097152 | tf_op jit(solution)/shard_map/all_to_all | solution.py:25
  113.9 3.8 %reshape.16 = bf16[1024,1,8,64]{3,2,1,0:T(8,128)(2,1)S(1)} reshape(bf16[16,2,16384]{2,1,0:T(2,128)(2,1)} %all_to_all.18) | data formatting | bytes 2097152
  117.7 2.7 %copy.11 = bf16[8,16,64,1,64]{2,1,4,0,3:T(8,128)(2,1)} copy(bf16[8,16,64,1,64]{2,0,4,1,3:T(8,128)(2,1)S(1)} %bitcast.26) | data formatting | bytes 2097152 | tf_op jit(solution)/shard_map/all_to_all | solution.py:25
  120.4 4.1 %all_to_all.16 = bf16[8,1024,1,64]{1,3,2,0:T(8,128)(2,1)} reshape(bf16[8,16,64,1,64]{2,1,4,0,3:T(8,128)(2,1)} %copy.11) | data formatting | bytes 2097152 | tf_op jit(solution)/shard_map/all_to_all | solution.py:25
  124.5 0.0 reduce-scatter.2.cloned.1.call-update
  124.6 7.0 %reduce-scatter.2.cloned.1.call-done = bf16[4,1024,1,64]{1,3,2,0:T(8,128)(2,1)} async-done(((bf16[8,1024,1,64]{1,3,2,0:T(8,128)(2,1)}), bf16[4,1024,1,64]{1,3,2,0:T(8,128)(2,1)}) %reduce-scatter.2.cloned.1.call-update) | async-done | bytes 524304 | tf_op jit(solution)/shard_map/reduce_scatter | solution.py:28
  (1 shorter events, 0.0 us)
Async XLA Ops:
  6.5 67.0 %all-gather.2.cloned.1.call-start = ((), (), s32[]{:S(2)}) async-start(), calls=%async_computation.2 | async-start | bytes 2228224 | tf_op jit(solution)/shard_map/all_gather | solution.py:22
  8.3 123.3 %reduce-scatter.2.cloned.1.call-start = ((), (), s32[]{:S(2)}) async-start(), calls=%async_computation.3 | async-start | bytes 1572864 | tf_op jit(solution)/shard_map/reduce_scatter | solution.py:28
Sparse Core Ops, SparseCore 0:
  10.1 63.3 all-gather.1
  124.7 6.8 reduce-scatter.1
where the time goes:
time: 139 us; the launch traced here: 138 us
  waiting for transfers between devices  67.3 us (48%)
  blocking collectives  30 us (22%)
  local copies, waits for them, and re-layouts  21 us (15%)
  between operations  13.5 us (10%)
  other arithmetic  4.18 us (3%)
  matrix products  2.48 us (2%)
    all_gather x1, waiting for transfers between devices, per_device(): lax.all_gather(cycle_integrals, 'tr', axis=3, tiled=True)  60.2 us
    all_to_all x1, blocking collectives, per_device(): lax.all_to_all(partial_value.astype(jnp.bfloat16), 'tr', split_axis=3, co...  30 us
    reduce_scatter x1, waiting for transfers between devices, per_device(): lax.psum_scatter(moved_parts.astype(jnp.float32).astype(jnp.bfloat16), 'c...  7.01 us
    unnamed x3, local copies, waits for them, and re-layouts  6.92 us
    all_to_all x2, local copies, waits for them, and re-layouts, per_device(): lax.all_to_all(partial_value.astype(jnp.bfloat16), 'tr', split_axis=3, co...  6.81 us
    all_gather x1, local copies, waits for them, and re-layouts, per_device(): lax.all_gather(cycle_integrals, 'tr', axis=3, tiled=True)  4.73 us
    mul x1, other arithmetic, per_device(): amplitudes * row_live[:, :, None, None] * col_live[None, None, :, :]  3.3 us
  transfers between devices with their start and end apart: 2, of which 2 were waited for; matrix products, arithmetic and copies ran while one was open for 4% of the time, Pallas kernels for 0%

commit v1 on v0

v1 whole, which is shorter than its diff:
```python
import functools

import jax
import jax.numpy as jnp
from jax import lax
from jax.experimental import pallas as pl
from jax.experimental.pallas import tpu as pltpu
from jax.sharding import PartitionSpec as P

F32 = jnp.float32
VMEM = pl.BlockSpec(memory_space=pltpu.VMEM)
SMEM = pl.BlockSpec(memory_space=pltpu.SMEM)
PARAMS = pltpu.CompilerParams(vmem_limit_bytes=48 * 1024 * 1024)


def partials_kernel(n_ct, place, live, *refs):
    mine, theirs, tiles, outs = refs[0], refs[1], refs[2:-n_ct], refs[-n_ct:]
    tr, ct = place[0], place[1]
    n_i, n_k, vt, cols = mine.shape
    n_local = n_i // n_ct
    first = (tr % 2) == 0
    even = (tr // 2) * 2
    col_tile = lax.broadcasted_iota(jnp.int32, (1, cols), 1) // vt
    col_masks = []
    for k in range(n_k):
        mask = jnp.zeros((1, cols), F32)
        for t in range(cols // vt):
            kept = live[k, ct * (cols // vt) + t].astype(F32)
            mask = jnp.where(col_tile == t, kept, mask)
        col_masks.append(mask.astype(jnp.bfloat16))
    lhs = []
    for k in range(n_k):
        stacked = jnp.concatenate([ref[s, k] for ref in tiles for s in range(ref.shape[0])], axis=0)
        lhs.append(stacked * col_masks[k])
    half = lax.broadcasted_iota(jnp.int32, (1, 2 * vt), 1) < vt
    entries = [(e, local) for e in range(n_ct) for local in range(n_local)]
    for at in range(0, n_i, 2):
        total = None
        for k in range(n_k):
            rows = []
            for e, local in entries[at : at + 2]:
                i = (ct ^ e) * n_local + local
                own, other = mine[i, k], theirs[i, k]
                rows += [jnp.where(first, own, other), jnp.where(first, other, own)]
            term = lax.dot_general(
                lhs[k],
                jnp.concatenate(rows, axis=0),
                (((1,), (1,)), ((), ())),
                preferred_element_type=F32,
            )
            total = term if total is None else total + term
        for n, (e, local) in enumerate(entries[at : at + 2]):
            i = (ct ^ e) * n_local + local
            row_mask = jnp.where(half, live[i, even].astype(F32), live[i, even + 1].astype(F32))
            outs[e][local] = (total[:, n * 2 * vt : (n + 1) * 2 * vt] * row_mask).astype(outs[e].dtype)


def add_kernel(n_parts, *refs):
    parts, outs = refs[:n_parts], refs[n_parts:]
    vt = outs[0].shape[1]
    for d, out in enumerate(outs):
        total = parts[0][:, pl.ds(d * vt, vt)].astype(F32)
        for part in parts[1:]:
            total += part[:, pl.ds(d * vt, vt)].astype(F32)
        out[...] = total.astype(out.dtype)


def place_kernel(offsets, place, *refs):
    parts, out = refs[:-1], refs[-1]
    width = parts[0].shape[2]
    pair = place[0] // 2
    for d, part in zip(offsets, parts, strict=True):
        at = pl.multiple_of((pair ^ (d // 2)) * width, width)
        out[:, :, pl.ds(at, width)] = part[...]


def per_device(n_tr, n_ct, amplitudes, cycle_integrals, pair_live):
    n_i, vt, n_k, cols = amplitudes.shape
    n_j = cycle_integrals.shape[2]
    n_local = n_i // n_ct
    tr, ct = lax.axis_index("tr"), lax.axis_index("ct")
    place = jnp.stack([tr, ct]).astype(jnp.int32)

    def swap(value, d, axis="tr", size=n_tr):
        return lax.ppermute(value, axis, [(n, n ^ d) for n in range(size)])

    own_w = jnp.transpose(cycle_integrals, (2, 0, 3, 1))
    other = swap(amplitudes, 1)
    far = list(range(4, n_tr, 4))
    arrived = [swap(own_w, d) for d in far]
    near = swap(own_w, 2)
    forwarded = [swap(w, 2) for w in arrived]
    tiles = [own_w, near] + [w for both in zip(arrived, forwarded) for w in both]
    offsets = [0, 2] + [d + y for d in far for y in (0, 2)]

    rows = len(tiles) * vt
    partials = pl.pallas_call(
        functools.partial(partials_kernel, n_ct),
        out_shape=[jax.ShapeDtypeStruct((n_local, rows, 2 * vt), jnp.bfloat16)] * n_ct,
        in_specs=[SMEM, SMEM] + [VMEM] * (2 + len(tiles)),
        out_specs=[VMEM] * n_ct,
        compiler_params=PARAMS,
    )(place, pair_live, jnp.transpose(amplitudes, (0, 2, 1, 3)), jnp.transpose(other, (0, 2, 1, 3)), *tiles)

    parts = [partials[0]] + [swap(partials[e], e, "ct", n_ct) for e in range(1, n_ct)]
    blocks = pl.pallas_call(
        functools.partial(add_kernel, n_ct),
        out_shape=[jax.ShapeDtypeStruct((n_local, vt, 2 * vt), jnp.bfloat16)] * len(tiles),
        in_specs=[VMEM] * n_ct,
        out_specs=[VMEM] * len(tiles),
        compiler_params=PARAMS,
    )(*parts)
    moved = [b if d == 0 else swap(b, d) for d, b in zip(offsets, blocks)]
    result = pl.pallas_call(
        functools.partial(place_kernel, offsets),
        out_shape=jax.ShapeDtypeStruct((n_local, vt, n_tr * vt), jnp.bfloat16),
        in_specs=[SMEM] + [VMEM] * len(moved),
        out_specs=VMEM,
        compiler_params=PARAMS,
    )(place, *moved)
    return result.reshape(n_local, vt, n_j, n_tr * vt)


def solution(mesh):
    return jax.shard_map(
        functools.partial(per_device, mesh.shape["tr"], mesh.shape["ct"]),
        mesh=mesh,
        in_specs=(P(None, "tr", None, "ct"), P(None, "ct", None, "tr"), P()),
        out_specs=P("ct", "tr", None, None),
        check_vma=False,
    )
```

time: 139 us -> 51.6 us (0.37)
  waiting for transfers between devices: 67.3 us -> 22.6 us
  blocking collectives: 30 us -> 0 us
  starting transfers between devices: 0.04 us -> 23.8 us
  local copies, waits for them, and re-layouts: 21 us -> 1.47 us
  between operations: 13.5 us -> 0.05 us
  other arithmetic: 4.18 us -> 0.07 us
  Pallas kernels: 0 us -> 3.51 us
  matrix products: 2.48 us -> 0 us
    all_gather x1 -> x0, waiting for transfers between devices: 60.2 us -> none  [per_device(): lax.all_gather(cycle_integrals, 'tr', axis=3, tiled=True)]
    all_to_all x1 -> x0, blocking collectives: 30 us -> none  [per_device(): lax.all_to_all(partial_value.astype(jnp.bfloat16), 'tr', split_axis=3, co...]
    ppermute x0 -> x16, starting transfers between devices: none -> 23.8 us  [swap(): return lax.ppermute(value, axis, [(n, n ^ d) for n in range(size)])]
    ppermute x0 -> x16, waiting for transfers between devices: none -> 22.6 us  [swap(): return lax.ppermute(value, axis, [(n, n ^ d) for n in range(size)])]
    reduce_scatter x1 -> x0, waiting for transfers between devices: 7.01 us -> none  [per_device(): lax.psum_scatter(moved_parts.astype(jnp.float32).astype(jnp.bfloat16), 'c...]
    all_to_all x2 -> x0, local copies, waits for them, and re-layouts: 6.81 us -> none  [per_device(): lax.all_to_all(partial_value.astype(jnp.bfloat16), 'tr', split_axis=3, co...]
    unnamed x3 -> x5, local copies, waits for them, and re-layouts: 6.92 us -> 1.47 us
    all_gather x1 -> x0, local copies, waits for them, and re-layouts: 4.73 us -> none  [per_device(): lax.all_gather(cycle_integrals, 'tr', axis=3, tiled=True)]
  transfers between devices with their start and end apart: 2 -> 16, of which waited for: 2 -> 8; matrix products, arithmetic and copies ran while one was open for 4% -> 0% of each run, Pallas kernels for 0% -> 0%
where the time goes in v1:
time: 51.6 us; the launch traced here: 51.5 us
  starting transfers between devices  23.8 us (46%)
  waiting for transfers between devices  22.6 us (44%)
  Pallas kernels  3.51 us (7%)
  local copies, waits for them, and re-layouts  1.47 us (3%)
    ppermute x16, starting transfers between devices, swap(): return lax.ppermute(value, axis, [(n, n ^ d) for n in range(size)])  23.8 us
    ppermute x16, waiting for transfers between devices, swap(): return lax.ppermute(value, axis, [(n, n ^ d) for n in range(size)])  22.6 us
    pallas_call x1, Pallas kernels, per_device(): pl.pallas_call(functools.partial(partials_kernel, n_ct), out_shape=[jax.S...  1.91 us
    pallas_call x1, Pallas kernels, per_device(): pl.pallas_call(functools.partial(place_kernel, offsets), out_shape=jax.Sh...  1.48 us
    unnamed x5, local copies, waits for them, and re-layouts  1.47 us
  transfers between devices with their start and end apart: 16, of which 8 were waited for; matrix products, arithmetic and copies ran while one was open for 0% of the time, Pallas kernels for 0%

profile of v1, /device:TPU:0, one launch (start us, length us, event | category | flops | bytes accessed | tf_op | source)
XLA Modules:
  0.0 51.5 jit_solution(3179151558712530489)
XLA Ops:
  0.0 0.0 copy-start
  0.0 1.5 %copy.10 = bf16[8,64,2,512]{3,1,2,0:T(8,128)(2,1)S(1)} copy(bf16[8,64,2,512]{3,2,1,0:T(2,128)(2,1)} %param.3) | data formatting | bytes 2097152 | tf_op args[0]
  1.5 3.0 %collective-permute-start = (bf16[8,64,2,512]{3,1,2,0:T(8,128)(2,1)S(1)}, bf16[8,64,2,512]{3,1,2,0:T(8,128)(2,1)S(1)}, u32[]{:S(2)}, u32[]{:S(2)}) collective-permute-start(bf16[8,64,2,512]{3,1,2,0:T(8,128)(2,1)S(1)} %copy.10), channel_id=1, source_target_pairs={{0,2},{2,0},{4,6},{6,4},{8,10},{10,8},{12,14},{14,12},{16,18},{18,... | collective-permute-start | bytes 3145736 | tf_op jit(solution)/shard_map/ppermute | solution.py:85
  4.5 0.0 copy-done
  4.5 3.6 %collective-permute-start.6 = (bf16[1,2,64,512]{3,2,1,0:T(8,128)(2,1)S(1)}, bf16[1,2,64,512]{3,2,1,0:T(8,128)(2,1)S(1)}, u32[]{:S(2)}, u32[]{:S(2)}) collective-permute-start(bf16[1,2,64,512]{3,2,1,0:T(8,128)(2,1)S(1)} %bitcast.13), channel_id=1, source_target_pairs={{0,24},{2,26},{4,28},{6,30},{8,16},{10,18},{12,20},{14,22},{16,8},... | collective-permute-start | bytes 393224 | tf_op jit(solution)/shard_map/ppermute | solution.py:85
  8.1 0.0 collective-permute-start.4
  8.1 0.8 %collective-permute-start.2 = (bf16[1,2,64,512]{3,2,1,0:T(8,128)(2,1)S(1)}, bf16[1,2,64,512]{3,2,1,0:T(8,128)(2,1)S(1)}, u32[]{:S(2)}, u32[]{:S(2)}) collective-permute-start(bf16[1,2,64,512]{3,2,1,0:T(8,128)(2,1)S(1)} %bitcast.15), channel_id=1, source_target_pairs={{0,8},{2,10},{4,12},{6,14},{8,0},{10,2},{12,4},{14,6},{16,24},{18,... | collective-permute-start | bytes 393224 | tf_op jit(solution)/shard_map/ppermute | solution.py:85
  8.9 1.5 %collective-permute-start.1 = (bf16[1,2,64,512]{3,2,1,0:T(8,128)(2,1)S(1)}, bf16[1,2,64,512]{3,2,1,0:T(8,128)(2,1)S(1)}, u32[]{:S(2)}, u32[]{:S(2)}) collective-permute-start(bf16[1,2,64,512]{3,2,1,0:T(8,128)(2,1)S(1)} %bitcast.16), channel_id=1, source_target_pairs={{0,4},{2,6},{4,0},{6,2},{8,12},{10,14},{12,8},{14,10},{16,20},{18,... | collective-permute-start | bytes 393224 | tf_op jit(solution)/shard_map/ppermute | solution.py:85
  10.4 2.4 %collective-permute-done.6.refs_8_ = bf16[1,2,64,512]{3,2,1,0:T(8,128)(2,1)S(1)} collective-permute-done((bf16[1,2,64,512]{3,2,1,0:T(8,128)(2,1)S(1)}, bf16[1,2,64,512]{3,2,1,0:T(8,128)(2,1)S(1)}, u32[]{:S(2)}, u32[]{:S(2)}) %collective-permute-start.6) | collective-permute-done | bytes 131104 | tf_op jit(solution)/shard_map/ppermute | solution.py:85
  12.8 1.5 %collective-permute-start.7 = (bf16[1,2,64,512]{3,2,1,0:T(8,128)(2,1)S(1)}, bf16[1,2,64,512]{3,2,1,0:T(8,128)(2,1)S(1)}, u32[]{:S(2)}, u32[]{:S(2)}) collective-permute-start(bf16[1,2,64,512]{3,2,1,0:T(8,128)(2,1)S(1)} %collective-permute-done.6.refs_8_), channel_id=1, source_target_pairs={{0,4},{2,6},{4,0},{6,2},{8,12},{10,14},{12,8},{14,10},{16,20},{18,... | collective-permute-start | bytes 393224 | tf_op jit(solution)/shard_map/ppermute | solution.py:85
  14.3 4.6 %collective-permute-done.4.refs_6_ = bf16[1,2,64,512]{3,2,1,0:T(8,128)(2,1)S(1)} collective-permute-done((bf16[1,2,64,512]{3,2,1,0:T(8,128)(2,1)S(1)}, bf16[1,2,64,512]{3,2,1,0:T(8,128)(2,1)S(1)}, u32[]{:S(2)}, u32[]{:S(2)}) %collective-permute-start.4) | collective-permute-done | bytes 131104 | tf_op jit(solution)/shard_map/ppermute | solution.py:85
  18.9 1.5 %collective-permute-start.5 = (bf16[1,2,64,512]{3,2,1,0:T(8,128)(2,1)S(1)}, bf16[1,2,64,512]{3,2,1,0:T(8,128)(2,1)S(1)}, u32[]{:S(2)}, u32[]{:S(2)}) collective-permute-start(bf16[1,2,64,512]{3,2,1,0:T(8,128)(2,1)S(1)} %collective-permute-done.4.refs_6_), channel_id=1, source_target_pairs={{0,4},{2,6},{4,0},{6,2},{8,12},{10,14},{12,8},{14,10},{16,20},{18,... | collective-permute-start | bytes 393224 | tf_op jit(solution)/shard_map/ppermute | solution.py:85
  20.4 0.0 collective-permute-done.2.refs_4_
  20.4 0.5 collective-permute-start.3
  20.9 0.0 copy-start.1
  20.9 0.1 pad_add_fusion.place
  21.0 0.0 collective-permute-done.1.refs_3_
  21.0 0.0 collective-permute-done.7.refs_9_
  21.0 3.8 %collective-permute-done.5.refs_7_ = bf16[1,2,64,512]{3,2,1,0:T(8,128)(2,1)S(1)} collective-permute-done((bf16[1,2,64,512]{3,2,1,0:T(8,128)(2,1)S(1)}, bf16[1,2,64,512]{3,2,1,0:T(8,128)(2,1)S(1)}, u32[]{:S(2)}, u32[]{:S(2)}) %collective-permute-start.5) | collective-permute-done | bytes 131104 | tf_op jit(solution)/shard_map/ppermute | solution.py:85
  24.8 1.4 %collective-permute-done.3.refs_5_ = bf16[1,2,64,512]{3,2,1,0:T(8,128)(2,1)S(1)} collective-permute-done((bf16[1,2,64,512]{3,2,1,0:T(8,128)(2,1)S(1)}, bf16[1,2,64,512]{3,2,1,0:T(8,128)(2,1)S(1)}, u32[]{:S(2)}, u32[]{:S(2)}) %collective-permute-start.3) | collective-permute-done | bytes 131104 | tf_op jit(solution)/shard_map/ppermute | solution.py:85
  26.2 1.4 %collective-permute-done = bf16[8,64,2,512]{3,1,2,0:T(8,128)(2,1)S(1)} collective-permute-done((bf16[8,64,2,512]{3,1,2,0:T(8,128)(2,1)S(1)}, bf16[8,64,2,512]{3,1,2,0:T(8,128)(2,1)S(1)}, u32[]{:S(2)}, u32[]{:S(2)}) %collective-permute-start) | collective-permute-done | bytes 1048608 | tf_op jit(solution)/shard_map/ppermute | solution.py:85
  27.6 0.0 copy-done.1
  27.6 1.9 %shard_map.37 = (bf16[4,512,128]{2,1,0:T(8,128)(2,1)S(1)}, bf16[4,512,128]{2,1,0:T(8,128)(2,1)S(1)}) custom-call(s32[2]{0:T(128)S(1)} %pad_add_fusion.place, s32[8,16]{1,0:T(8,128)S(1)} %copy-done.1, bf16[8,2,64,512]{3,2,1,0:T(8,128)(2,1)S(1)} %bitcast.11, bf16[8,2,64,512]{3,2,1,0:T(8,128)(2,1)S(1)} %bitcast.12, bf16[1,2,64,512]{3,2,1,0:T(8,128)(2,1)S(1)} %bitcast.17, ...), custom_call_target="tpu_custom_call" | custom-call | tf_op jit(solution)/shard_map/pallas_call | solution.py:97
  29.6 0.1 collective-permute-start.8
  29.6 1.9 %collective-permute-done.8.refs_1_ = bf16[4,512,128]{2,1,0:T(8,128)(2,1)S(1)} collective-permute-done((bf16[4,512,128]{2,1,0:T(8,128)(2,1)S(1)}, bf16[4,512,128]{2,1,0:T(8,128)(2,1)S(1)}, u32[]{:S(2)}, u32[]{:S(2)}) %collective-permute-start.8) | collective-permute-done | bytes 524320 | tf_op jit(solution)/shard_map/ppermute | solution.py:85
  31.5 0.1 shard_map.38
  31.7 1.8 %collective-permute-start.9 = (bf16[4,64,128]{2,1,0:T(8,128)(2,1)S(1)}, bf16[4,64,128]{2,1,0:T(8,128)(2,1)S(1)}, u32[]{:S(2)}, u32[]{:S(2)}) collective-permute-start(bf16[4,64,128]{2,1,0:T(8,128)(2,1)S(1)} %get-tuple-element.18), channel_id=1, source_target_pairs={{0,4},{2,6},{4,0},{6,2},{8,12},{10,14},{12,8},{14,10},{16,20},{18,... | collective-permute-start | bytes 196616 | tf_op jit(solution)/shard_map/ppermute | solution.py:85
  33.5 1.6 %collective-permute-start.10 = (bf16[4,64,128]{2,1,0:T(8,128)(2,1)S(1)}, bf16[4,64,128]{2,1,0:T(8,128)(2,1)S(1)}, u32[]{:S(2)}, u32[]{:S(2)}) collective-permute-start(bf16[4,64,128]{2,1,0:T(8,128)(2,1)S(1)} %get-tuple-element.19), channel_id=1, source_target_pairs={{0,8},{2,10},{4,12},{6,14},{8,0},{10,2},{12,4},{14,6},{16,24},{18,... | collective-permute-start | bytes 196616 | tf_op jit(solution)/shard_map/ppermute | solution.py:85
  35.1 0.2 collective-permute-start.11
  35.2 2.8 %collective-permute-start.12 = (bf16[4,64,128]{2,1,0:T(8,128)(2,1)S(1)}, bf16[4,64,128]{2,1,0:T(8,128)(2,1)S(1)}, u32[]{:S(2)}, u32[]{:S(2)}) collective-permute-start(bf16[4,64,128]{2,1,0:T(8,128)(2,1)S(1)} %get-tuple-element.21), channel_id=1, source_target_pairs={{0,16},{2,18},{4,20},{6,22},{8,24},{10,26},{12,28},{14,30},{16,0},... | collective-permute-start | bytes 196616 | tf_op jit(solution)/shard_map/ppermute | solution.py:85
  38.0 1.3 %collective-permute-start.13 = (bf16[4,64,128]{2,1,0:T(8,128)(2,1)S(1)}, bf16[4,64,128]{2,1,0:T(8,128)(2,1)S(1)}, u32[]{:S(2)}, u32[]{:S(2)}) collective-permute-start(bf16[4,64,128]{2,1,0:T(8,128)(2,1)S(1)} %get-tuple-element.22), channel_id=1, source_target_pairs={{0,20},{2,22},{4,16},{6,18},{8,28},{10,30},{12,24},{14,26},{16,4},... | collective-permute-start | bytes 196616 | tf_op jit(solution)/shard_map/ppermute | solution.py:85
  39.3 0.0 collective-permute-done.9.refs_1_
  39.3 3.6 %collective-permute-start.14 = (bf16[4,64,128]{2,1,0:T(8,128)(2,1)S(1)}, bf16[4,64,128]{2,1,0:T(8,128)(2,1)S(1)}, u32[]{:S(2)}, u32[]{:S(2)}) collective-permute-start(bf16[4,64,128]{2,1,0:T(8,128)(2,1)S(1)} %get-tuple-element.23), channel_id=1, source_target_pairs={{0,24},{2,26},{4,28},{6,30},{8,16},{10,18},{12,20},{14,22},{16,8},... | collective-permute-start | bytes 196616 | tf_op jit(solution)/shard_map/ppermute | solution.py:85
  42.9 0.0 collective-permute-done.10.refs_2_
  42.9 0.0 collective-permute-start.15
  43.0 0.0 collective-permute-done.11.refs_3_
  43.0 0.0 collective-permute-done.12.refs_4_
  43.0 5.6 %collective-permute-done.13.refs_5_ = bf16[4,64,128]{2,1,0:T(8,128)(2,1)S(1)} collective-permute-done((bf16[4,64,128]{2,1,0:T(8,128)(2,1)S(1)}, bf16[4,64,128]{2,1,0:T(8,128)(2,1)S(1)}, u32[]{:S(2)}, u32[]{:S(2)}) %collective-permute-start.13) | collective-permute-done | bytes 65568 | tf_op jit(solution)/shard_map/ppermute | solution.py:85
  48.5 0.0 collective-permute-done.14.refs_6_
  48.5 1.5 %collective-permute-done.15.refs_7_ = bf16[4,64,128]{2,1,0:T(8,128)(2,1)S(1)} collective-permute-done((bf16[4,64,128]{2,1,0:T(8,128)(2,1)S(1)}, bf16[4,64,128]{2,1,0:T(8,128)(2,1)S(1)}, u32[]{:S(2)}, u32[]{:S(2)}) %collective-permute-start.15) | collective-permute-done | bytes 65568 | tf_op jit(solution)/shard_map/ppermute | solution.py:85
  50.0 1.5 %shard_map.39 = bf16[4,64,1024]{2,1,0:T(8,128)(2,1)} custom-call(s32[2]{0:T(128)S(1)} %pad_add_fusion.place, bf16[4,64,128]{2,1,0:T(8,128)(2,1)S(1)} %get-tuple-element.17.refs_0_, bf16[4,64,128]{2,1,0:T(8,128)(2,1)S(1)} %collective-permute-done.9.refs_1_, bf16[4,64,128]{2,1,0:T(8,128)(2,1)S(1)} %collective-permute-done.10.refs_2_, ...), custom_call_target="tpu_custom_call" | custom-call | tf_op jit(solution)/shard_map/pallas_call | solution.py:114
Async XLA Ops:
  0.0 4.5 %copy-start = (bf16[2,512,1,64]{1,3,2,0:T(8,128)(2,1)S(1)}, bf16[2,512,1,64]{1,3,2,0:T(8,128)(2,1)}, u32[]{:S(2)}) copy-start(bf16[2,512,1,64]{1,3,2,0:T(8,128)(2,1)} %param.4) | copy-start | bytes 393220
  1.5 26.2 %collective-permute-start = (bf16[8,64,2,512]{3,1,2,0:T(8,128)(2,1)S(1)}, bf16[8,64,2,512]{3,1,2,0:T(8,128)(2,1)S(1)}, u32[]{:S(2)}, u32[]{:S(2)}) collective-permute-start(bf16[8,64,2,512]{3,1,2,0:T(8,128)(2,1)S(1)} %copy.10), channel_id=1, source_target_pairs={{0,2},{2,0},{4,6},{6,4},{8,10},{10,8},{12,14},{14,12},{16,18},{18,... | collective-permute-start | bytes 3145736 | tf_op jit(solution)/shard_map/ppermute | solution.py:85
  4.5 8.3 %collective-permute-start.6 = (bf16[1,2,64,512]{3,2,1,0:T(8,128)(2,1)S(1)}, bf16[1,2,64,512]{3,2,1,0:T(8,128)(2,1)S(1)}, u32[]{:S(2)}, u32[]{:S(2)}) collective-permute-start(bf16[1,2,64,512]{3,2,1,0:T(8,128)(2,1)S(1)} %bitcast.13), channel_id=1, source_target_pairs={{0,24},{2,26},{4,28},{6,30},{8,16},{10,18},{12,20},{14,22},{16,8},... | collective-permute-start | bytes 393224 | tf_op jit(solution)/shard_map/ppermute | solution.py:85
  8.1 10.8 %collective-permute-start.4 = (bf16[1,2,64,512]{3,2,1,0:T(8,128)(2,1)S(1)}, bf16[1,2,64,512]{3,2,1,0:T(8,128)(2,1)S(1)}, u32[]{:S(2)}, u32[]{:S(2)}) collective-permute-start(bf16[1,2,64,512]{3,2,1,0:T(8,128)(2,1)S(1)} %bitcast.14), channel_id=1, source_target_pairs={{0,16},{2,18},{4,20},{6,22},{8,24},{10,26},{12,28},{14,30},{16,0},... | collective-permute-start | bytes 393224 | tf_op jit(solution)/shard_map/ppermute | solution.py:85
  8.1 12.3 %collective-permute-start.2 = (bf16[1,2,64,512]{3,2,1,0:T(8,128)(2,1)S(1)}, bf16[1,2,64,512]{3,2,1,0:T(8,128)(2,1)S(1)}, u32[]{:S(2)}, u32[]{:S(2)}) collective-permute-start(bf16[1,2,64,512]{3,2,1,0:T(8,128)(2,1)S(1)} %bitcast.15), channel_id=1, source_target_pairs={{0,8},{2,10},{4,12},{6,14},{8,0},{10,2},{12,4},{14,6},{16,24},{18,... | collective-permute-start | bytes 393224 | tf_op jit(solution)/shard_map/ppermute | solution.py:85
  8.9 12.1 %collective-permute-start.1 = (bf16[1,2,64,512]{3,2,1,0:T(8,128)(2,1)S(1)}, bf16[1,2,64,512]{3,2,1,0:T(8,128)(2,1)S(1)}, u32[]{:S(2)}, u32[]{:S(2)}) collective-permute-start(bf16[1,2,64,512]{3,2,1,0:T(8,128)(2,1)S(1)} %bitcast.16), channel_id=1, source_target_pairs={{0,4},{2,6},{4,0},{6,2},{8,12},{10,14},{12,8},{14,10},{16,20},{18,... | collective-permute-start | bytes 393224 | tf_op jit(solution)/shard_map/ppermute | solution.py:85
  12.8 8.2 %collective-permute-start.7 = (bf16[1,2,64,512]{3,2,1,0:T(8,128)(2,1)S(1)}, bf16[1,2,64,512]{3,2,1,0:T(8,128)(2,1)S(1)}, u32[]{:S(2)}, u32[]{:S(2)}) collective-permute-start(bf16[1,2,64,512]{3,2,1,0:T(8,128)(2,1)S(1)} %collective-permute-done.6.refs_8_), channel_id=1, source_target_pairs={{0,4},{2,6},{4,0},{6,2},{8,12},{10,14},{12,8},{14,10},{16,20},{18,... | collective-permute-start | bytes 393224 | tf_op jit(solution)/shard_map/ppermute | solution.py:85
  18.9 5.9 %collective-permute-start.5 = (bf16[1,2,64,512]{3,2,1,0:T(8,128)(2,1)S(1)}, bf16[1,2,64,512]{3,2,1,0:T(8,128)(2,1)S(1)}, u32[]{:S(2)}, u32[]{:S(2)}) collective-permute-start(bf16[1,2,64,512]{3,2,1,0:T(8,128)(2,1)S(1)} %collective-permute-done.4.refs_6_), channel_id=1, source_target_pairs={{0,4},{2,6},{4,0},{6,2},{8,12},{10,14},{12,8},{14,10},{16,20},{18,... | collective-permute-start | bytes 393224 | tf_op jit(solution)/shard_map/ppermute | solution.py:85
  20.4 5.8 %collective-permute-start.3 = (bf16[1,2,64,512]{3,2,1,0:T(8,128)(2,1)S(1)}, bf16[1,2,64,512]{3,2,1,0:T(8,128)(2,1)S(1)}, u32[]{:S(2)}, u32[]{:S(2)}) collective-permute-start(bf16[1,2,64,512]{3,2,1,0:T(8,128)(2,1)S(1)} %collective-permute-done.2.refs_4_), channel_id=1, source_target_pairs={{0,4},{2,6},{4,0},{6,2},{8,12},{10,14},{12,8},{14,10},{16,20},{18,... | collective-permute-start | bytes 393224 | tf_op jit(solution)/shard_map/ppermute | solution.py:85
  20.9 6.7 %copy-start.1 = (s32[8,16]{1,0:T(8,128)S(1)}, s32[8,16]{1,0:T(8,128)}, u32[]{:S(2)}) copy-start(s32[8,16]{1,0:T(8,128)} %live.1) | copy-start | bytes 1540
  29.6 2.0 %collective-permute-start.8 = (bf16[4,512,128]{2,1,0:T(8,128)(2,1)S(1)}, bf16[4,512,128]{2,1,0:T(8,128)(2,1)S(1)}, u32[]{:S(2)}, u32[]{:S(2)}) collective-permute-start(bf16[4,512,128]{2,1,0:T(8,128)(2,1)S(1)} %get-tuple-element.16), channel_id=1, source_target_pairs={{0,1},{1,0},{2,3},{3,2},{4,5},{5,4},{6,7},{7,6},{8,9},{9,8},{10,11... | collective-permute-start | bytes 1572872 | tf_op jit(solution)/shard_map/ppermute | solution.py:85
  31.7 7.7 %collective-permute-start.9 = (bf16[4,64,128]{2,1,0:T(8,128)(2,1)S(1)}, bf16[4,64,128]{2,1,0:T(8,128)(2,1)S(1)}, u32[]{:S(2)}, u32[]{:S(2)}) collective-permute-start(bf16[4,64,128]{2,1,0:T(8,128)(2,1)S(1)} %get-tuple-element.18), channel_id=1, source_target_pairs={{0,4},{2,6},{4,0},{6,2},{8,12},{10,14},{12,8},{14,10},{16,20},{18,... | collective-permute-start | bytes 196616 | tf_op jit(solution)/shard_map/ppermute | solution.py:85
  33.5 9.5 %collective-permute-start.10 = (bf16[4,64,128]{2,1,0:T(8,128)(2,1)S(1)}, bf16[4,64,128]{2,1,0:T(8,128)(2,1)S(1)}, u32[]{:S(2)}, u32[]{:S(2)}) collective-permute-start(bf16[4,64,128]{2,1,0:T(8,128)(2,1)S(1)} %get-tuple-element.19), channel_id=1, source_target_pairs={{0,8},{2,10},{4,12},{6,14},{8,0},{10,2},{12,4},{14,6},{16,24},{18,... | collective-permute-start | bytes 196616 | tf_op jit(solution)/shard_map/ppermute | solution.py:85
  35.1 7.9 %collective-permute-start.11 = (bf16[4,64,128]{2,1,0:T(8,128)(2,1)S(1)}, bf16[4,64,128]{2,1,0:T(8,128)(2,1)S(1)}, u32[]{:S(2)}, u32[]{:S(2)}) collective-permute-start(bf16[4,64,128]{2,1,0:T(8,128)(2,1)S(1)} %get-tuple-element.20), channel_id=1, source_target_pairs={{0,12},{2,14},{4,8},{6,10},{8,4},{10,6},{12,0},{14,2},{16,28},{18,... | collective-permute-start | bytes 196616 | tf_op jit(solution)/shard_map/ppermute | solution.py:85
  35.2 7.8 %collective-permute-start.12 = (bf16[4,64,128]{2,1,0:T(8,128)(2,1)S(1)}, bf16[4,64,128]{2,1,0:T(8,128)(2,1)S(1)}, u32[]{:S(2)}, u32[]{:S(2)}) collective-permute-start(bf16[4,64,128]{2,1,0:T(8,128)(2,1)S(1)} %get-tuple-element.21), channel_id=1, source_target_pairs={{0,16},{2,18},{4,20},{6,22},{8,24},{10,26},{12,28},{14,30},{16,0},... | collective-permute-start | bytes 196616 | tf_op jit(solution)/shard_map/ppermute | solution.py:85
  38.0 10.5 %collective-permute-start.13 = (bf16[4,64,128]{2,1,0:T(8,128)(2,1)S(1)}, bf16[4,64,128]{2,1,0:T(8,128)(2,1)S(1)}, u32[]{:S(2)}, u32[]{:S(2)}) collective-permute-start(bf16[4,64,128]{2,1,0:T(8,128)(2,1)S(1)} %get-tuple-element.22), channel_id=1, source_target_pairs={{0,20},{2,22},{4,16},{6,18},{8,28},{10,30},{12,24},{14,26},{16,4},... | collective-permute-start | bytes 196616 | tf_op jit(solution)/shard_map/ppermute | solution.py:85
  39.3 9.2 %collective-permute-start.14 = (bf16[4,64,128]{2,1,0:T(8,128)(2,1)S(1)}, bf16[4,64,128]{2,1,0:T(8,128)(2,1)S(1)}, u32[]{:S(2)}, u32[]{:S(2)}) collective-permute-start(bf16[4,64,128]{2,1,0:T(8,128)(2,1)S(1)} %get-tuple-element.23), channel_id=1, source_target_pairs={{0,24},{2,26},{4,28},{6,30},{8,16},{10,18},{12,20},{14,22},{16,8},... | collective-permute-start | bytes 196616 | tf_op jit(solution)/shard_map/ppermute | solution.py:85
  42.9 7.1 %collective-permute-start.15 = (bf16[4,64,128]{2,1,0:T(8,128)(2,1)S(1)}, bf16[4,64,128]{2,1,0:T(8,128)(2,1)S(1)}, u32[]{:S(2)}, u32[]{:S(2)}) collective-permute-start(bf16[4,64,128]{2,1,0:T(8,128)(2,1)S(1)} %get-tuple-element.24), channel_id=1, source_target_pairs={{0,28},{2,30},{4,24},{6,26},{8,20},{10,22},{12,16},{14,18},{16,12}... | collective-permute-start | bytes 196616 | tf_op jit(solution)/shard_map/ppermute | solution.py:85

commit v2 on v0

v2 whole, which is shorter than its diff:
```python
import functools

import jax
import jax.numpy as jnp
from jax import lax
from jax.experimental import pallas as pl
from jax.experimental.pallas import tpu as pltpu
from jax.sharding import PartitionSpec as P

F32 = jnp.float32
VMEM = pl.BlockSpec(memory_space=pltpu.VMEM)
ANY = pl.BlockSpec(memory_space=pl.ANY)
SMEM = pl.BlockSpec(memory_space=pltpu.SMEM)
BIG = pl.CostEstimate(flops=10_000_000_000, bytes_accessed=1, transcendentals=0)
WAIT = pl.CostEstimate(flops=3_000_000_000, bytes_accessed=1, transcendentals=0)
COST = pl.CostEstimate(flops=1, bytes_accessed=1, transcendentals=0)
PARAMS = pltpu.CompilerParams(vmem_limit_bytes=16 * 1024 * 1024)


def pair_bit(ct):
    return 1 + ct % 2


def masks_kernel(n_ct, n_k, n_local, vt, live, out):
    tr, ct = lax.axis_index("tr"), lax.axis_index("ct")
    cols = out.shape[1]
    bit = pair_bit(ct)
    turned = (bit == 2) & ((tr & 1) == 1)
    members = [(tr & ~bit) + jnp.where(turned, bit, 0), (tr & ~bit) + jnp.where(turned, 0, bit)]
    tile = lax.broadcasted_iota(jnp.int32, (1, cols), 1) // vt
    for e in range(n_ct):
        for k in range(n_k):
            mask = jnp.zeros((1, cols), F32)
            for t in range(cols // vt):
                mask = jnp.where(tile == t, live[k, (ct ^ e) * (cols // vt) + t].astype(F32), mask)
            out[pl.ds(e * n_k + k, 1)] = mask
    for i in range(n_local):
        row = ct * n_local + i
        both = jnp.where(tile < 1, live[row, members[0]].astype(F32), live[row, members[1]].astype(F32))
        out[pl.ds(n_ct * n_k + i, 1)] = both
    out[pl.ds(n_ct * n_k + n_local, 1)] = jnp.full((1, cols), (members[0] == tr).astype(F32))


def blocks_kernel(n_ct, own_at, their_at, tiles_at, masks, *refs):
    outs = refs[-len(tiles_at) :]
    n_local, n_k, vt, cols = refs[own_at[0][0]].shape[1:]
    first = masks[pl.ds(n_ct * n_k + n_local, 1)] > 0
    lhs = {}
    for e in range(n_ct):
        for k in range(n_k):
            stacked = jnp.concatenate([refs[n][at, k] for n, at in (tile[e] for tile in tiles_at)], axis=0)
            lhs[e, k] = stacked * masks[pl.ds(e * n_k + k, 1)].astype(jnp.bfloat16)
    step = min(2, n_local)
    for start in range(0, n_local, step):
        total = None
        for (e, k), left in lhs.items():
            rows = []
            for i in range(start, start + step):
                a, b = (refs[n][at, i, k] for n, at in (own_at[e], their_at[e]))
                rows += [jnp.where(first, a, b), jnp.where(first, b, a)]
            term = lax.dot_general(
                left,
                jnp.concatenate(rows, axis=0),
                (((1,), (1,)), ((), ())),
                preferred_element_type=F32,
            )
            total = term if total is None else total + term
        for i in range(start, start + step):
            row_mask = masks[pl.ds(n_ct * n_k + i, 1), pl.ds(0, 2 * vt)]
            kept = total[:, (i - start) * 2 * vt : (i - start + 1) * 2 * vt] * row_mask
            for d, out in enumerate(outs):
                out[i] = kept[d * vt : (d + 1) * vt].astype(out.dtype)


def place_kernel(shifts, order, *refs):
    parts, (out, stage, sems) = dict(zip(order, refs)), refs[-3:]
    tr, ct = lax.axis_index("tr"), lax.axis_index("ct")
    wide = parts[0].shape[2]
    half = lax.broadcasted_iota(jnp.int32, (1, wide), 1) < wide // 2
    straight = pair_bit(ct) == 1
    own_first = (tr & (3 - pair_bit(ct))) == 0
    copies = []
    for n, by_core in enumerate(shifts):
        shift = sum(jnp.where(ct == c, z, 0) for c, z in enumerate(by_core))
        at = pl.multiple_of(((tr // 4) ^ shift) * 2 * wide, 2 * wide)
        for i in range(out.shape[0]):
            a, b = parts[2 * n][i], parts[2 * n + 1][i]
            lo, hi = jnp.where(own_first, a, b), jnp.where(own_first, b, a)
            across = pltpu.roll(jnp.where(half, hi, lo).astype(F32), wide // 2, 1).astype(lo.dtype)
            stage[n, i, :, pl.ds(0, wide)] = jnp.where(straight, lo, jnp.where(half, lo, hi))
            stage[n, i, :, pl.ds(wide, wide)] = jnp.where(straight, hi, across)
        copies.append(pltpu.make_async_copy(stage.at[n], out.at[:, :, pl.ds(at, 2 * wide)], sems.at[n]))
        copies[-1].start()
    for copy in copies:
        copy.wait()


def per_device(n_tr, n_ct, amplitudes, cycle_integrals, pair_live):
    n_i, vt, n_k, cols = amplitudes.shape
    n_j = cycle_integrals.shape[2]
    n_local = n_i // n_ct
    tr, ct = lax.axis_index("tr"), lax.axis_index("ct")

    def over_ct(value, e):
        return lax.ppermute(value, "ct", [(c, c ^ e) for c in range(n_ct)])

    def over_tr(value, move, e=0):
        pairs = [(r * n_ct + c, (r ^ move(c ^ e)) * n_ct + (c ^ e)) for r in range(n_tr) for c in range(n_ct)]
        return lax.ppermute(value, ("tr", "ct"), pairs)

    def gathered(value):
        return [value] + [over_ct(value, e) for e in range(1, n_ct)]

    own_w = jnp.transpose(cycle_integrals, (2, 0, 3, 1))
    n_z = n_tr // 4
    far = sorted(range(1, n_z), key=lambda z: -z)
    shared, split = far[: len(far) // n_ct * n_ct], far[len(far) // n_ct * n_ct :]
    groups = [shared[n : n + n_ct] for n in range(0, len(shared), n_ct)]
    shifts = [[group[c ^ e] for c in range(n_ct)] for group in groups for e in range(n_ct)]
    shifts += [[z] * n_ct for z in split] + [[0] * n_ct]

    def beside(c):
        return 3 - pair_bit(c)

    def pack(parts, after=(), cost=COST):
        def kernel(*refs):
            out, at = refs[-1], 0
            for ref in refs[: len(parts)]:
                out[pl.ds(at, ref.shape[0])] = ref[...]
                at += ref.shape[0]

        return pl.pallas_call(
            kernel,
            out_shape=jax.ShapeDtypeStruct((sum(p.shape[0] for p in parts), *parts[0].shape[1:]), parts[0].dtype),
            in_specs=[VMEM] * len(parts) + [ANY] * len(after),
            out_specs=VMEM,
            compiler_params=PARAMS,
            cost_estimate=cost,
        )(*parts, *after)

    masks = pl.pallas_call(
        functools.partial(masks_kernel, n_ct, n_k, n_local, vt),
        out_shape=jax.ShapeDtypeStruct((n_ct * n_k + n_local + 1, cols), F32),
        in_specs=[SMEM],
        out_specs=VMEM,
        compiler_params=PARAMS,
        cost_estimate=COST,
    )(pair_live)
    by_group = jnp.transpose(amplitudes, (0, 2, 1, 3)).reshape(n_ct, n_local, n_k, vt, cols)
    given = [lax.dynamic_index_in_dim(by_group, ct ^ e, 0) for e in range(n_ct)]
    own_a = [given[0]] + [over_ct(given[e], e) for e in range(1, n_ct)]
    own_parts = pack(gathered(own_w))
    whole = [over_tr(own_parts, lambda c, group=group: 4 * group[c]) for group in groups]
    some = [over_tr(own_w, lambda c, z=z: 4 * z) for z in split]
    their_a = [over_tr(value, pair_bit, e) for e, value in enumerate(given)]
    whole = pack(whole, [masks], WAIT)
    whole_rest = [over_ct(whole, e) for e in range(1, n_ct)]
    whole_side = [over_tr(whole, beside, e) for e in range(n_ct)]
    some = pack([own_w, *some], [])
    some_rest = [over_ct(some, e) for e in range(1, n_ct)]
    some_side = [over_tr(some, beside, e) for e in range(n_ct)]

    group_tiles = [[(n, g * n_ct + (e ^ n)) for e in range(n_ct)] for g in range(len(groups)) for n in range(n_ct)]
    split_tiles = [[(n_ct + e, n) for e in range(n_ct)] for n in [*range(1, len(split) + 1), 0]]

    def blocks(tiles, arrays, after=(), cost=COST):
        used = sorted({n for tile in tiles for n, _ in tile})
        arrays = [*own_a, *their_a, *[arrays[n] for n in used]]
        own_at, their_at = [(e, 0) for e in range(n_ct)], [(n_ct + e, 0) for e in range(n_ct)]
        tiles_at = [[(2 * n_ct + used.index(n), at) for n, at in tile] for tile in tiles]
        return pl.pallas_call(
            functools.partial(blocks_kernel, n_ct, own_at, their_at, tiles_at),
            out_shape=[jax.ShapeDtypeStruct((n_local, vt, 2 * vt), jnp.bfloat16)] * len(tiles),
            in_specs=[VMEM] * (1 + len(arrays)) + [ANY] * len(after),
            out_specs=[VMEM] * len(tiles),
            compiler_params=PARAMS,
            cost_estimate=cost,
        )(masks, *arrays, *after)

    near = blocks(group_tiles + split_tiles, [whole, *whole_rest, some, *some_rest])
    near_made = near
    near = [over_tr(b, lambda c, by=by: 4 * by[c]) if any(by) else b for b, by in zip(near, shifts)]
    side = blocks(group_tiles, whole_side, near[:1], WAIT)
    side += blocks(split_tiles, [None] * n_ct + some_side, [side[0], *near[:-1]], WAIT)
    side = [over_tr(b, lambda c, by=by: 4 * by[c] + beside(c)) for b, by in zip(side, shifts)]
    moved = [b for both in zip(near, side) for b in both]
    order = list(range(len(moved)))
    result = pl.pallas_call(
        functools.partial(place_kernel, shifts, order),
        out_shape=jax.ShapeDtypeStruct((n_local, vt, n_tr * vt), jnp.bfloat16),
        in_specs=[VMEM] * len(moved),
        out_specs=ANY,
        scratch_shapes=[
            pltpu.VMEM((n_z, n_local, vt, 4 * vt), jnp.bfloat16),
            pltpu.SemaphoreType.DMA((n_z,)),
        ],
        compiler_params=PARAMS,
        cost_estimate=COST,
    )(*[moved[n] for n in order])
    return result.reshape(n_local, vt, n_j, n_tr * vt)


def solution(mesh):
    return jax.shard_map(
        functools.partial(per_device, mesh.shape["tr"], mesh.shape["ct"]),
        mesh=mesh,
        in_specs=(P(None, "tr", None, "ct"), P(None, "ct", None, "tr"), P()),
        out_specs=P("ct", "tr", None, None),
        check_vma=False,
    )
```

time: 139 us -> 44 us (0.32)
  waiting for transfers between devices: 67.3 us -> 11.1 us
  blocking collectives: 30 us -> 0 us
  starting transfers between devices: 0.04 us -> 27 us
  local copies, waits for them, and re-layouts: 21 us -> 1.56 us
  between operations: 13.5 us -> 0.13 us
  other arithmetic: 4.18 us -> 0 us
  Pallas kernels: 0 us -> 4.05 us
  matrix products: 2.48 us -> 0 us
    all_gather x1 -> x0, waiting for transfers between devices: 60.2 us -> none  [per_device(): lax.all_gather(cycle_integrals, 'tr', axis=3, tiled=True)]
    all_to_all x1 -> x0, blocking collectives: 30 us -> none  [per_device(): lax.all_to_all(partial_value.astype(jnp.bfloat16), 'tr', split_axis=3, co...]
    ppermute x0 -> x19, starting transfers between devices: none -> 27 us  [the longest x15 24.6 us: over_tr(): return lax.ppermute(value, ('tr', 'ct'), pairs)]
    ppermute x0 -> x19, waiting for transfers between devices: none -> 11.1 us  [the longest x15 11.1 us: over_tr(): return lax.ppermute(value, ('tr', 'ct'), pairs)]
    reduce_scatter x1 -> x0, waiting for transfers between devices: 7.01 us -> none  [per_device(): lax.psum_scatter(moved_parts.astype(jnp.float32).astype(jnp.bfloat16), 'c...]
    unnamed x3 -> x4, local copies, waits for them, and re-layouts: 6.92 us -> 0.01 us
    all_to_all x2 -> x0, local copies, waits for them, and re-layouts: 6.81 us -> none  [per_device(): lax.all_to_all(partial_value.astype(jnp.bfloat16), 'tr', split_axis=3, co...]
    all_gather x1 -> x0, local copies, waits for them, and re-layouts: 4.73 us -> none  [per_device(): lax.all_gather(cycle_integrals, 'tr', axis=3, tiled=True)]
  transfers between devices with their start and end apart: 2 -> 19, of which waited for: 2 -> 9; matrix products, arithmetic and copies ran while one was open for 4% -> 4% of each run, Pallas kernels for 0% -> 7%
where the time goes in v2:
time: 44 us; the launch traced here: 43.8 us
  starting transfers between devices  27 us (61%)
  waiting for transfers between devices  11.1 us (25%)
  Pallas kernels  4.05 us (9%)
  local copies, waits for them, and re-layouts  1.56 us (4%)
    ppermute x15, starting transfers between devices, over_tr(): return lax.ppermute(value, ('tr', 'ct'), pairs)  24.6 us
    ppermute x15, waiting for transfers between devices, over_tr(): return lax.ppermute(value, ('tr', 'ct'), pairs)  11.1 us
    ppermute x4, starting transfers between devices, over_ct(): return lax.ppermute(value, 'ct', [(c, c ^ e) for c in range(n_ct)])  2.43 us
    pallas_call x3, Pallas kernels, blocks(): pl.pallas_call(functools.partial(blocks_kernel, n_ct, own_at, their_at, t...  2.36 us
    transpose x1, local copies, waits for them, and re-layouts, per_device(): jnp.transpose(amplitudes, (0, 2, 1, 3))  1.46 us
    pallas_call x1, Pallas kernels, per_device(): pl.pallas_call(functools.partial(place_kernel, shifts, order), out_shape=...  0.95 us
  transfers between devices with their start and end apart: 19, of which 9 were waited for; matrix products, arithmetic and copies ran while one was open for 4% of the time, Pallas kernels for 7%

profile of v2, /device:TPU:0, one launch (start us, length us, event | category | flops | bytes accessed | tf_op | source)
XLA Modules:
  0.0 43.8 jit_solution(5176230340741851899)
XLA Ops:
  0.0 0.5 %collective-permute-start.3 = (bf16[1,2,64,512]{3,2,1,0:T(8,128)(2,1)}, bf16[1,2,64,512]{3,2,1,0:T(8,128)(2,1)S(1)}, u32[]{:S(2)}, u32[]{:S(2)}) collective-permute-start(bf16[1,2,64,512]{3,2,1,0:T(8,128)(2,1)} %bitcast.8), channel_id=1, source_target_pairs={{0,1},{1,0},{2,3},{3,2},{4,5},{5,4},{6,7},{7,6},{8,9},{9,8},{10,11... | collective-permute-start | bytes 393224 | tf_op jit(solution)/shard_map/ppermute | solution.py:105
  0.5 0.0 copy-start
  0.5 1.5 %copy.4 = bf16[8,2,64,512]{3,2,1,0:T(8,128)(2,1)S(1)} copy(bf16[8,2,64,512]{3,1,2,0:T(2,128)(2,1)} %bitcast.13) | data formatting | bytes 2097152 | tf_op jit(solution)/shard_map/transpose | solution.py:149
  1.9 0.0 collective-permute-done.3.refs_1_
  1.9 0.0 copy-done
  2.0 4.7 %collective-permute-start.4 = (bf16[2,2,64,512]{3,2,1,0:T(8,128)(2,1)S(1)}, bf16[2,2,64,512]{3,2,1,0:T(8,128)(2,1)S(1)}, u32[]{:S(2)}, u32[]{:S(2)}) collective-permute-start(bf16[2,2,64,512]{3,2,1,0:T(8,128)(2,1)S(1)} %shard_map.38), channel_id=1, source_target_pairs={{0,24},{1,17},{2,26},{3,19},{4,28},{5,21},{6,30},{7,23},{8,16},{9,... | collective-permute-start | bytes 786440 | tf_op jit(solution)/shard_map/ppermute | solution.py:109
  6.7 0.1 constant_dynamic-slice_fusion
  6.8 1.6 %collective-permute-start.1 = (bf16[1,4,2,64,512]{4,3,2,1,0:T(8,128)(2,1)S(1)}, bf16[1,4,2,64,512]{4,3,2,1,0:T(8,128)(2,1)S(1)}, u32[]{:S(2)}, u32[]{:S(2)}) collective-permute-start(bf16[1,4,2,64,512]{4,3,2,1,0:T(8,128)(2,1)S(1)} %get-tuple-element.22.refs_0_), channel_id=1, source_target_pairs={{0,2},{1,5},{2,0},{3,7},{4,6},{5,1},{6,4},{7,3},{8,10},{9,13},{10,... | collective-permute-start | bytes 1572872 | tf_op jit(solution)/shard_map/ppermute | solution.py:109
  8.4 0.0 collective-permute-start.6
  8.4 0.2 collective-permute-start
  8.6 1.4 %collective-permute-start.2 = (bf16[1,4,2,64,512]{4,3,2,1,0:T(8,128)(2,1)S(1)}, bf16[1,4,2,64,512]{4,3,2,1,0:T(8,128)(2,1)S(1)}, u32[]{:S(2)}, u32[]{:S(2)}) collective-permute-start(bf16[1,4,2,64,512]{4,3,2,1,0:T(8,128)(2,1)S(1)} %get-tuple-element.21), channel_id=1, source_target_pairs={{0,5},{1,2},{2,7},{3,0},{4,1},{5,6},{6,3},{7,4},{8,13},{9,10},{10,... | collective-permute-start | bytes 1572872 | tf_op jit(solution)/shard_map/ppermute | solution.py:109
  10.0 0.0 copy-done.1
  10.0 0.7 %shard_map.37.refs_1_.masks = f32[9,512]{1,0:T(8,128)S(1)} custom-call(s32[8,16]{1,0:T(8,128)S(1)} %copy-done.1), custom_call_target="tpu_custom_call" | custom-call | flops 1 | bytes 1 | tf_op jit(solution)/shard_map/pallas_call | solution.py:141
  10.7 5.0 %collective-permute-done.6.refs_1_ = bf16[1,2,64,512]{3,2,1,0:T(8,128)(2,1)S(1)} collective-permute-done((bf16[1,2,64,512]{3,2,1,0:T(8,128)(2,1)S(1)}, bf16[1,2,64,512]{3,2,1,0:T(8,128)(2,1)S(1)}, u32[]{:S(2)}, u32[]{:S(2)}) %collective-permute-start.6) | collective-permute-done | bytes 131104 | tf_op jit(solution)/shard_map/ppermute | solution.py:109
  15.7 0.1 collective-permute-start.7
  15.8 0.0 collective-permute-done.4.refs_0_
  15.8 1.7 %collective-permute-start.5 = (bf16[2,2,64,512]{3,2,1,0:T(8,128)(2,1)S(1)}, bf16[2,2,64,512]{3,2,1,0:T(8,128)(2,1)S(1)}, u32[]{:S(2)}, u32[]{:S(2)}) collective-permute-start(bf16[2,2,64,512]{3,2,1,0:T(8,128)(2,1)S(1)} %shard_map.39.refs_4_), channel_id=1, source_target_pairs={{0,1},{1,0},{2,3},{3,2},{4,5},{5,4},{6,7},{7,6},{8,9},{9,8},{10,11... | collective-permute-start | bytes 786440 | tf_op jit(solution)/shard_map/ppermute | solution.py:105
  17.5 0.0 collective-permute-done.7.refs_7_
  17.5 1.3 %collective-permute-start.10 = (bf16[2,2,64,512]{3,2,1,0:T(8,128)(2,1)S(1)}, bf16[2,2,64,512]{3,2,1,0:T(8,128)(2,1)S(1)}, u32[]{:S(2)}, u32[]{:S(2)}) collective-permute-start(bf16[2,2,64,512]{3,2,1,0:T(8,128)(2,1)S(1)} %shard_map.39.refs_4_), channel_id=1, source_target_pairs={{0,3},{1,4},{2,1},{3,6},{4,7},{5,0},{6,5},{7,2},{8,11},{9,12},{10,... | collective-permute-start | bytes 786440 | tf_op jit(solution)/shard_map/ppermute | solution.py:109
  18.8 1.7 %collective-permute-done.1.refs_2_ = bf16[1,4,2,64,512]{4,3,2,1,0:T(8,128)(2,1)S(1)} collective-permute-done((bf16[1,4,2,64,512]{4,3,2,1,0:T(8,128)(2,1)S(1)}, bf16[1,4,2,64,512]{4,3,2,1,0:T(8,128)(2,1)S(1)}, u32[]{:S(2)}, u32[]{:S(2)}) %collective-permute-start.1) | collective-permute-done | bytes 524320 | tf_op jit(solution)/shard_map/ppermute | solution.py:109
  20.5 1.7 %collective-permute-start.9 = (bf16[2,2,64,512]{3,2,1,0:T(8,128)(2,1)S(1)}, bf16[2,2,64,512]{3,2,1,0:T(8,128)(2,1)S(1)}, u32[]{:S(2)}, u32[]{:S(2)}) collective-permute-start(bf16[2,2,64,512]{3,2,1,0:T(8,128)(2,1)S(1)} %shard_map.39.refs_4_), channel_id=1, source_target_pairs={{0,4},{1,3},{2,6},{3,1},{4,0},{5,7},{6,2},{7,5},{8,12},{9,11},{10,... | collective-permute-start | bytes 786440 | tf_op jit(solution)/shard_map/ppermute | solution.py:109
  22.3 0.0 collective-permute-done.refs_1_
  22.3 0.2 collective-permute-done.2.refs_3_
  22.5 0.0 collective-permute-done.5.refs_5_
  22.5 0.7 %shard_map.41 = (bf16[4,64,128]{2,1,0:T(8,128)(2,1)S(1)}, bf16[4,64,128]{2,1,0:T(8,128)(2,1)S(1)}, bf16[4,64,128]{2,1,0:T(8,128)(2,1)S(1)}, bf16[4,64,128]{2,1,0:T(8,128)(2,1)S(1)}) custom-call(f32[9,512]{1,0:T(8,128)S(1)} %shard_map.37.refs_1_.masks, bf16[1,4,2,64,512]{4,3,2,1,0:T(8,128)(2,1)S(1)} %get-tuple-element.22.refs_0_, ...), custom_call_target="tpu_custom_call" | custom-call | flops 1 | bytes 1 | tf_op jit(solution)/shard_map/pallas_call | solution.py:171
  23.3 1.6 %collective-permute-start.8 = (bf16[4,64,128]{2,1,0:T(8,128)(2,1)S(1)}, bf16[4,64,128]{2,1,0:T(8,128)(2,1)S(1)}, u32[]{:S(2)}, u32[]{:S(2)}) collective-permute-start(bf16[4,64,128]{2,1,0:T(8,128)(2,1)S(1)} %get-tuple-element.13), channel_id=1, source_target_pairs={{0,24},{1,17},{2,26},{3,19},{4,28},{5,21},{6,30},{7,23},{8,16},{9,... | collective-permute-start | bytes 196616 | tf_op jit(solution)/shard_map/ppermute | solution.py:109
  24.8 0.5 %collective-permute-start.15 = (bf16[2,2,64,512]{3,2,1,0:T(8,128)(2,1)S(1)}, bf16[2,2,64,512]{3,2,1,0:T(8,128)(2,1)S(1)}, u32[]{:S(2)}, u32[]{:S(2)}) collective-permute-start(bf16[2,2,64,512]{3,2,1,0:T(8,128)(2,1)S(1)} %shard_map.40.refs_6_), channel_id=1, source_target_pairs={{0,4},{1,3},{2,6},{3,1},{4,0},{5,7},{6,2},{7,5},{8,12},{9,11},{10,... | collective-permute-start | bytes 786440 | tf_op jit(solution)/shard_map/ppermute | solution.py:109
  25.3 0.0 collective-permute-start.16
  25.3 0.2 collective-permute-done.10.refs_5_
  25.5 2.4 %collective-permute-start.12 = (bf16[4,64,128]{2,1,0:T(8,128)(2,1)S(1)}, bf16[4,64,128]{2,1,0:T(8,128)(2,1)S(1)}, u32[]{:S(2)}, u32[]{:S(2)}) collective-permute-start(bf16[4,64,128]{2,1,0:T(8,128)(2,1)S(1)} %get-tuple-element.15), channel_id=1, source_target_pairs={{0,16},{1,25},{2,18},{3,27},{4,20},{5,29},{6,22},{7,31},{8,24},{9,... | collective-permute-start | bytes 196616 | tf_op jit(solution)/shard_map/ppermute | solution.py:109
  27.9 0.0 collective-permute-done.9.refs_4_
  27.9 1.3 %collective-permute-start.14 = (bf16[4,64,128]{2,1,0:T(8,128)(2,1)S(1)}, bf16[4,64,128]{2,1,0:T(8,128)(2,1)S(1)}, u32[]{:S(2)}, u32[]{:S(2)}) collective-permute-start(bf16[4,64,128]{2,1,0:T(8,128)(2,1)S(1)} %get-tuple-element.17), channel_id=1, source_target_pairs={{0,8},{1,9},{2,10},{3,11},{4,12},{5,13},{6,14},{7,15},{8,0},{9,1},... | collective-permute-start | bytes 196616 | tf_op jit(solution)/shard_map/ppermute | solution.py:109
  29.2 0.2 collective-permute-done.8.refs_6_.refs_7_.refs_0_
  29.4 0.8 %shard_map.42 = (bf16[4,64,128]{2,1,0:T(8,128)(2,1)S(1)}, bf16[4,64,128]{2,1,0:T(8,128)(2,1)S(1)}) custom-call(f32[9,512]{1,0:T(8,128)S(1)} %shard_map.37.refs_1_.masks, bf16[1,4,2,64,512]{4,3,2,1,0:T(8,128)(2,1)S(1)} %get-tuple-element.22.refs_0_, bf16[1,4,2,64,512]{4,3,2,1,0:T(8,128)(2,1)S(1)} %collective-permute-done.refs_1_, ...), custom_call_target="tpu_custom_call" | custom-call | flops 3000000000 | bytes 1 | tf_op jit(solution)/shard_map/pallas_call | solution.py:171
  30.2 2.8 %collective-permute-start.11 = (bf16[4,64,128]{2,1,0:T(8,128)(2,1)S(1)}, bf16[4,64,128]{2,1,0:T(8,128)(2,1)S(1)}, u32[]{:S(2)}, u32[]{:S(2)}) collective-permute-start(bf16[4,64,128]{2,1,0:T(8,128)(2,1)S(1)} %get-tuple-element.14.refs_6_), channel_id=1, source_target_pairs={{0,28},{1,19},{2,30},{3,17},{4,24},{5,23},{6,26},{7,21},{8,20},{9,... | collective-permute-start | bytes 196616 | tf_op jit(solution)/shard_map/ppermute | solution.py:109
  33.1 0.9 %collective-permute-done.15.refs_4_ = bf16[2,2,64,512]{3,2,1,0:T(8,128)(2,1)S(1)} collective-permute-done((bf16[2,2,64,512]{3,2,1,0:T(8,128)(2,1)S(1)}, bf16[2,2,64,512]{3,2,1,0:T(8,128)(2,1)S(1)}, u32[]{:S(2)}, u32[]{:S(2)}) %collective-permute-start.15) | collective-permute-done | bytes 262176 | tf_op jit(solution)/shard_map/ppermute | solution.py:109
  33.9 0.0 collective-permute-done.16.refs_5_
  33.9 0.0 collective-permute-done.12.refs_8_.refs_2_
  33.9 0.0 collective-permute-done.14.refs_9_.refs_4_
  33.9 0.8 %shard_map.43 = (bf16[4,64,128]{2,1,0:T(8,128)(2,1)S(1)}, bf16[4,64,128]{2,1,0:T(8,128)(2,1)S(1)}) custom-call(f32[9,512]{1,0:T(8,128)S(1)} %shard_map.37.refs_1_.masks, bf16[1,4,2,64,512]{4,3,2,1,0:T(8,128)(2,1)S(1)} %get-tuple-element.22.refs_0_, bf16[1,4,2,64,512]{4,3,2,1,0:T(8,128)(2,1)S(1)} %collective-permute-done.refs_1_, ...), custom_call_target="tpu_custom_call" | custom-call | flops 3000000000 | bytes 1 | tf_op jit(solution)/shard_map/pallas_call | solution.py:171
  34.8 1.7 %collective-permute-start.17 = (bf16[4,64,128]{2,1,0:T(8,128)(2,1)S(1)}, bf16[4,64,128]{2,1,0:T(8,128)(2,1)S(1)}, u32[]{:S(2)}, u32[]{:S(2)}) collective-permute-start(bf16[4,64,128]{2,1,0:T(8,128)(2,1)S(1)} %get-tuple-element.18), channel_id=1, source_target_pairs={{0,12},{1,11},{2,14},{3,9},{4,8},{5,15},{6,10},{7,13},{8,4},{9,3},... | collective-permute-start | bytes 196616 | tf_op jit(solution)/shard_map/ppermute | solution.py:109
  36.5 0.0 collective-permute-start.18
  36.5 3.6 %collective-permute-start.13 = (bf16[4,64,128]{2,1,0:T(8,128)(2,1)S(1)}, bf16[4,64,128]{2,1,0:T(8,128)(2,1)S(1)}, u32[]{:S(2)}, u32[]{:S(2)}) collective-permute-start(bf16[4,64,128]{2,1,0:T(8,128)(2,1)S(1)} %get-tuple-element.16), channel_id=1, source_target_pairs={{0,20},{1,27},{2,22},{3,25},{4,16},{5,31},{6,18},{7,29},{8,28},{9,... | collective-permute-start | bytes 196616 | tf_op jit(solution)/shard_map/ppermute | solution.py:109
  40.1 0.5 %collective-permute-done.17.refs_5_ = bf16[4,64,128]{2,1,0:T(8,128)(2,1)S(1)} collective-permute-done((bf16[4,64,128]{2,1,0:T(8,128)(2,1)S(1)}, bf16[4,64,128]{2,1,0:T(8,128)(2,1)S(1)}, u32[]{:S(2)}, u32[]{:S(2)}) %collective-permute-start.17) | collective-permute-done | bytes 65568 | tf_op jit(solution)/shard_map/ppermute | solution.py:109
  40.6 0.5 %collective-permute-done.18.refs_7_ = bf16[4,64,128]{2,1,0:T(8,128)(2,1)S(1)} collective-permute-done((bf16[4,64,128]{2,1,0:T(8,128)(2,1)S(1)}, bf16[4,64,128]{2,1,0:T(8,128)(2,1)S(1)}, u32[]{:S(2)}, u32[]{:S(2)}) %collective-permute-start.18) | collective-permute-done | bytes 65568 | tf_op jit(solution)/shard_map/ppermute | solution.py:109
  41.1 0.0 collective-permute-done.11.refs_1_
  41.1 1.8 %collective-permute-done.13.refs_3_ = bf16[4,64,128]{2,1,0:T(8,128)(2,1)S(1)} collective-permute-done((bf16[4,64,128]{2,1,0:T(8,128)(2,1)S(1)}, bf16[4,64,128]{2,1,0:T(8,128)(2,1)S(1)}, u32[]{:S(2)}, u32[]{:S(2)}) %collective-permute-start.13) | collective-permute-done | bytes 65568 | tf_op jit(solution)/shard_map/ppermute | solution.py:109
  42.9 1.0 %shard_map.44 = bf16[4,64,1024]{2,1,0:T(8,128)(2,1)} custom-call(bf16[4,64,128]{2,1,0:T(8,128)(2,1)S(1)} %collective-permute-done.8.refs_6_.refs_7_.refs_0_, bf16[4,64,128]{2,1,0:T(8,128)(2,1)S(1)} %collective-permute-done.11.refs_1_, bf16[4,64,128]{2,1,0:T(8,128)(2,1)S(1)} %collective-permute-done.12.refs_8_.refs_2_, ...), custom_call_target="tpu_custom_call" | custom-call | flops 1 | bytes 1 | tf_op jit(solution)/shard_map/pallas_call | solution.py:188
  (4 shorter events, 0.1 us)
Async XLA Ops:
  0.0 1.9 %collective-permute-start.3 = (bf16[1,2,64,512]{3,2,1,0:T(8,128)(2,1)}, bf16[1,2,64,512]{3,2,1,0:T(8,128)(2,1)S(1)}, u32[]{:S(2)}, u32[]{:S(2)}) collective-permute-start(bf16[1,2,64,512]{3,2,1,0:T(8,128)(2,1)} %bitcast.8), channel_id=1, source_target_pairs={{0,1},{1,0},{2,3},{3,2},{4,5},{5,4},{6,7},{7,6},{8,9},{9,8},{10,11... | collective-permute-start | bytes 393224 | tf_op jit(solution)/shard_map/ppermute | solution.py:105
  0.5 1.5 %copy-start = (bf16[2,512,1,64]{1,3,2,0:T(8,128)(2,1)S(1)}, bf16[2,512,1,64]{1,3,2,0:T(8,128)(2,1)}, u32[]{:S(2)}) copy-start(bf16[2,512,1,64]{1,3,2,0:T(8,128)(2,1)} %param.4) | copy-start | bytes 393220
  2.0 13.8 %collective-permute-start.4 = (bf16[2,2,64,512]{3,2,1,0:T(8,128)(2,1)S(1)}, bf16[2,2,64,512]{3,2,1,0:T(8,128)(2,1)S(1)}, u32[]{:S(2)}, u32[]{:S(2)}) collective-permute-start(bf16[2,2,64,512]{3,2,1,0:T(8,128)(2,1)S(1)} %shard_map.38), channel_id=1, source_target_pairs={{0,24},{1,17},{2,26},{3,19},{4,28},{5,21},{6,30},{7,23},{8,16},{9,... | collective-permute-start | bytes 786440 | tf_op jit(solution)/shard_map/ppermute | solution.py:109
  6.7 3.3 %copy-start.1 = (s32[8,16]{1,0:T(8,128)S(1)}, s32[8,16]{1,0:T(8,128)}, u32[]{:S(2)}) copy-start(s32[8,16]{1,0:T(8,128)} %live.1) | copy-start | bytes 1540
  6.8 13.7 %collective-permute-start.1 = (bf16[1,4,2,64,512]{4,3,2,1,0:T(8,128)(2,1)S(1)}, bf16[1,4,2,64,512]{4,3,2,1,0:T(8,128)(2,1)S(1)}, u32[]{:S(2)}, u32[]{:S(2)}) collective-permute-start(bf16[1,4,2,64,512]{4,3,2,1,0:T(8,128)(2,1)S(1)} %get-tuple-element.22.refs_0_), channel_id=1, source_target_pairs={{0,2},{1,5},{2,0},{3,7},{4,6},{5,1},{6,4},{7,3},{8,10},{9,13},{10,... | collective-permute-start | bytes 1572872 | tf_op jit(solution)/shard_map/ppermute | solution.py:109
  8.4 7.3 %collective-permute-start.6 = (bf16[1,2,64,512]{3,2,1,0:T(8,128)(2,1)S(1)}, bf16[1,2,64,512]{3,2,1,0:T(8,128)(2,1)S(1)}, u32[]{:S(2)}, u32[]{:S(2)}) collective-permute-start(bf16[1,2,64,512]{3,2,1,0:T(8,128)(2,1)S(1)} %bitcast.10), channel_id=1, source_target_pairs={{0,8},{1,9},{2,10},{3,11},{4,12},{5,13},{6,14},{7,15},{8,0},{9,1},... | collective-permute-start | bytes 393224 | tf_op jit(solution)/shard_map/ppermute | solution.py:109
  8.4 13.9 %collective-permute-start = (bf16[1,4,2,64,512]{4,3,2,1,0:T(8,128)(2,1)S(1)}, bf16[1,4,2,64,512]{4,3,2,1,0:T(8,128)(2,1)S(1)}, u32[]{:S(2)}, u32[]{:S(2)}) collective-permute-start(bf16[1,4,2,64,512]{4,3,2,1,0:T(8,128)(2,1)S(1)} %get-tuple-element.21), channel_id=1, source_target_pairs={{0,1},{1,0},{2,3},{3,2},{4,5},{5,4},{6,7},{7,6},{8,9},{9,8},{10,11... | collective-permute-start | bytes 1572872 | tf_op jit(solution)/shard_map/ppermute | solution.py:105
  8.6 14.0 %collective-permute-start.2 = (bf16[1,4,2,64,512]{4,3,2,1,0:T(8,128)(2,1)S(1)}, bf16[1,4,2,64,512]{4,3,2,1,0:T(8,128)(2,1)S(1)}, u32[]{:S(2)}, u32[]{:S(2)}) collective-permute-start(bf16[1,4,2,64,512]{4,3,2,1,0:T(8,128)(2,1)S(1)} %get-tuple-element.21), channel_id=1, source_target_pairs={{0,5},{1,2},{2,7},{3,0},{4,1},{5,6},{6,3},{7,4},{8,13},{9,10},{10,... | collective-permute-start | bytes 1572872 | tf_op jit(solution)/shard_map/ppermute | solution.py:109
  15.7 1.8 %collective-permute-start.7 = (bf16[2,2,64,512]{3,2,1,0:T(8,128)(2,1)S(1)}, bf16[2,2,64,512]{3,2,1,0:T(8,128)(2,1)S(1)}, u32[]{:S(2)}, u32[]{:S(2)}) collective-permute-start(bf16[2,2,64,512]{3,2,1,0:T(8,128)(2,1)S(1)} %shard_map.40.refs_6_), channel_id=1, source_target_pairs={{0,1},{1,0},{2,3},{3,2},{4,5},{5,4},{6,7},{7,6},{8,9},{9,8},{10,11... | collective-permute-start | bytes 786440 | tf_op jit(solution)/shard_map/ppermute | solution.py:105
  15.8 6.7 %collective-permute-start.5 = (bf16[2,2,64,512]{3,2,1,0:T(8,128)(2,1)S(1)}, bf16[2,2,64,512]{3,2,1,0:T(8,128)(2,1)S(1)}, u32[]{:S(2)}, u32[]{:S(2)}) collective-permute-start(bf16[2,2,64,512]{3,2,1,0:T(8,128)(2,1)S(1)} %shard_map.39.refs_4_), channel_id=1, source_target_pairs={{0,1},{1,0},{2,3},{3,2},{4,5},{5,4},{6,7},{7,6},{8,9},{9,8},{10,11... | collective-permute-start | bytes 786440 | tf_op jit(solution)/shard_map/ppermute | solution.py:105
  17.5 8.0 %collective-permute-start.10 = (bf16[2,2,64,512]{3,2,1,0:T(8,128)(2,1)S(1)}, bf16[2,2,64,512]{3,2,1,0:T(8,128)(2,1)S(1)}, u32[]{:S(2)}, u32[]{:S(2)}) collective-permute-start(bf16[2,2,64,512]{3,2,1,0:T(8,128)(2,1)S(1)} %shard_map.39.refs_4_), channel_id=1, source_target_pairs={{0,3},{1,4},{2,1},{3,6},{4,7},{5,0},{6,5},{7,2},{8,11},{9,12},{10,... | collective-permute-start | bytes 786440 | tf_op jit(solution)/shard_map/ppermute | solution.py:109
  20.5 7.4 %collective-permute-start.9 = (bf16[2,2,64,512]{3,2,1,0:T(8,128)(2,1)S(1)}, bf16[2,2,64,512]{3,2,1,0:T(8,128)(2,1)S(1)}, u32[]{:S(2)}, u32[]{:S(2)}) collective-permute-start(bf16[2,2,64,512]{3,2,1,0:T(8,128)(2,1)S(1)} %shard_map.39.refs_4_), channel_id=1, source_target_pairs={{0,4},{1,3},{2,6},{3,1},{4,0},{5,7},{6,2},{7,5},{8,12},{9,11},{10,... | collective-permute-start | bytes 786440 | tf_op jit(solution)/shard_map/ppermute | solution.py:109
  23.3 6.1 %collective-permute-start.8 = (bf16[4,64,128]{2,1,0:T(8,128)(2,1)S(1)}, bf16[4,64,128]{2,1,0:T(8,128)(2,1)S(1)}, u32[]{:S(2)}, u32[]{:S(2)}) collective-permute-start(bf16[4,64,128]{2,1,0:T(8,128)(2,1)S(1)} %get-tuple-element.13), channel_id=1, source_target_pairs={{0,24},{1,17},{2,26},{3,19},{4,28},{5,21},{6,30},{7,23},{8,16},{9,... | collective-permute-start | bytes 196616 | tf_op jit(solution)/shard_map/ppermute | solution.py:109
  24.8 9.1 %collective-permute-start.15 = (bf16[2,2,64,512]{3,2,1,0:T(8,128)(2,1)S(1)}, bf16[2,2,64,512]{3,2,1,0:T(8,128)(2,1)S(1)}, u32[]{:S(2)}, u32[]{:S(2)}) collective-permute-start(bf16[2,2,64,512]{3,2,1,0:T(8,128)(2,1)S(1)} %shard_map.40.refs_6_), channel_id=1, source_target_pairs={{0,4},{1,3},{2,6},{3,1},{4,0},{5,7},{6,2},{7,5},{8,12},{9,11},{10,... | collective-permute-start | bytes 786440 | tf_op jit(solution)/shard_map/ppermute | solution.py:109
  25.3 8.6 %collective-permute-start.16 = (bf16[2,2,64,512]{3,2,1,0:T(8,128)(2,1)S(1)}, bf16[2,2,64,512]{3,2,1,0:T(8,128)(2,1)S(1)}, u32[]{:S(2)}, u32[]{:S(2)}) collective-permute-start(bf16[2,2,64,512]{3,2,1,0:T(8,128)(2,1)S(1)} %shard_map.40.refs_6_), channel_id=1, source_target_pairs={{0,3},{1,4},{2,1},{3,6},{4,7},{5,0},{6,5},{7,2},{8,11},{9,12},{10,... | collective-permute-start | bytes 786440 | tf_op jit(solution)/shard_map/ppermute | solution.py:109
  25.5 8.4 %collective-permute-start.12 = (bf16[4,64,128]{2,1,0:T(8,128)(2,1)S(1)}, bf16[4,64,128]{2,1,0:T(8,128)(2,1)S(1)}, u32[]{:S(2)}, u32[]{:S(2)}) collective-permute-start(bf16[4,64,128]{2,1,0:T(8,128)(2,1)S(1)} %get-tuple-element.15), channel_id=1, source_target_pairs={{0,16},{1,25},{2,18},{3,27},{4,20},{5,29},{6,22},{7,31},{8,24},{9,... | collective-permute-start | bytes 196616 | tf_op jit(solution)/shard_map/ppermute | solution.py:109
  27.9 6.0 %collective-permute-start.14 = (bf16[4,64,128]{2,1,0:T(8,128)(2,1)S(1)}, bf16[4,64,128]{2,1,0:T(8,128)(2,1)S(1)}, u32[]{:S(2)}, u32[]{:S(2)}) collective-permute-start(bf16[4,64,128]{2,1,0:T(8,128)(2,1)S(1)} %get-tuple-element.17), channel_id=1, source_target_pairs={{0,8},{1,9},{2,10},{3,11},{4,12},{5,13},{6,14},{7,15},{8,0},{9,1},... | collective-permute-start | bytes 196616 | tf_op jit(solution)/shard_map/ppermute | solution.py:109
  30.2 10.9 %collective-permute-start.11 = (bf16[4,64,128]{2,1,0:T(8,128)(2,1)S(1)}, bf16[4,64,128]{2,1,0:T(8,128)(2,1)S(1)}, u32[]{:S(2)}, u32[]{:S(2)}) collective-permute-start(bf16[4,64,128]{2,1,0:T(8,128)(2,1)S(1)} %get-tuple-element.14.refs_6_), channel_id=1, source_target_pairs={{0,28},{1,19},{2,30},{3,17},{4,24},{5,23},{6,26},{7,21},{8,20},{9,... | collective-permute-start | bytes 196616 | tf_op jit(solution)/shard_map/ppermute | solution.py:109
  34.8 5.8 %collective-permute-start.17 = (bf16[4,64,128]{2,1,0:T(8,128)(2,1)S(1)}, bf16[4,64,128]{2,1,0:T(8,128)(2,1)S(1)}, u32[]{:S(2)}, u32[]{:S(2)}) collective-permute-start(bf16[4,64,128]{2,1,0:T(8,128)(2,1)S(1)} %get-tuple-element.18), channel_id=1, source_target_pairs={{0,12},{1,11},{2,14},{3,9},{4,8},{5,15},{6,10},{7,13},{8,4},{9,3},... | collective-permute-start | bytes 196616 | tf_op jit(solution)/shard_map/ppermute | solution.py:109
  36.5 4.6 %collective-permute-start.18 = (bf16[4,64,128]{2,1,0:T(8,128)(2,1)S(1)}, bf16[4,64,128]{2,1,0:T(8,128)(2,1)S(1)}, u32[]{:S(2)}, u32[]{:S(2)}) collective-permute-start(bf16[4,64,128]{2,1,0:T(8,128)(2,1)S(1)} %get-tuple-element.20), channel_id=1, source_target_pairs={{0,4},{1,3},{2,6},{3,1},{4,0},{5,7},{6,2},{7,5},{8,12},{9,11},{10,... | collective-permute-start | bytes 196616 | tf_op jit(solution)/shard_map/ppermute | solution.py:109
  36.5 6.4 %collective-permute-start.13 = (bf16[4,64,128]{2,1,0:T(8,128)(2,1)S(1)}, bf16[4,64,128]{2,1,0:T(8,128)(2,1)S(1)}, u32[]{:S(2)}, u32[]{:S(2)}) collective-permute-start(bf16[4,64,128]{2,1,0:T(8,128)(2,1)S(1)} %get-tuple-element.16), channel_id=1, source_target_pairs={{0,20},{1,27},{2,22},{3,25},{4,16},{5,31},{6,18},{7,29},{8,28},{9,... | collective-permute-start | bytes 196616 | tf_op jit(solution)/shard_map/ppermute | solution.py:109

commit v3 on v2

v3 whole, which is shorter than its diff:
```python
import functools

import jax
import jax.numpy as jnp
from jax import lax
from jax.experimental import pallas as pl
from jax.experimental.pallas import tpu as pltpu
from jax.sharding import PartitionSpec as P

F32 = jnp.float32
VMEM = pl.BlockSpec(memory_space=pltpu.VMEM)
ANY = pl.BlockSpec(memory_space=pl.ANY)
SMEM = pl.BlockSpec(memory_space=pltpu.SMEM)
PARAMS = pltpu.CompilerParams(vmem_limit_bytes=16 * 1024 * 1024)


def cost(gflop=0):
    return pl.CostEstimate(flops=1 + gflop * 1_000_000_000, bytes_accessed=1, transcendentals=0)


def pair_bit(ct):
    return 1 + ct % 2


def masks_kernel(n_ct, n_k, n_local, vt, live, out):
    tr, ct = lax.axis_index("tr"), lax.axis_index("ct")
    cols = out.shape[1]
    bit = pair_bit(ct)
    turned = (bit == 2) & ((tr & 1) == 1)
    members = [(tr & ~bit) + jnp.where(turned, bit, 0), (tr & ~bit) + jnp.where(turned, 0, bit)]
    tile = lax.broadcasted_iota(jnp.int32, (1, cols), 1) // vt
    for e in range(n_ct):
        for k in range(n_k):
            mask = jnp.zeros((1, cols), F32)
            for t in range(cols // vt):
                mask = jnp.where(tile == t, live[k, (ct ^ e) * (cols // vt) + t].astype(F32), mask)
            out[pl.ds(e * n_k + k, 1)] = mask
    for i in range(n_local):
        row = ct * n_local + i
        both = jnp.where(tile < 1, live[row, members[0]].astype(F32), live[row, members[1]].astype(F32))
        out[pl.ds(n_ct * n_k + i, 1)] = both
    out[pl.ds(n_ct * n_k + n_local, 1)] = jnp.full((1, cols), (members[0] == tr).astype(F32))


def pack_kernel(count, *refs):
    out, at = refs[-1], 0
    for ref in refs[:count]:
        out[pl.ds(at, ref.shape[0])] = ref[...]
        at += ref.shape[0]


def blocks_kernel(n_ct, tiles_at, masks, *refs):
    own, theirs, arrays, outs = refs[:n_ct], refs[n_ct : 2 * n_ct], refs[2 * n_ct :], refs[-len(tiles_at) :]
    n_local, n_k, vt, cols = own[0].shape[1:]
    first = masks[pl.ds(n_ct * n_k + n_local, 1)] > 0
    lhs = {}
    for e in range(n_ct):
        for k in range(n_k):
            stacked = jnp.concatenate([arrays[n][at, k] for n, at in (tile[e] for tile in tiles_at)], axis=0)
            lhs[e, k] = stacked * masks[pl.ds(e * n_k + k, 1)].astype(jnp.bfloat16)
    step = min(2, n_local)
    for start in range(0, n_local, step):
        total = None
        for (e, k), left in lhs.items():
            rows = []
            for i in range(start, start + step):
                a, b = own[e][0, i, k], theirs[e][0, i, k]
                rows += [jnp.where(first, a, b), jnp.where(first, b, a)]
            term = lax.dot_general(
                left,
                jnp.concatenate(rows, axis=0),
                (((1,), (1,)), ((), ())),
                preferred_element_type=F32,
            )
            total = term if total is None else total + term
        for i in range(start, start + step):
            row_mask = masks[pl.ds(n_ct * n_k + i, 1), pl.ds(0, 2 * vt)]
            kept = total[:, (i - start) * 2 * vt : (i - start + 1) * 2 * vt] * row_mask
            for d, out in enumerate(outs):
                out[i] = kept[d * vt : (d + 1) * vt].astype(out.dtype)


def join_kernel(*refs):
    refs[-1][...] = jnp.zeros_like(refs[-1])


def place_kernel(shifts, *refs):
    parts, (out, stage, sems) = refs, refs[-3:]
    tr, ct = lax.axis_index("tr"), lax.axis_index("ct")
    wide = parts[0].shape[2]
    half = lax.broadcasted_iota(jnp.int32, (1, wide), 1) < wide // 2
    straight = pair_bit(ct) == 1
    own_first = (tr & (3 - pair_bit(ct))) == 0
    copies = []
    for n, by_core in enumerate(shifts):
        shift = sum(jnp.where(ct == c, z, 0) for c, z in enumerate(by_core))
        at = pl.multiple_of(((tr // 4) ^ shift) * 2 * wide, 2 * wide)
        for i in range(out.shape[0]):
            a, b = parts[2 * n][i], parts[2 * n + 1][i]
            lo, hi = jnp.where(own_first, a, b), jnp.where(own_first, b, a)
            across = pltpu.roll(jnp.where(half, hi, lo).astype(F32), wide // 2, 1).astype(lo.dtype)
            stage[n, i, :, pl.ds(0, wide)] = jnp.where(straight, lo, jnp.where(half, lo, hi))
            stage[n, i, :, pl.ds(wide, wide)] = jnp.where(straight, hi, across)
        copies.append(pltpu.make_async_copy(stage.at[n], out.at[:, :, pl.ds(at, 2 * wide)], sems.at[n]))
        copies[-1].start()
    for copy in copies:
        copy.wait()


def per_device(n_tr, n_ct, amplitudes, cycle_integrals, pair_live):
    n_i, vt, n_k, cols = amplitudes.shape
    n_j = cycle_integrals.shape[2]
    n_local = n_i // n_ct
    n_z = n_tr // 4
    ct = lax.axis_index("ct")
    far = sorted(range(1, n_z), key=lambda z: -z)
    shared, split = far[: len(far) // n_ct * n_ct], far[len(far) // n_ct * n_ct :]
    groups = [shared[n : n + n_ct] for n in range(0, len(shared), n_ct)]
    shifts = [[group[c ^ e] for c in range(n_ct)] for group in groups for e in range(n_ct)]
    shifts += [[z] * n_ct for z in split] + [[0] * n_ct]

    def beside(c):
        return 3 - pair_bit(c)

    def over_ct(value, e):
        return lax.ppermute(value, "ct", [(c, c ^ e) for c in range(n_ct)])

    def over_tr(value, move, e=0):
        pairs = [(r * n_ct + c, (r ^ move(c ^ e)) * n_ct + (c ^ e)) for r in range(n_tr) for c in range(n_ct)]
        return lax.ppermute(value, ("tr", "ct"), pairs)

    def call(kernel, shape, inputs, after=(), gflop=0, dtype=jnp.bfloat16, count=None):
        result = jax.ShapeDtypeStruct(shape, dtype)
        return pl.pallas_call(
            kernel,
            out_shape=result if count is None else [result] * count,
            in_specs=[VMEM] * len(inputs) + [ANY] * len(after),
            out_specs=VMEM if count is None else [VMEM] * count,
            compiler_params=PARAMS,
            cost_estimate=cost(gflop),
        )(*inputs, *after)

    def pack(parts, after=(), gflop=0):
        shape = (sum(part.shape[0] for part in parts), *parts[0].shape[1:])
        return call(functools.partial(pack_kernel, len(parts)), shape, parts, after, gflop)

    own_w = jnp.transpose(cycle_integrals, (2, 0, 3, 1))
    masks = pl.pallas_call(
        functools.partial(masks_kernel, n_ct, n_k, n_local, vt),
        out_shape=jax.ShapeDtypeStruct((n_ct * n_k + n_local + 1, cols), F32),
        in_specs=[SMEM],
        out_specs=VMEM,
        compiler_params=PARAMS,
        cost_estimate=cost(),
    )(pair_live)

    by_group = jnp.transpose(amplitudes, (0, 2, 1, 3)).reshape(n_ct, n_local, n_k, vt, cols)
    given = [lax.dynamic_index_in_dim(by_group, ct ^ e, 0) for e in range(n_ct)]
    own_a = [given[0]] + [over_ct(given[e], e) for e in range(1, n_ct)]

    own_parts = pack([own_w] + [over_ct(own_w, e) for e in range(1, n_ct)], [given[0]])
    some = [over_tr(own_w, lambda c, z=z: 4 * z) for z in split]
    whole = [over_tr(own_parts, lambda c, group=group: 4 * group[c]) for group in groups]
    their_a = [over_tr(value, pair_bit, e) for e, value in enumerate(given)]
    whole = pack(whole, [masks, *some], 3)
    some = some[0] if len(some) == 1 else pack(some)
    whole_rest = [over_ct(whole, e) for e in range(1, n_ct)]
    whole_side = over_tr(pack([whole, *whole_rest]), beside)
    some_rest = [over_ct(some, e) for e in range(1, n_ct)]
    some_side = over_tr(pack([own_parts, some, *some_rest], their_a), beside)

    n_whole, n_some = whole.shape[0], some.shape[0]
    of_group = [[(n, g * n_ct + (e ^ n)) for e in range(n_ct)] for g in range(len(groups)) for n in range(n_ct)]
    column = of_group + [[(n_ct + e, n) for e in range(n_ct)] for n in range(len(split))]
    column += [[(2 * n_ct, e) for e in range(n_ct)]]
    side_far = [[(0, n * n_whole + at) for n, at in tile] for tile in of_group]
    side_near = [[(0, n_ct + e * n_some + n) for e in range(n_ct)] for n in range(len(split))]
    side_near += [[(0, e) for e in range(n_ct)]]

    def blocks(tiles, arrays, after, gflop):
        kernel = functools.partial(blocks_kernel, n_ct, tiles)
        inputs = [masks, *own_a, *their_a, *arrays]
        return call(kernel, (n_local, vt, 2 * vt), inputs, after, gflop, count=len(tiles))

    near = blocks(column, [whole, *whole_rest, some, *some_rest, own_parts], [], 5)
    made = near[:1]
    near = [over_tr(b, lambda c, by=by: 4 * by[c]) if any(by) else b for b, by in zip(near, shifts)]
    side = blocks(side_far, [whole_side], made, 6)
    made = side[:1]
    side = [over_tr(b, lambda c, by=by: 4 * by[c] + beside(c)) for b, by in zip(side, shifts)]
    late = blocks(side_near, [some_side], [*made, *near[:2]], 3)
    done = call(join_kernel, (8, 128), [], side, 10, F32)
    side += [over_tr(b, lambda c, by=by: 4 * by[c] + beside(c)) for b, by in zip(late, shifts[len(shared) :])]

    moved = [block for both in zip(near, side) for block in both]
    result = pl.pallas_call(
        functools.partial(place_kernel, shifts),
        out_shape=jax.ShapeDtypeStruct((n_local, vt, n_tr * vt), jnp.bfloat16),
        in_specs=[VMEM] * len(moved) + [ANY],
        out_specs=ANY,
        scratch_shapes=[
            pltpu.VMEM((n_z, n_local, vt, 4 * vt), jnp.bfloat16),
            pltpu.SemaphoreType.DMA((n_z,)),
        ],
        compiler_params=PARAMS,
        cost_estimate=cost(),
    )(*moved, done)
    return result.reshape(n_local, vt, n_j, n_tr * vt)


def solution(mesh):
    return jax.shard_map(
        functools.partial(per_device, mesh.shape["tr"], mesh.shape["ct"]),
        mesh=mesh,
        in_specs=(P(None, "tr", None, "ct"), P(None, "ct", None, "tr"), P()),
        out_specs=P("ct", "tr", None, None),
        check_vma=False,
    )
```

time: 44 us -> 43.4 us (0.986)
  waiting for transfers between devices: 11.1 us -> 9.89 us
  local copies, waits for them, and re-layouts: 1.56 us -> 2.31 us
    ppermute x15 -> x13, waiting for transfers between devices: 11.1 us -> 8.79 us  [over_tr(): return lax.ppermute(value, ('tr', 'ct'), pairs)]
    ppermute x4, waiting for transfers between devices: 0.01 us -> 1.09 us  [over_ct(): return lax.ppermute(value, 'ct', [(c, c ^ e) for c in range(n_ct)])]
    ppermute x15 -> x13, starting transfers between devices: 24.6 us -> 23.5 us  [over_tr(): return lax.ppermute(value, ('tr', 'ct'), pairs)]
    ppermute x4, starting transfers between devices: 2.43 us -> 3.34 us  [over_ct(): return lax.ppermute(value, 'ct', [(c, c ^ e) for c in range(n_ct)])]
    unnamed x4, local copies, waits for them, and re-layouts: 0.01 us -> 0.79 us
    pallas_call x7 -> x9, Pallas kernels: 3.37 us -> 3.41 us  [the longest x8 2.45 us: call(): pl.pallas_call(kernel, out_shape=result if count is None else [result] *...]
  transfers between devices with their start and end apart: 19 -> 17, of which waited for: 9 -> 7; matrix products, arithmetic and copies ran while one was open for 4% -> 4% of each run, Pallas kernels for 7% -> 7%
where the time goes in v3:
time: 43.4 us; the launch traced here: 43.3 us
  starting transfers between devices  26.9 us (62%)
  waiting for transfers between devices  9.89 us (23%)
  Pallas kernels  4.09 us (9%)
  local copies, waits for them, and re-layouts  2.31 us (5%)
    ppermute x13, starting transfers between devices, over_tr(): return lax.ppermute(value, ('tr', 'ct'), pairs)  23.5 us
    ppermute x13, waiting for transfers between devices, over_tr(): return lax.ppermute(value, ('tr', 'ct'), pairs)  8.79 us
    ppermute x4, starting transfers between devices, over_ct(): return lax.ppermute(value, 'ct', [(c, c ^ e) for c in range(n_ct)])  3.34 us
    pallas_call x8, Pallas kernels, call(): pl.pallas_call(kernel, out_shape=result if count is None else [result] *...  2.45 us
    transpose x1, local copies, waits for them, and re-layouts, per_device(): jnp.transpose(amplitudes, (0, 2, 1, 3))  1.43 us
    ppermute x4, waiting for transfers between devices, over_ct(): return lax.ppermute(value, 'ct', [(c, c ^ e) for c in range(n_ct)])  1.09 us
    pallas_call x1, Pallas kernels, per_device(): pl.pallas_call(functools.partial(place_kernel, shifts), out_shape=jax.Sha...  0.96 us
  transfers between devices with their start and end apart: 17, of which 7 were waited for; matrix products, arithmetic and copies ran while one was open for 4% of the time, Pallas kernels for 7%

profile of v3, /device:TPU:0, one launch (start us, length us, event | category | flops | bytes accessed | tf_op | source)
XLA Modules:
  0.0 43.3 jit_solution(15035135028290975288)
XLA Ops:
  0.0 0.5 %collective-permute-start.3 = (bf16[1,2,64,512]{3,2,1,0:T(8,128)(2,1)}, bf16[1,2,64,512]{3,2,1,0:T(8,128)(2,1)S(1)}, u32[]{:S(2)}, u32[]{:S(2)}) collective-permute-start(bf16[1,2,64,512]{3,2,1,0:T(8,128)(2,1)} %bitcast.8), channel_id=1, source_target_pairs={{0,1},{1,0},{2,3},{3,2},{4,5},{5,4},{6,7},{7,6},{8,9},{9,8},{10,11... | collective-permute-start | bytes 393224 | tf_op jit(solution)/shard_map/ppermute | solution.py:126
  0.5 1.4 %copy.4 = bf16[8,2,64,512]{3,2,1,0:T(8,128)(2,1)S(1)} copy(bf16[8,2,64,512]{3,1,2,0:T(2,128)(2,1)} %bitcast.12) | data formatting | bytes 2097152 | tf_op jit(solution)/shard_map/transpose | solution.py:157
  1.9 0.0 copy-start
  1.9 0.1 constant_dynamic-slice_fusion
  2.0 0.0 collective-permute-done.3.refs_1_
  2.0 0.8 %copy-done = bf16[2,512,1,64]{1,3,2,0:T(8,128)(2,1)S(1)} copy-done((bf16[2,512,1,64]{1,3,2,0:T(8,128)(2,1)S(1)}, bf16[2,512,1,64]{1,3,2,0:T(8,128)(2,1)}, u32[]{:S(2)}) %copy-start) | copy-done | bytes 131096
  2.8 0.0 copy-start.1
  2.8 4.7 %collective-permute-start.4 = (bf16[2,2,64,512]{3,2,1,0:T(8,128)(2,1)S(1)}, bf16[2,2,64,512]{3,2,1,0:T(8,128)(2,1)S(1)}, u32[]{:S(2)}, u32[]{:S(2)}) collective-permute-start(bf16[2,2,64,512]{3,2,1,0:T(8,128)(2,1)S(1)} %shard_map.38.refs_8_.refs_0_), channel_id=1, source_target_pairs={{0,24},{1,17},{2,26},{3,19},{4,28},{5,21},{6,30},{7,23},{8,16},{9,... | collective-permute-start | bytes 786440 | tf_op jit(solution)/shard_map/ppermute | solution.py:130
  7.5 0.0 collective-permute-start.5
  7.5 1.6 %collective-permute-start.2 = (bf16[1,4,2,64,512]{4,3,2,1,0:T(8,128)(2,1)S(1)}, bf16[1,4,2,64,512]{4,3,2,1,0:T(8,128)(2,1)S(1)}, u32[]{:S(2)}, u32[]{:S(2)}) collective-permute-start(bf16[1,4,2,64,512]{4,3,2,1,0:T(8,128)(2,1)S(1)} %get-tuple-element.21), channel_id=1, source_target_pairs={{0,5},{1,2},{2,7},{3,0},{4,1},{5,6},{6,3},{7,4},{8,13},{9,10},{10,... | collective-permute-start | bytes 1572872 | tf_op jit(solution)/shard_map/ppermute | solution.py:130
  9.1 0.0 collective-permute-start
  9.1 1.5 %collective-permute-start.1 = (bf16[1,4,2,64,512]{4,3,2,1,0:T(8,128)(2,1)S(1)}, bf16[1,4,2,64,512]{4,3,2,1,0:T(8,128)(2,1)S(1)}, u32[]{:S(2)}, u32[]{:S(2)}) collective-permute-start(bf16[1,4,2,64,512]{4,3,2,1,0:T(8,128)(2,1)S(1)} %get-tuple-element.22.refs_2_.refs_0_), channel_id=1, source_target_pairs={{0,2},{1,5},{2,0},{3,7},{4,6},{5,1},{6,4},{7,3},{8,10},{9,13},{10,... | collective-permute-start | bytes 1572872 | tf_op jit(solution)/shard_map/ppermute | solution.py:130
  10.6 0.0 copy-done.1
  10.6 0.7 %shard_map.37.refs_1_.masks = f32[9,512]{1,0:T(8,128)S(1)} custom-call(s32[8,16]{1,0:T(8,128)S(1)} %copy-done.1), custom_call_target="tpu_custom_call" | custom-call | flops 1 | bytes 1 | tf_op jit(solution)/shard_map/pallas_call | solution.py:148
  11.3 4.3 %collective-permute-done.5.refs_2_.refs_6_.refs_1_ = bf16[1,2,64,512]{3,2,1,0:T(8,128)(2,1)S(1)} collective-permute-done((bf16[1,2,64,512]{3,2,1,0:T(8,128)(2,1)S(1)}, bf16[1,2,64,512]{3,2,1,0:T(8,128)(2,1)S(1)}, u32[]{:S(2)}, u32[]{:S(2)}) %collective-permute-start.5) | collective-permute-done | bytes 131104 | tf_op jit(solution)/shard_map/ppermute | solution.py:130
  15.6 0.0 collective-permute-done.4.refs_0_
  15.6 2.8 %collective-permute-start.6 = (bf16[2,2,64,512]{3,2,1,0:T(8,128)(2,1)S(1)}, bf16[2,2,64,512]{3,2,1,0:T(8,128)(2,1)S(1)}, u32[]{:S(2)}, u32[]{:S(2)}) collective-permute-start(bf16[2,2,64,512]{3,2,1,0:T(8,128)(2,1)S(1)} %shard_map.39.refs_4_.refs_0_), channel_id=1, source_target_pairs={{0,1},{1,0},{2,3},{3,2},{4,5},{5,4},{6,7},{7,6},{8,9},{9,8},{10,11... | collective-permute-start | bytes 786440 | tf_op jit(solution)/shard_map/ppermute | solution.py:126
  18.4 0.1 collective-permute-start.7
  18.5 1.1 %collective-permute-done.6.refs_5_.refs_1_ = bf16[2,2,64,512]{3,2,1,0:T(8,128)(2,1)S(1)} collective-permute-done((bf16[2,2,64,512]{3,2,1,0:T(8,128)(2,1)S(1)}, bf16[2,2,64,512]{3,2,1,0:T(8,128)(2,1)S(1)}, u32[]{:S(2)}, u32[]{:S(2)}) %collective-permute-start.6) | collective-permute-done | bytes 262176 | tf_op jit(solution)/shard_map/ppermute | solution.py:126
  19.6 1.7 %collective-permute-start.9 = (bf16[4,2,64,512]{3,2,1,0:T(8,128)(2,1)S(1)}, bf16[4,2,64,512]{3,2,1,0:T(8,128)(2,1)S(1)}, u32[]{:S(2)}, u32[]{:S(2)}) collective-permute-start(bf16[4,2,64,512]{3,2,1,0:T(8,128)(2,1)S(1)} %shard_map.41), channel_id=1, source_target_pairs={{0,4},{1,3},{2,6},{3,1},{4,0},{5,7},{6,2},{7,5},{8,12},{9,11},{10,... | collective-permute-start | bytes 1572872 | tf_op jit(solution)/shard_map/ppermute | solution.py:130
  21.3 0.0 collective-permute-done.7.refs_7_.refs_2_
  21.3 0.0 collective-permute-done.2.refs_3_.refs_4_
  21.3 0.4 collective-permute-done.1.refs_2_.refs_3_
  21.8 1.6 %collective-permute-start.14 = (bf16[4,2,64,512]{3,2,1,0:T(8,128)(2,1)S(1)}, bf16[4,2,64,512]{3,2,1,0:T(8,128)(2,1)S(1)}, u32[]{:S(2)}, u32[]{:S(2)}) collective-permute-start(bf16[4,2,64,512]{3,2,1,0:T(8,128)(2,1)S(1)} %shard_map.43), channel_id=1, source_target_pairs={{0,4},{1,3},{2,6},{3,1},{4,0},{5,7},{6,2},{7,5},{8,12},{9,11},{10,... | collective-permute-start | bytes 1572872 | tf_op jit(solution)/shard_map/ppermute | solution.py:130
  23.3 0.0 collective-permute-done.refs_1_
  23.3 0.7 %shard_map.40 = (bf16[4,64,128]{2,1,0:T(8,128)(2,1)S(1)}, bf16[4,64,128]{2,1,0:T(8,128)(2,1)S(1)}, bf16[4,64,128]{2,1,0:T(8,128)(2,1)S(1)}, bf16[4,64,128]{2,1,0:T(8,128)(2,1)S(1)}) custom-call(f32[9,512]{1,0:T(8,128)S(1)} %shard_map.37.refs_1_.masks, bf16[1,4,2,64,512]{4,3,2,1,0:T(8,128)(2,1)S(1)} %get-tuple-element.22.refs_2_.refs_0_, ...), custom_call_target="tpu_custom_call" | custom-call | flops 5000000000 | bytes 1 | tf_op jit(solution)/shard_map/pallas_call | solution.py:134
  24.1 1.4 %collective-permute-start.11 = (bf16[4,64,128]{2,1,0:T(8,128)(2,1)S(1)}, bf16[4,64,128]{2,1,0:T(8,128)(2,1)S(1)}, u32[]{:S(2)}, u32[]{:S(2)}) collective-permute-start(bf16[4,64,128]{2,1,0:T(8,128)(2,1)S(1)} %get-tuple-element.15), channel_id=1, source_target_pairs={{0,16},{1,25},{2,18},{3,27},{4,20},{5,29},{6,22},{7,31},{8,24},{9,... | collective-permute-start | bytes 196616 | tf_op jit(solution)/shard_map/ppermute | solution.py:130
  25.5 1.4 %collective-permute-start.13 = (bf16[4,64,128]{2,1,0:T(8,128)(2,1)S(1)}, bf16[4,64,128]{2,1,0:T(8,128)(2,1)S(1)}, u32[]{:S(2)}, u32[]{:S(2)}) collective-permute-start(bf16[4,64,128]{2,1,0:T(8,128)(2,1)S(1)} %get-tuple-element.17), channel_id=1, source_target_pairs={{0,8},{1,9},{2,10},{3,11},{4,12},{5,13},{6,14},{7,15},{8,0},{9,1},... | collective-permute-start | bytes 196616 | tf_op jit(solution)/shard_map/ppermute | solution.py:130
  26.9 1.7 %collective-permute-start.8 = (bf16[4,64,128]{2,1,0:T(8,128)(2,1)S(1)}, bf16[4,64,128]{2,1,0:T(8,128)(2,1)S(1)}, u32[]{:S(2)}, u32[]{:S(2)}) collective-permute-start(bf16[4,64,128]{2,1,0:T(8,128)(2,1)S(1)} %get-tuple-element.13.refs_5_), channel_id=1, source_target_pairs={{0,24},{1,17},{2,26},{3,19},{4,28},{5,21},{6,30},{7,23},{8,16},{9,... | collective-permute-start | bytes 196616 | tf_op jit(solution)/shard_map/ppermute | solution.py:130
  28.5 0.3 collective-permute-done.9.refs_4_
  28.9 0.8 %shard_map.42 = (bf16[4,64,128]{2,1,0:T(8,128)(2,1)S(1)}, bf16[4,64,128]{2,1,0:T(8,128)(2,1)S(1)}) custom-call(f32[9,512]{1,0:T(8,128)S(1)} %shard_map.37.refs_1_.masks, bf16[1,4,2,64,512]{4,3,2,1,0:T(8,128)(2,1)S(1)} %get-tuple-element.22.refs_2_.refs_0_, bf16[1,4,2,64,512]{4,3,2,1,0:T(8,128)(2,1)S(1)} %collective-permute-done.refs_1_, ...), custom_call_target="tpu_custom_call" | custom-call | flops 6000000000 | bytes 1 | tf_op jit(solution)/shard_map/pallas_call | solution.py:134
  29.7 3.9 %collective-permute-start.12 = (bf16[4,64,128]{2,1,0:T(8,128)(2,1)S(1)}, bf16[4,64,128]{2,1,0:T(8,128)(2,1)S(1)}, u32[]{:S(2)}, u32[]{:S(2)}) collective-permute-start(bf16[4,64,128]{2,1,0:T(8,128)(2,1)S(1)} %get-tuple-element.16), channel_id=1, source_target_pairs={{0,20},{1,27},{2,22},{3,25},{4,16},{5,31},{6,18},{7,29},{8,28},{9,... | collective-permute-start | bytes 196616 | tf_op jit(solution)/shard_map/ppermute | solution.py:130
  33.5 0.0 collective-permute-done.11.refs_7_.refs_2_
  33.5 1.1 %collective-permute-start.10 = (bf16[4,64,128]{2,1,0:T(8,128)(2,1)S(1)}, bf16[4,64,128]{2,1,0:T(8,128)(2,1)S(1)}, u32[]{:S(2)}, u32[]{:S(2)}) collective-permute-start(bf16[4,64,128]{2,1,0:T(8,128)(2,1)S(1)} %get-tuple-element.14.refs_5_), channel_id=1, source_target_pairs={{0,28},{1,19},{2,30},{3,17},{4,24},{5,23},{6,26},{7,21},{8,20},{9,... | collective-permute-start | bytes 196616 | tf_op jit(solution)/shard_map/ppermute | solution.py:130
  34.7 0.0 collective-permute-done.8.refs_6_.refs_0_
  34.7 0.0 collective-permute-done.14.refs_4_
  34.7 0.8 %shard_map.44 = (bf16[4,64,128]{2,1,0:T(8,128)(2,1)S(1)}, bf16[4,64,128]{2,1,0:T(8,128)(2,1)S(1)}) custom-call(f32[9,512]{1,0:T(8,128)S(1)} %shard_map.37.refs_1_.masks, bf16[1,4,2,64,512]{4,3,2,1,0:T(8,128)(2,1)S(1)} %get-tuple-element.22.refs_2_.refs_0_, bf16[1,4,2,64,512]{4,3,2,1,0:T(8,128)(2,1)S(1)} %collective-permute-done.refs_1_, ...), custom_call_target="tpu_custom_call" | custom-call | flops 3000000000 | bytes 1 | tf_op jit(solution)/shard_map/pallas_call | solution.py:134
  35.5 2.5 %collective-permute-start.15 = (bf16[4,64,128]{2,1,0:T(8,128)(2,1)S(1)}, bf16[4,64,128]{2,1,0:T(8,128)(2,1)S(1)}, u32[]{:S(2)}, u32[]{:S(2)}) collective-permute-start(bf16[4,64,128]{2,1,0:T(8,128)(2,1)S(1)} %get-tuple-element.18), channel_id=1, source_target_pairs={{0,12},{1,11},{2,14},{3,9},{4,8},{5,15},{6,10},{7,13},{8,4},{9,3},... | collective-permute-start | bytes 196616 | tf_op jit(solution)/shard_map/ppermute | solution.py:130
  38.0 0.5 %collective-permute-start.16 = (bf16[4,64,128]{2,1,0:T(8,128)(2,1)S(1)}, bf16[4,64,128]{2,1,0:T(8,128)(2,1)S(1)}, u32[]{:S(2)}, u32[]{:S(2)}) collective-permute-start(bf16[4,64,128]{2,1,0:T(8,128)(2,1)S(1)} %get-tuple-element.20), channel_id=1, source_target_pairs={{0,4},{1,3},{2,6},{3,1},{4,0},{5,7},{6,2},{7,5},{8,12},{9,11},{10,... | collective-permute-start | bytes 196616 | tf_op jit(solution)/shard_map/ppermute | solution.py:130
  38.5 0.0 collective-permute-done.12.refs_1_.refs_3_
  38.5 2.1 %collective-permute-done.10.refs_0_.refs_1_ = bf16[4,64,128]{2,1,0:T(8,128)(2,1)S(1)} collective-permute-done((bf16[4,64,128]{2,1,0:T(8,128)(2,1)S(1)}, bf16[4,64,128]{2,1,0:T(8,128)(2,1)S(1)}, u32[]{:S(2)}, u32[]{:S(2)}) %collective-permute-start.10) | collective-permute-done | bytes 65568 | tf_op jit(solution)/shard_map/ppermute | solution.py:130
  40.6 0.0 collective-permute-done.13.refs_4_
  40.6 0.9 %collective-permute-done.15.refs_5_ = bf16[4,64,128]{2,1,0:T(8,128)(2,1)S(1)} collective-permute-done((bf16[4,64,128]{2,1,0:T(8,128)(2,1)S(1)}, bf16[4,64,128]{2,1,0:T(8,128)(2,1)S(1)}, u32[]{:S(2)}, u32[]{:S(2)}) %collective-permute-start.15) | collective-permute-done | bytes 65568 | tf_op jit(solution)/shard_map/ppermute | solution.py:130
  41.6 0.8 %collective-permute-done.16.refs_7_ = bf16[4,64,128]{2,1,0:T(8,128)(2,1)S(1)} collective-permute-done((bf16[4,64,128]{2,1,0:T(8,128)(2,1)S(1)}, bf16[4,64,128]{2,1,0:T(8,128)(2,1)S(1)}, u32[]{:S(2)}, u32[]{:S(2)}) %collective-permute-start.16) | collective-permute-done | bytes 65568 | tf_op jit(solution)/shard_map/ppermute | solution.py:130
  42.3 1.0 %shard_map.46 = bf16[4,64,1024]{2,1,0:T(8,128)(2,1)} custom-call(bf16[4,64,128]{2,1,0:T(8,128)(2,1)S(1)} %collective-permute-done.8.refs_6_.refs_0_, bf16[4,64,128]{2,1,0:T(8,128)(2,1)S(1)} %collective-permute-done.10.refs_0_.refs_1_, bf16[4,64,128]{2,1,0:T(8,128)(2,1)S(1)} %collective-permute-done.11.refs_7_.refs_2_, ...), custom_call_target="tpu_custom_call" | custom-call | flops 1 | bytes 1 | tf_op jit(solution)/shard_map/pallas_call | solution.py:196
  (5 shorter events, 0.1 us)
Async XLA Ops:
  0.0 2.0 %collective-permute-start.3 = (bf16[1,2,64,512]{3,2,1,0:T(8,128)(2,1)}, bf16[1,2,64,512]{3,2,1,0:T(8,128)(2,1)S(1)}, u32[]{:S(2)}, u32[]{:S(2)}) collective-permute-start(bf16[1,2,64,512]{3,2,1,0:T(8,128)(2,1)} %bitcast.8), channel_id=1, source_target_pairs={{0,1},{1,0},{2,3},{3,2},{4,5},{5,4},{6,7},{7,6},{8,9},{9,8},{10,11... | collective-permute-start | bytes 393224 | tf_op jit(solution)/shard_map/ppermute | solution.py:126
  1.9 0.9 %copy-start = (bf16[2,512,1,64]{1,3,2,0:T(8,128)(2,1)S(1)}, bf16[2,512,1,64]{1,3,2,0:T(8,128)(2,1)}, u32[]{:S(2)}) copy-start(bf16[2,512,1,64]{1,3,2,0:T(8,128)(2,1)} %param.4) | copy-start | bytes 393220
  2.8 7.8 %copy-start.1 = (s32[8,16]{1,0:T(8,128)S(1)}, s32[8,16]{1,0:T(8,128)}, u32[]{:S(2)}) copy-start(s32[8,16]{1,0:T(8,128)} %live.1) | copy-start | bytes 1540
  2.8 12.7 %collective-permute-start.4 = (bf16[2,2,64,512]{3,2,1,0:T(8,128)(2,1)S(1)}, bf16[2,2,64,512]{3,2,1,0:T(8,128)(2,1)S(1)}, u32[]{:S(2)}, u32[]{:S(2)}) collective-permute-start(bf16[2,2,64,512]{3,2,1,0:T(8,128)(2,1)S(1)} %shard_map.38.refs_8_.refs_0_), channel_id=1, source_target_pairs={{0,24},{1,17},{2,26},{3,19},{4,28},{5,21},{6,30},{7,23},{8,16},{9,... | collective-permute-start | bytes 786440 | tf_op jit(solution)/shard_map/ppermute | solution.py:130
  7.5 8.1 %collective-permute-start.5 = (bf16[1,2,64,512]{3,2,1,0:T(8,128)(2,1)S(1)}, bf16[1,2,64,512]{3,2,1,0:T(8,128)(2,1)S(1)}, u32[]{:S(2)}, u32[]{:S(2)}) collective-permute-start(bf16[1,2,64,512]{3,2,1,0:T(8,128)(2,1)S(1)} %bitcast.10), channel_id=1, source_target_pairs={{0,8},{1,9},{2,10},{3,11},{4,12},{5,13},{6,14},{7,15},{8,0},{9,1},... | collective-permute-start | bytes 393224 | tf_op jit(solution)/shard_map/ppermute | solution.py:130
  7.5 13.8 %collective-permute-start.2 = (bf16[1,4,2,64,512]{4,3,2,1,0:T(8,128)(2,1)S(1)}, bf16[1,4,2,64,512]{4,3,2,1,0:T(8,128)(2,1)S(1)}, u32[]{:S(2)}, u32[]{:S(2)}) collective-permute-start(bf16[1,4,2,64,512]{4,3,2,1,0:T(8,128)(2,1)S(1)} %get-tuple-element.21), channel_id=1, source_target_pairs={{0,5},{1,2},{2,7},{3,0},{4,1},{5,6},{6,3},{7,4},{8,13},{9,10},{10,... | collective-permute-start | bytes 1572872 | tf_op jit(solution)/shard_map/ppermute | solution.py:130
  9.1 14.2 %collective-permute-start = (bf16[1,4,2,64,512]{4,3,2,1,0:T(8,128)(2,1)S(1)}, bf16[1,4,2,64,512]{4,3,2,1,0:T(8,128)(2,1)S(1)}, u32[]{:S(2)}, u32[]{:S(2)}) collective-permute-start(bf16[1,4,2,64,512]{4,3,2,1,0:T(8,128)(2,1)S(1)} %get-tuple-element.21), channel_id=1, source_target_pairs={{0,1},{1,0},{2,3},{3,2},{4,5},{5,4},{6,7},{7,6},{8,9},{9,8},{10,11... | collective-permute-start | bytes 1572872 | tf_op jit(solution)/shard_map/ppermute | solution.py:126
  9.1 12.6 %collective-permute-start.1 = (bf16[1,4,2,64,512]{4,3,2,1,0:T(8,128)(2,1)S(1)}, bf16[1,4,2,64,512]{4,3,2,1,0:T(8,128)(2,1)S(1)}, u32[]{:S(2)}, u32[]{:S(2)}) collective-permute-start(bf16[1,4,2,64,512]{4,3,2,1,0:T(8,128)(2,1)S(1)} %get-tuple-element.22.refs_2_.refs_0_), channel_id=1, source_target_pairs={{0,2},{1,5},{2,0},{3,7},{4,6},{5,1},{6,4},{7,3},{8,10},{9,13},{10,... | collective-permute-start | bytes 1572872 | tf_op jit(solution)/shard_map/ppermute | solution.py:130
  15.6 4.0 %collective-permute-start.6 = (bf16[2,2,64,512]{3,2,1,0:T(8,128)(2,1)S(1)}, bf16[2,2,64,512]{3,2,1,0:T(8,128)(2,1)S(1)}, u32[]{:S(2)}, u32[]{:S(2)}) collective-permute-start(bf16[2,2,64,512]{3,2,1,0:T(8,128)(2,1)S(1)} %shard_map.39.refs_4_.refs_0_), channel_id=1, source_target_pairs={{0,1},{1,0},{2,3},{3,2},{4,5},{5,4},{6,7},{7,6},{8,9},{9,8},{10,11... | collective-permute-start | bytes 786440 | tf_op jit(solution)/shard_map/ppermute | solution.py:126
  18.4 2.9 %collective-permute-start.7 = (bf16[1,2,64,512]{3,2,1,0:T(8,128)(2,1)S(1)}, bf16[1,2,64,512]{3,2,1,0:T(8,128)(2,1)S(1)}, u32[]{:S(2)}, u32[]{:S(2)}) collective-permute-start(bf16[1,2,64,512]{3,2,1,0:T(8,128)(2,1)S(1)} %collective-permute-done.5.refs_2_.refs_6_.refs_1_), channel_id=1, source_target_pairs={{0,1},{1,0},{2,3},{3,2},{4,5},{5,4},{6,7},{7,6},{8,9},{9,8},{10,11... | collective-permute-start | bytes 393224 | tf_op jit(solution)/shard_map/ppermute | solution.py:126
  19.6 9.2 %collective-permute-start.9 = (bf16[4,2,64,512]{3,2,1,0:T(8,128)(2,1)S(1)}, bf16[4,2,64,512]{3,2,1,0:T(8,128)(2,1)S(1)}, u32[]{:S(2)}, u32[]{:S(2)}) collective-permute-start(bf16[4,2,64,512]{3,2,1,0:T(8,128)(2,1)S(1)} %shard_map.41), channel_id=1, source_target_pairs={{0,4},{1,3},{2,6},{3,1},{4,0},{5,7},{6,2},{7,5},{8,12},{9,11},{10,... | collective-permute-start | bytes 1572872 | tf_op jit(solution)/shard_map/ppermute | solution.py:130
  21.8 12.9 %collective-permute-start.14 = (bf16[4,2,64,512]{3,2,1,0:T(8,128)(2,1)S(1)}, bf16[4,2,64,512]{3,2,1,0:T(8,128)(2,1)S(1)}, u32[]{:S(2)}, u32[]{:S(2)}) collective-permute-start(bf16[4,2,64,512]{3,2,1,0:T(8,128)(2,1)S(1)} %shard_map.43), channel_id=1, source_target_pairs={{0,4},{1,3},{2,6},{3,1},{4,0},{5,7},{6,2},{7,5},{8,12},{9,11},{10,... | collective-permute-start | bytes 1572872 | tf_op jit(solution)/shard_map/ppermute | solution.py:130
  24.1 9.5 %collective-permute-start.11 = (bf16[4,64,128]{2,1,0:T(8,128)(2,1)S(1)}, bf16[4,64,128]{2,1,0:T(8,128)(2,1)S(1)}, u32[]{:S(2)}, u32[]{:S(2)}) collective-permute-start(bf16[4,64,128]{2,1,0:T(8,128)(2,1)S(1)} %get-tuple-element.15), channel_id=1, source_target_pairs={{0,16},{1,25},{2,18},{3,27},{4,20},{5,29},{6,22},{7,31},{8,24},{9,... | collective-permute-start | bytes 196616 | tf_op jit(solution)/shard_map/ppermute | solution.py:130
  25.5 15.1 %collective-permute-start.13 = (bf16[4,64,128]{2,1,0:T(8,128)(2,1)S(1)}, bf16[4,64,128]{2,1,0:T(8,128)(2,1)S(1)}, u32[]{:S(2)}, u32[]{:S(2)}) collective-permute-start(bf16[4,64,128]{2,1,0:T(8,128)(2,1)S(1)} %get-tuple-element.17), channel_id=1, source_target_pairs={{0,8},{1,9},{2,10},{3,11},{4,12},{5,13},{6,14},{7,15},{8,0},{9,1},... | collective-permute-start | bytes 196616 | tf_op jit(solution)/shard_map/ppermute | solution.py:130
  26.9 7.8 %collective-permute-start.8 = (bf16[4,64,128]{2,1,0:T(8,128)(2,1)S(1)}, bf16[4,64,128]{2,1,0:T(8,128)(2,1)S(1)}, u32[]{:S(2)}, u32[]{:S(2)}) collective-permute-start(bf16[4,64,128]{2,1,0:T(8,128)(2,1)S(1)} %get-tuple-element.13.refs_5_), channel_id=1, source_target_pairs={{0,24},{1,17},{2,26},{3,19},{4,28},{5,21},{6,30},{7,23},{8,16},{9,... | collective-permute-start | bytes 196616 | tf_op jit(solution)/shard_map/ppermute | solution.py:130
  29.7 8.8 %collective-permute-start.12 = (bf16[4,64,128]{2,1,0:T(8,128)(2,1)S(1)}, bf16[4,64,128]{2,1,0:T(8,128)(2,1)S(1)}, u32[]{:S(2)}, u32[]{:S(2)}) collective-permute-start(bf16[4,64,128]{2,1,0:T(8,128)(2,1)S(1)} %get-tuple-element.16), channel_id=1, source_target_pairs={{0,20},{1,27},{2,22},{3,25},{4,16},{5,31},{6,18},{7,29},{8,28},{9,... | collective-permute-start | bytes 196616 | tf_op jit(solution)/shard_map/ppermute | solution.py:130
  33.5 7.1 %collective-permute-start.10 = (bf16[4,64,128]{2,1,0:T(8,128)(2,1)S(1)}, bf16[4,64,128]{2,1,0:T(8,128)(2,1)S(1)}, u32[]{:S(2)}, u32[]{:S(2)}) collective-permute-start(bf16[4,64,128]{2,1,0:T(8,128)(2,1)S(1)} %get-tuple-element.14.refs_5_), channel_id=1, source_target_pairs={{0,28},{1,19},{2,30},{3,17},{4,24},{5,23},{6,26},{7,21},{8,20},{9,... | collective-permute-start | bytes 196616 | tf_op jit(solution)/shard_map/ppermute | solution.py:130
  35.5 6.0 %collective-permute-start.15 = (bf16[4,64,128]{2,1,0:T(8,128)(2,1)S(1)}, bf16[4,64,128]{2,1,0:T(8,128)(2,1)S(1)}, u32[]{:S(2)}, u32[]{:S(2)}) collective-permute-start(bf16[4,64,128]{2,1,0:T(8,128)(2,1)S(1)} %get-tuple-element.18), channel_id=1, source_target_pairs={{0,12},{1,11},{2,14},{3,9},{4,8},{5,15},{6,10},{7,13},{8,4},{9,3},... | collective-permute-start | bytes 196616 | tf_op jit(solution)/shard_map/ppermute | solution.py:130
  38.0 4.3 %collective-permute-start.16 = (bf16[4,64,128]{2,1,0:T(8,128)(2,1)S(1)}, bf16[4,64,128]{2,1,0:T(8,128)(2,1)S(1)}, u32[]{:S(2)}, u32[]{:S(2)}) collective-permute-start(bf16[4,64,128]{2,1,0:T(8,128)(2,1)S(1)} %get-tuple-element.20), channel_id=1, source_target_pairs={{0,4},{1,3},{2,6},{3,1},{4,0},{5,7},{6,2},{7,5},{8,12},{9,11},{10,... | collective-permute-start | bytes 196616 | tf_op jit(solution)/shard_map/ppermute | solution.py:130

commit v4 on v3

--- a/solution.py
+++ b/solution.py
@@ -164,16 +164,15 @@
     their_a = [over_tr(value, pair_bit, e) for e, value in enumerate(given)]
     whole = pack(whole, [masks, *some], 3)
     some = some[0] if len(some) == 1 else pack(some)
+    whole_side = [over_tr(whole, beside, e) for e in range(n_ct)]
     whole_rest = [over_ct(whole, e) for e in range(1, n_ct)]
-    whole_side = over_tr(pack([whole, *whole_rest]), beside)
     some_rest = [over_ct(some, e) for e in range(1, n_ct)]
     some_side = over_tr(pack([own_parts, some, *some_rest], their_a), beside)
 
-    n_whole, n_some = whole.shape[0], some.shape[0]
+    n_some = some.shape[0]
     of_group = [[(n, g * n_ct + (e ^ n)) for e in range(n_ct)] for g in range(len(groups)) for n in range(n_ct)]
     column = of_group + [[(n_ct + e, n) for e in range(n_ct)] for n in range(len(split))]
     column += [[(2 * n_ct, e) for e in range(n_ct)]]
-    side_far = [[(0, n * n_whole + at) for n, at in tile] for tile in of_group]
     side_near = [[(0, n_ct + e * n_some + n) for e in range(n_ct)] for n in range(len(split))]
     side_near += [[(0, e) for e in range(n_ct)]]
 
@@ -182,10 +181,10 @@
         inputs = [masks, *own_a, *their_a, *arrays]
         return call(kernel, (n_local, vt, 2 * vt), inputs, after, gflop, count=len(tiles))
 
-    near = blocks(column, [whole, *whole_rest, some, *some_rest, own_parts], [], 5)
+    near = blocks(column, [whole, *whole_rest, some, *some_rest, own_parts], [], 0)
     made = near[:1]
     near = [over_tr(b, lambda c, by=by: 4 * by[c]) if any(by) else b for b, by in zip(near, shifts)]
-    side = blocks(side_far, [whole_side], made, 6)
+    side = blocks(of_group, whole_side, made, 6)
     made = side[:1]
     side = [over_tr(b, lambda c, by=by: 4 * by[c] + beside(c)) for b, by in zip(side, shifts)]
     late = blocks(side_near, [some_side], [*made, *near[:2]], 3)

time: 43.4 us -> 41.9 us (0.965)
  starting transfers between devices: 26.9 us -> 22.7 us
  waiting for transfers between devices: 9.89 us -> 12.6 us
    ppermute x13 -> x14, waiting for transfers between devices: 8.79 us -> 12.6 us  [over_tr(): return lax.ppermute(value, ('tr', 'ct'), pairs)]
    ppermute x13 -> x14, starting transfers between devices: 23.5 us -> 19.9 us  [over_tr(): return lax.ppermute(value, ('tr', 'ct'), pairs)]
    ppermute x4, waiting for transfers between devices: 1.09 us -> 0.01 us  [over_ct(): return lax.ppermute(value, 'ct', [(c, c ^ e) for c in range(n_ct)])]
    ppermute x4, starting transfers between devices: 3.34 us -> 2.83 us  [over_ct(): return lax.ppermute(value, 'ct', [(c, c ^ e) for c in range(n_ct)])]
    pallas_call x8 -> x7, Pallas kernels: 2.45 us -> 2.43 us  [call(): pl.pallas_call(kernel, out_shape=result if count is None else [result] *...]
  transfers between devices with their start and end apart: 17 -> 18, of which waited for: 7 -> 6; matrix products, arithmetic and copies ran while one was open for 4% -> 4% of each run, Pallas kernels for 7% -> 7%
where the time goes in v4:
time: 41.9 us; the launch traced here: 41.7 us
  starting transfers between devices  22.7 us (54%)
  waiting for transfers between devices  12.6 us (30%)
  Pallas kernels  4.06 us (10%)
  local copies, waits for them, and re-layouts  2.31 us (6%)
    ppermute x14, starting transfers between devices, over_tr(): return lax.ppermute(value, ('tr', 'ct'), pairs)  19.9 us
    ppermute x14, waiting for transfers between devices, over_tr(): return lax.ppermute(value, ('tr', 'ct'), pairs)  12.6 us
    ppermute x4, starting transfers between devices, over_ct(): return lax.ppermute(value, 'ct', [(c, c ^ e) for c in range(n_ct)])  2.83 us
    pallas_call x7, Pallas kernels, call(): pl.pallas_call(kernel, out_shape=result if count is None else [result] *...  2.43 us
    transpose x1, local copies, waits for them, and re-layouts, per_device(): jnp.transpose(amplitudes, (0, 2, 1, 3))  1.43 us
    pallas_call x1, Pallas kernels, per_device(): pl.pallas_call(functools.partial(place_kernel, shifts), out_shape=jax.Sha...  0.95 us
  transfers between devices with their start and end apart: 18, of which 6 were waited for; matrix products, arithmetic and copies ran while one was open for 4% of the time, Pallas kernels for 7%

profile of v4, /device:TPU:0, one launch (start us, length us, event | category | flops | bytes accessed | tf_op | source)
XLA Modules:
  0.0 41.7 jit_solution(11813753014710779518)
XLA Ops:
  0.0 0.5 %collective-permute-start.3 = (bf16[1,2,64,512]{3,2,1,0:T(8,128)(2,1)}, bf16[1,2,64,512]{3,2,1,0:T(8,128)(2,1)S(1)}, u32[]{:S(2)}, u32[]{:S(2)}) collective-permute-start(bf16[1,2,64,512]{3,2,1,0:T(8,128)(2,1)} %bitcast.8), channel_id=1, source_target_pairs={{0,1},{1,0},{2,3},{3,2},{4,5},{5,4},{6,7},{7,6},{8,9},{9,8},{10,11... | collective-permute-start | bytes 393224 | tf_op jit(solution)/shard_map/ppermute | solution.py:126
  0.5 1.4 %copy.4 = bf16[8,2,64,512]{3,2,1,0:T(8,128)(2,1)S(1)} copy(bf16[8,2,64,512]{3,1,2,0:T(2,128)(2,1)} %bitcast.12) | data formatting | bytes 2097152 | tf_op jit(solution)/shard_map/transpose | solution.py:157
  1.9 0.0 copy-start
  1.9 0.1 constant_dynamic-slice_fusion
  2.0 0.0 collective-permute-done.3.refs_1_
  2.0 0.8 %copy-done = bf16[2,512,1,64]{1,3,2,0:T(8,128)(2,1)S(1)} copy-done((bf16[2,512,1,64]{1,3,2,0:T(8,128)(2,1)S(1)}, bf16[2,512,1,64]{1,3,2,0:T(8,128)(2,1)}, u32[]{:S(2)}) %copy-start) | copy-done | bytes 131096
  2.8 0.0 copy-start.1
  2.8 4.7 %collective-permute-start.4 = (bf16[2,2,64,512]{3,2,1,0:T(8,128)(2,1)S(1)}, bf16[2,2,64,512]{3,2,1,0:T(8,128)(2,1)S(1)}, u32[]{:S(2)}, u32[]{:S(2)}) collective-permute-start(bf16[2,2,64,512]{3,2,1,0:T(8,128)(2,1)S(1)} %shard_map.38.refs_8_.refs_0_), channel_id=1, source_target_pairs={{0,24},{1,17},{2,26},{3,19},{4,28},{5,21},{6,30},{7,23},{8,16},{9,... | collective-permute-start | bytes 786440 | tf_op jit(solution)/shard_map/ppermute | solution.py:130
  7.5 1.5 %collective-permute-start.1 = (bf16[1,4,2,64,512]{4,3,2,1,0:T(8,128)(2,1)S(1)}, bf16[1,4,2,64,512]{4,3,2,1,0:T(8,128)(2,1)S(1)}, u32[]{:S(2)}, u32[]{:S(2)}) collective-permute-start(bf16[1,4,2,64,512]{4,3,2,1,0:T(8,128)(2,1)S(1)} %get-tuple-element.22.refs_2_.refs_0_), channel_id=1, source_target_pairs={{0,2},{1,5},{2,0},{3,7},{4,6},{5,1},{6,4},{7,3},{8,10},{9,13},{10,... | collective-permute-start | bytes 1572872 | tf_op jit(solution)/shard_map/ppermute | solution.py:130
  9.0 0.0 collective-permute-start.5
  9.0 0.4 collective-permute-start.2
  9.4 0.3 collective-permute-start
  9.6 0.0 copy-done.1
  9.6 0.7 %shard_map.37.refs_1_.masks = f32[9,512]{1,0:T(8,128)S(1)} custom-call(s32[8,16]{1,0:T(8,128)S(1)} %copy-done.1), custom_call_target="tpu_custom_call" | custom-call | flops 1 | bytes 1 | tf_op jit(solution)/shard_map/pallas_call | solution.py:148
  10.3 6.0 %collective-permute-done.5.refs_2_.refs_6_.refs_1_ = bf16[1,2,64,512]{3,2,1,0:T(8,128)(2,1)S(1)} collective-permute-done((bf16[1,2,64,512]{3,2,1,0:T(8,128)(2,1)S(1)}, bf16[1,2,64,512]{3,2,1,0:T(8,128)(2,1)S(1)}, u32[]{:S(2)}, u32[]{:S(2)}) %collective-permute-start.5) | collective-permute-done | bytes 131104 | tf_op jit(solution)/shard_map/ppermute | solution.py:130
  16.3 0.0 collective-permute-start.7
  16.3 0.0 collective-permute-done.4.refs_0_
  16.3 2.1 %collective-permute-start.6 = (bf16[2,2,64,512]{3,2,1,0:T(8,128)(2,1)S(1)}, bf16[2,2,64,512]{3,2,1,0:T(8,128)(2,1)S(1)}, u32[]{:S(2)}, u32[]{:S(2)}) collective-permute-start(bf16[2,2,64,512]{3,2,1,0:T(8,128)(2,1)S(1)} %shard_map.39.refs_4_), channel_id=1, source_target_pairs={{0,1},{1,0},{2,3},{3,2},{4,5},{5,4},{6,7},{7,6},{8,9},{9,8},{10,11... | collective-permute-start | bytes 786440 | tf_op jit(solution)/shard_map/ppermute | solution.py:126
  18.4 0.0 collective-permute-done.7.refs_7_.refs_2_
  18.4 1.3 %collective-permute-start.10 = (bf16[2,2,64,512]{3,2,1,0:T(8,128)(2,1)S(1)}, bf16[2,2,64,512]{3,2,1,0:T(8,128)(2,1)S(1)}, u32[]{:S(2)}, u32[]{:S(2)}) collective-permute-start(bf16[2,2,64,512]{3,2,1,0:T(8,128)(2,1)S(1)} %shard_map.39.refs_4_), channel_id=1, source_target_pairs={{0,3},{1,4},{2,1},{3,6},{4,7},{5,0},{6,5},{7,2},{8,11},{9,12},{10,... | collective-permute-start | bytes 786440 | tf_op jit(solution)/shard_map/ppermute | solution.py:130
  19.7 1.7 %collective-permute-done.1.refs_2_.refs_3_ = bf16[1,4,2,64,512]{4,3,2,1,0:T(8,128)(2,1)S(1)} collective-permute-done((bf16[1,4,2,64,512]{4,3,2,1,0:T(8,128)(2,1)S(1)}, bf16[1,4,2,64,512]{4,3,2,1,0:T(8,128)(2,1)S(1)}, u32[]{:S(2)}, u32[]{:S(2)}) %collective-permute-start.1) | collective-permute-done | bytes 524320 | tf_op jit(solution)/shard_map/ppermute | solution.py:130
  21.4 1.5 %collective-permute-start.9 = (bf16[2,2,64,512]{3,2,1,0:T(8,128)(2,1)S(1)}, bf16[2,2,64,512]{3,2,1,0:T(8,128)(2,1)S(1)}, u32[]{:S(2)}, u32[]{:S(2)}) collective-permute-start(bf16[2,2,64,512]{3,2,1,0:T(8,128)(2,1)S(1)} %shard_map.39.refs_4_), channel_id=1, source_target_pairs={{0,4},{1,3},{2,6},{3,1},{4,0},{5,7},{6,2},{7,5},{8,12},{9,11},{10,... | collective-permute-start | bytes 786440 | tf_op jit(solution)/shard_map/ppermute | solution.py:130
  22.9 0.0 collective-permute-done.2.refs_3_.refs_4_
  22.9 1.4 %collective-permute-start.15 = (bf16[4,2,64,512]{3,2,1,0:T(8,128)(2,1)S(1)}, bf16[4,2,64,512]{3,2,1,0:T(8,128)(2,1)S(1)}, u32[]{:S(2)}, u32[]{:S(2)}) collective-permute-start(bf16[4,2,64,512]{3,2,1,0:T(8,128)(2,1)S(1)} %shard_map.42), channel_id=1, source_target_pairs={{0,4},{1,3},{2,6},{3,1},{4,0},{5,7},{6,2},{7,5},{8,12},{9,11},{10,... | collective-permute-start | bytes 1572872 | tf_op jit(solution)/shard_map/ppermute | solution.py:130
  24.4 0.0 collective-permute-done.refs_1_
  24.4 0.0 collective-permute-done.6.refs_5_
  24.4 0.7 %shard_map.40 = (bf16[4,64,128]{2,1,0:T(8,128)(2,1)S(1)}, bf16[4,64,128]{2,1,0:T(8,128)(2,1)S(1)}, bf16[4,64,128]{2,1,0:T(8,128)(2,1)S(1)}, bf16[4,64,128]{2,1,0:T(8,128)(2,1)S(1)}) custom-call(f32[9,512]{1,0:T(8,128)S(1)} %shard_map.37.refs_1_.masks, bf16[1,4,2,64,512]{4,3,2,1,0:T(8,128)(2,1)S(1)} %get-tuple-element.22.refs_2_.refs_0_, ...), custom_call_target="tpu_custom_call" | custom-call | flops 1 | bytes 1 | tf_op jit(solution)/shard_map/pallas_call | solution.py:134
  25.1 0.3 collective-permute-start.12
  25.5 1.3 %collective-permute-start.8 = (bf16[4,64,128]{2,1,0:T(8,128)(2,1)S(1)}, bf16[4,64,128]{2,1,0:T(8,128)(2,1)S(1)}, u32[]{:S(2)}, u32[]{:S(2)}) collective-permute-start(bf16[4,64,128]{2,1,0:T(8,128)(2,1)S(1)} %get-tuple-element.13.refs_6_), channel_id=1, source_target_pairs={{0,24},{1,17},{2,26},{3,19},{4,28},{5,21},{6,30},{7,23},{8,16},{9,... | collective-permute-start | bytes 196616 | tf_op jit(solution)/shard_map/ppermute | solution.py:130
  26.7 0.0 collective-permute-done.10.refs_5_
  26.7 1.0 %collective-permute-done.9.refs_4_ = bf16[2,2,64,512]{3,2,1,0:T(8,128)(2,1)S(1)} collective-permute-done((bf16[2,2,64,512]{3,2,1,0:T(8,128)(2,1)S(1)}, bf16[2,2,64,512]{3,2,1,0:T(8,128)(2,1)S(1)}, u32[]{:S(2)}, u32[]{:S(2)}) %collective-permute-start.9) | collective-permute-done | bytes 262176 | tf_op jit(solution)/shard_map/ppermute | solution.py:130
  27.8 0.8 %shard_map.41 = (bf16[4,64,128]{2,1,0:T(8,128)(2,1)S(1)}, bf16[4,64,128]{2,1,0:T(8,128)(2,1)S(1)}) custom-call(f32[9,512]{1,0:T(8,128)S(1)} %shard_map.37.refs_1_.masks, bf16[1,4,2,64,512]{4,3,2,1,0:T(8,128)(2,1)S(1)} %get-tuple-element.22.refs_2_.refs_0_, bf16[1,4,2,64,512]{4,3,2,1,0:T(8,128)(2,1)S(1)} %collective-permute-done.refs_1_, ...), custom_call_target="tpu_custom_call" | custom-call | flops 6000000000 | bytes 1 | tf_op jit(solution)/shard_map/pallas_call | solution.py:134
  28.6 4.0 %collective-permute-start.11 = (bf16[4,64,128]{2,1,0:T(8,128)(2,1)S(1)}, bf16[4,64,128]{2,1,0:T(8,128)(2,1)S(1)}, u32[]{:S(2)}, u32[]{:S(2)}) collective-permute-start(bf16[4,64,128]{2,1,0:T(8,128)(2,1)S(1)} %get-tuple-element.14.refs_5_), channel_id=1, source_target_pairs={{0,28},{1,19},{2,30},{3,17},{4,24},{5,23},{6,26},{7,21},{8,20},{9,... | collective-permute-start | bytes 196616 | tf_op jit(solution)/shard_map/ppermute | solution.py:130
  32.5 0.0 collective-permute-start.13
  32.5 0.0 collective-permute-done.12.refs_7_.refs_2_
  32.5 1.4 %collective-permute-start.14 = (bf16[4,64,128]{2,1,0:T(8,128)(2,1)S(1)}, bf16[4,64,128]{2,1,0:T(8,128)(2,1)S(1)}, u32[]{:S(2)}, u32[]{:S(2)}) collective-permute-start(bf16[4,64,128]{2,1,0:T(8,128)(2,1)S(1)} %get-tuple-element.17), channel_id=1, source_target_pairs={{0,8},{1,9},{2,10},{3,11},{4,12},{5,13},{6,14},{7,15},{8,0},{9,1},... | collective-permute-start | bytes 196616 | tf_op jit(solution)/shard_map/ppermute | solution.py:130
  33.9 0.0 collective-permute-done.8.refs_6_.refs_0_
  33.9 0.0 collective-permute-done.15.refs_4_
  33.9 0.8 %shard_map.43 = (bf16[4,64,128]{2,1,0:T(8,128)(2,1)S(1)}, bf16[4,64,128]{2,1,0:T(8,128)(2,1)S(1)}) custom-call(f32[9,512]{1,0:T(8,128)S(1)} %shard_map.37.refs_1_.masks, bf16[1,4,2,64,512]{4,3,2,1,0:T(8,128)(2,1)S(1)} %get-tuple-element.22.refs_2_.refs_0_, bf16[1,4,2,64,512]{4,3,2,1,0:T(8,128)(2,1)S(1)} %collective-permute-done.refs_1_, ...), custom_call_target="tpu_custom_call" | custom-call | flops 3000000000 | bytes 1 | tf_op jit(solution)/shard_map/pallas_call | solution.py:134
  34.7 1.4 %collective-permute-start.16 = (bf16[4,64,128]{2,1,0:T(8,128)(2,1)S(1)}, bf16[4,64,128]{2,1,0:T(8,128)(2,1)S(1)}, u32[]{:S(2)}, u32[]{:S(2)}) collective-permute-start(bf16[4,64,128]{2,1,0:T(8,128)(2,1)S(1)} %get-tuple-element.18), channel_id=1, source_target_pairs={{0,12},{1,11},{2,14},{3,9},{4,8},{5,15},{6,10},{7,13},{8,4},{9,3},... | collective-permute-start | bytes 196616 | tf_op jit(solution)/shard_map/ppermute | solution.py:130
  36.2 0.7 %collective-permute-start.17 = (bf16[4,64,128]{2,1,0:T(8,128)(2,1)S(1)}, bf16[4,64,128]{2,1,0:T(8,128)(2,1)S(1)}, u32[]{:S(2)}, u32[]{:S(2)}) collective-permute-start(bf16[4,64,128]{2,1,0:T(8,128)(2,1)S(1)} %get-tuple-element.20), channel_id=1, source_target_pairs={{0,4},{1,3},{2,6},{3,1},{4,0},{5,7},{6,2},{7,5},{8,12},{9,11},{10,... | collective-permute-start | bytes 196616 | tf_op jit(solution)/shard_map/ppermute | solution.py:130
  36.9 0.0 collective-permute-done.11.refs_0_.refs_1_
  36.9 2.3 %collective-permute-done.13.refs_1_.refs_3_ = bf16[4,64,128]{2,1,0:T(8,128)(2,1)S(1)} collective-permute-done((bf16[4,64,128]{2,1,0:T(8,128)(2,1)S(1)}, bf16[4,64,128]{2,1,0:T(8,128)(2,1)S(1)}, u32[]{:S(2)}, u32[]{:S(2)}) %collective-permute-start.13) | collective-permute-done | bytes 65568 | tf_op jit(solution)/shard_map/ppermute | solution.py:130
  39.2 0.0 collective-permute-done.14.refs_4_
  39.2 1.2 %collective-permute-done.16.refs_5_ = bf16[4,64,128]{2,1,0:T(8,128)(2,1)S(1)} collective-permute-done((bf16[4,64,128]{2,1,0:T(8,128)(2,1)S(1)}, bf16[4,64,128]{2,1,0:T(8,128)(2,1)S(1)}, u32[]{:S(2)}, u32[]{:S(2)}) %collective-permute-start.16) | collective-permute-done | bytes 65568 | tf_op jit(solution)/shard_map/ppermute | solution.py:130
  40.4 0.4 collective-permute-done.17.refs_7_
  40.8 1.0 %shard_map.45 = bf16[4,64,1024]{2,1,0:T(8,128)(2,1)} custom-call(bf16[4,64,128]{2,1,0:T(8,128)(2,1)S(1)} %collective-permute-done.8.refs_6_.refs_0_, bf16[4,64,128]{2,1,0:T(8,128)(2,1)S(1)} %collective-permute-done.11.refs_0_.refs_1_, bf16[4,64,128]{2,1,0:T(8,128)(2,1)S(1)} %collective-permute-done.12.refs_7_.refs_2_, ...), custom_call_target="tpu_custom_call" | custom-call | flops 1 | bytes 1 | tf_op jit(solution)/shard_map/pallas_call | solution.py:195
  (4 shorter events, 0.1 us)
Async XLA Ops:
  0.0 2.0 %collective-permute-start.3 = (bf16[1,2,64,512]{3,2,1,0:T(8,128)(2,1)}, bf16[1,2,64,512]{3,2,1,0:T(8,128)(2,1)S(1)}, u32[]{:S(2)}, u32[]{:S(2)}) collective-permute-start(bf16[1,2,64,512]{3,2,1,0:T(8,128)(2,1)} %bitcast.8), channel_id=1, source_target_pairs={{0,1},{1,0},{2,3},{3,2},{4,5},{5,4},{6,7},{7,6},{8,9},{9,8},{10,11... | collective-permute-start | bytes 393224 | tf_op jit(solution)/shard_map/ppermute | solution.py:126
  1.9 0.9 %copy-start = (bf16[2,512,1,64]{1,3,2,0:T(8,128)(2,1)S(1)}, bf16[2,512,1,64]{1,3,2,0:T(8,128)(2,1)}, u32[]{:S(2)}) copy-start(bf16[2,512,1,64]{1,3,2,0:T(8,128)(2,1)} %param.4) | copy-start | bytes 393220
  2.8 6.8 %copy-start.1 = (s32[8,16]{1,0:T(8,128)S(1)}, s32[8,16]{1,0:T(8,128)}, u32[]{:S(2)}) copy-start(s32[8,16]{1,0:T(8,128)} %live.1) | copy-start | bytes 1540
  2.8 13.5 %collective-permute-start.4 = (bf16[2,2,64,512]{3,2,1,0:T(8,128)(2,1)S(1)}, bf16[2,2,64,512]{3,2,1,0:T(8,128)(2,1)S(1)}, u32[]{:S(2)}, u32[]{:S(2)}) collective-permute-start(bf16[2,2,64,512]{3,2,1,0:T(8,128)(2,1)S(1)} %shard_map.38.refs_8_.refs_0_), channel_id=1, source_target_pairs={{0,24},{1,17},{2,26},{3,19},{4,28},{5,21},{6,30},{7,23},{8,16},{9,... | collective-permute-start | bytes 786440 | tf_op jit(solution)/shard_map/ppermute | solution.py:130
  7.5 13.9 %collective-permute-start.1 = (bf16[1,4,2,64,512]{4,3,2,1,0:T(8,128)(2,1)S(1)}, bf16[1,4,2,64,512]{4,3,2,1,0:T(8,128)(2,1)S(1)}, u32[]{:S(2)}, u32[]{:S(2)}) collective-permute-start(bf16[1,4,2,64,512]{4,3,2,1,0:T(8,128)(2,1)S(1)} %get-tuple-element.22.refs_2_.refs_0_), channel_id=1, source_target_pairs={{0,2},{1,5},{2,0},{3,7},{4,6},{5,1},{6,4},{7,3},{8,10},{9,13},{10,... | collective-permute-start | bytes 1572872 | tf_op jit(solution)/shard_map/ppermute | solution.py:130
  9.0 7.3 %collective-permute-start.5 = (bf16[1,2,64,512]{3,2,1,0:T(8,128)(2,1)S(1)}, bf16[1,2,64,512]{3,2,1,0:T(8,128)(2,1)S(1)}, u32[]{:S(2)}, u32[]{:S(2)}) collective-permute-start(bf16[1,2,64,512]{3,2,1,0:T(8,128)(2,1)S(1)} %bitcast.10), channel_id=1, source_target_pairs={{0,8},{1,9},{2,10},{3,11},{4,12},{5,13},{6,14},{7,15},{8,0},{9,1},... | collective-permute-start | bytes 393224 | tf_op jit(solution)/shard_map/ppermute | solution.py:130
  9.0 13.9 %collective-permute-start.2 = (bf16[1,4,2,64,512]{4,3,2,1,0:T(8,128)(2,1)S(1)}, bf16[1,4,2,64,512]{4,3,2,1,0:T(8,128)(2,1)S(1)}, u32[]{:S(2)}, u32[]{:S(2)}) collective-permute-start(bf16[1,4,2,64,512]{4,3,2,1,0:T(8,128)(2,1)S(1)} %get-tuple-element.21), channel_id=1, source_target_pairs={{0,5},{1,2},{2,7},{3,0},{4,1},{5,6},{6,3},{7,4},{8,13},{9,10},{10,... | collective-permute-start | bytes 1572872 | tf_op jit(solution)/shard_map/ppermute | solution.py:130
  9.4 15.0 %collective-permute-start = (bf16[1,4,2,64,512]{4,3,2,1,0:T(8,128)(2,1)S(1)}, bf16[1,4,2,64,512]{4,3,2,1,0:T(8,128)(2,1)S(1)}, u32[]{:S(2)}, u32[]{:S(2)}) collective-permute-start(bf16[1,4,2,64,512]{4,3,2,1,0:T(8,128)(2,1)S(1)} %get-tuple-element.21), channel_id=1, source_target_pairs={{0,1},{1,0},{2,3},{3,2},{4,5},{5,4},{6,7},{7,6},{8,9},{9,8},{10,11... | collective-permute-start | bytes 1572872 | tf_op jit(solution)/shard_map/ppermute | solution.py:126
  16.3 2.1 %collective-permute-start.7 = (bf16[1,2,64,512]{3,2,1,0:T(8,128)(2,1)S(1)}, bf16[1,2,64,512]{3,2,1,0:T(8,128)(2,1)S(1)}, u32[]{:S(2)}, u32[]{:S(2)}) collective-permute-start(bf16[1,2,64,512]{3,2,1,0:T(8,128)(2,1)S(1)} %collective-permute-done.5.refs_2_.refs_6_.refs_1_), channel_id=1, source_target_pairs={{0,1},{1,0},{2,3},{3,2},{4,5},{5,4},{6,7},{7,6},{8,9},{9,8},{10,11... | collective-permute-start | bytes 393224 | tf_op jit(solution)/shard_map/ppermute | solution.py:126
  16.3 8.1 %collective-permute-start.6 = (bf16[2,2,64,512]{3,2,1,0:T(8,128)(2,1)S(1)}, bf16[2,2,64,512]{3,2,1,0:T(8,128)(2,1)S(1)}, u32[]{:S(2)}, u32[]{:S(2)}) collective-permute-start(bf16[2,2,64,512]{3,2,1,0:T(8,128)(2,1)S(1)} %shard_map.39.refs_4_), channel_id=1, source_target_pairs={{0,1},{1,0},{2,3},{3,2},{4,5},{5,4},{6,7},{7,6},{8,9},{9,8},{10,11... | collective-permute-start | bytes 786440 | tf_op jit(solution)/shard_map/ppermute | solution.py:126
  18.4 8.3 %collective-permute-start.10 = (bf16[2,2,64,512]{3,2,1,0:T(8,128)(2,1)S(1)}, bf16[2,2,64,512]{3,2,1,0:T(8,128)(2,1)S(1)}, u32[]{:S(2)}, u32[]{:S(2)}) collective-permute-start(bf16[2,2,64,512]{3,2,1,0:T(8,128)(2,1)S(1)} %shard_map.39.refs_4_), channel_id=1, source_target_pairs={{0,3},{1,4},{2,1},{3,6},{4,7},{5,0},{6,5},{7,2},{8,11},{9,12},{10,... | collective-permute-start | bytes 786440 | tf_op jit(solution)/shard_map/ppermute | solution.py:130
  21.4 6.4 %collective-permute-start.9 = (bf16[2,2,64,512]{3,2,1,0:T(8,128)(2,1)S(1)}, bf16[2,2,64,512]{3,2,1,0:T(8,128)(2,1)S(1)}, u32[]{:S(2)}, u32[]{:S(2)}) collective-permute-start(bf16[2,2,64,512]{3,2,1,0:T(8,128)(2,1)S(1)} %shard_map.39.refs_4_), channel_id=1, source_target_pairs={{0,4},{1,3},{2,6},{3,1},{4,0},{5,7},{6,2},{7,5},{8,12},{9,11},{10,... | collective-permute-start | bytes 786440 | tf_op jit(solution)/shard_map/ppermute | solution.py:130
  22.9 11.0 %collective-permute-start.15 = (bf16[4,2,64,512]{3,2,1,0:T(8,128)(2,1)S(1)}, bf16[4,2,64,512]{3,2,1,0:T(8,128)(2,1)S(1)}, u32[]{:S(2)}, u32[]{:S(2)}) collective-permute-start(bf16[4,2,64,512]{3,2,1,0:T(8,128)(2,1)S(1)} %shard_map.42), channel_id=1, source_target_pairs={{0,4},{1,3},{2,6},{3,1},{4,0},{5,7},{6,2},{7,5},{8,12},{9,11},{10,... | collective-permute-start | bytes 1572872 | tf_op jit(solution)/shard_map/ppermute | solution.py:130
  25.1 7.4 %collective-permute-start.12 = (bf16[4,64,128]{2,1,0:T(8,128)(2,1)S(1)}, bf16[4,64,128]{2,1,0:T(8,128)(2,1)S(1)}, u32[]{:S(2)}, u32[]{:S(2)}) collective-permute-start(bf16[4,64,128]{2,1,0:T(8,128)(2,1)S(1)} %get-tuple-element.15), channel_id=1, source_target_pairs={{0,16},{1,25},{2,18},{3,27},{4,20},{5,29},{6,22},{7,31},{8,24},{9,... | collective-permute-start | bytes 196616 | tf_op jit(solution)/shard_map/ppermute | solution.py:130
  25.5 8.5 %collective-permute-start.8 = (bf16[4,64,128]{2,1,0:T(8,128)(2,1)S(1)}, bf16[4,64,128]{2,1,0:T(8,128)(2,1)S(1)}, u32[]{:S(2)}, u32[]{:S(2)}) collective-permute-start(bf16[4,64,128]{2,1,0:T(8,128)(2,1)S(1)} %get-tuple-element.13.refs_6_), channel_id=1, source_target_pairs={{0,24},{1,17},{2,26},{3,19},{4,28},{5,21},{6,30},{7,23},{8,16},{9,... | collective-permute-start | bytes 196616 | tf_op jit(solution)/shard_map/ppermute | solution.py:130
  28.6 8.3 %collective-permute-start.11 = (bf16[4,64,128]{2,1,0:T(8,128)(2,1)S(1)}, bf16[4,64,128]{2,1,0:T(8,128)(2,1)S(1)}, u32[]{:S(2)}, u32[]{:S(2)}) collective-permute-start(bf16[4,64,128]{2,1,0:T(8,128)(2,1)S(1)} %get-tuple-element.14.refs_5_), channel_id=1, source_target_pairs={{0,28},{1,19},{2,30},{3,17},{4,24},{5,23},{6,26},{7,21},{8,20},{9,... | collective-permute-start | bytes 196616 | tf_op jit(solution)/shard_map/ppermute | solution.py:130
  32.5 6.7 %collective-permute-start.13 = (bf16[4,64,128]{2,1,0:T(8,128)(2,1)S(1)}, bf16[4,64,128]{2,1,0:T(8,128)(2,1)S(1)}, u32[]{:S(2)}, u32[]{:S(2)}) collective-permute-start(bf16[4,64,128]{2,1,0:T(8,128)(2,1)S(1)} %get-tuple-element.16), channel_id=1, source_target_pairs={{0,20},{1,27},{2,22},{3,25},{4,16},{5,31},{6,18},{7,29},{8,28},{9,... | collective-permute-start | bytes 196616 | tf_op jit(solution)/shard_map/ppermute | solution.py:130
  32.5 6.7 %collective-permute-start.14 = (bf16[4,64,128]{2,1,0:T(8,128)(2,1)S(1)}, bf16[4,64,128]{2,1,0:T(8,128)(2,1)S(1)}, u32[]{:S(2)}, u32[]{:S(2)}) collective-permute-start(bf16[4,64,128]{2,1,0:T(8,128)(2,1)S(1)} %get-tuple-element.17), channel_id=1, source_target_pairs={{0,8},{1,9},{2,10},{3,11},{4,12},{5,13},{6,14},{7,15},{8,0},{9,1},... | collective-permute-start | bytes 196616 | tf_op jit(solution)/shard_map/ppermute | solution.py:130
  34.7 5.6 %collective-permute-start.16 = (bf16[4,64,128]{2,1,0:T(8,128)(2,1)S(1)}, bf16[4,64,128]{2,1,0:T(8,128)(2,1)S(1)}, u32[]{:S(2)}, u32[]{:S(2)}) collective-permute-start(bf16[4,64,128]{2,1,0:T(8,128)(2,1)S(1)} %get-tuple-element.18), channel_id=1, source_target_pairs={{0,12},{1,11},{2,14},{3,9},{4,8},{5,15},{6,10},{7,13},{8,4},{9,3},... | collective-permute-start | bytes 196616 | tf_op jit(solution)/shard_map/ppermute | solution.py:130
  36.2 4.6 %collective-permute-start.17 = (bf16[4,64,128]{2,1,0:T(8,128)(2,1)S(1)}, bf16[4,64,128]{2,1,0:T(8,128)(2,1)S(1)}, u32[]{:S(2)}, u32[]{:S(2)}) collective-permute-start(bf16[4,64,128]{2,1,0:T(8,128)(2,1)S(1)} %get-tuple-element.20), channel_id=1, source_target_pairs={{0,4},{1,3},{2,6},{3,1},{4,0},{5,7},{6,2},{7,5},{8,12},{9,11},{10,... | collective-permute-start | bytes 196616 | tf_op jit(solution)/shard_map/ppermute | solution.py:130

commit v5 on v4

--- a/solution.py
+++ b/solution.py
@@ -158,7 +158,7 @@
     given = [lax.dynamic_index_in_dim(by_group, ct ^ e, 0) for e in range(n_ct)]
     own_a = [given[0]] + [over_ct(given[e], e) for e in range(1, n_ct)]
 
-    own_parts = pack([own_w] + [over_ct(own_w, e) for e in range(1, n_ct)], [given[0]])
+    own_parts = pack([own_w] + [over_ct(own_w, e) for e in range(1, n_ct)])
     some = [over_tr(own_w, lambda c, z=z: 4 * z) for z in split]
     whole = [over_tr(own_parts, lambda c, group=group: 4 * group[c]) for group in groups]
     their_a = [over_tr(value, pair_bit, e) for e, value in enumerate(given)]
@@ -167,7 +167,7 @@
     whole_side = [over_tr(whole, beside, e) for e in range(n_ct)]
     whole_rest = [over_ct(whole, e) for e in range(1, n_ct)]
     some_rest = [over_ct(some, e) for e in range(1, n_ct)]
-    some_side = over_tr(pack([own_parts, some, *some_rest], their_a), beside)
+    some_side = over_tr(pack([own_parts, some, *some_rest], their_a[:1]), beside)
 
     n_some = some.shape[0]
     of_group = [[(n, g * n_ct + (e ^ n)) for e in range(n_ct)] for g in range(len(groups)) for n in range(n_ct)]

time: 41.9 us -> 41.2 us (0.983)
  starting transfers between devices: 22.7 us -> 23.7 us
  waiting for transfers between devices: 12.6 us -> 11.7 us
  local copies, waits for them, and re-layouts: 2.31 us -> 1.56 us
    ppermute x14, starting transfers between devices: 19.9 us -> 21.2 us  [over_tr(): return lax.ppermute(value, ('tr', 'ct'), pairs)]
    ppermute x14, waiting for transfers between devices: 12.6 us -> 11.7 us  [over_tr(): return lax.ppermute(value, ('tr', 'ct'), pairs)]
    unnamed x4, local copies, waits for them, and re-layouts: 0.79 us -> 0.01 us
where the time goes in v5:
time: 41.2 us; the launch traced here: 41.1 us
  starting transfers between devices  23.7 us (58%)
  waiting for transfers between devices  11.7 us (28%)
  Pallas kernels  4.05 us (10%)
  local copies, waits for them, and re-layouts  1.56 us (4%)
    ppermute x14, starting transfers between devices, over_tr(): return lax.ppermute(value, ('tr', 'ct'), pairs)  21.2 us
    ppermute x14, waiting for transfers between devices, over_tr(): return lax.ppermute(value, ('tr', 'ct'), pairs)  11.7 us
    ppermute x4, starting transfers between devices, over_ct(): return lax.ppermute(value, 'ct', [(c, c ^ e) for c in range(n_ct)])  2.47 us
    pallas_call x7, Pallas kernels, call(): pl.pallas_call(kernel, out_shape=result if count is None else [result] *...  2.42 us
    transpose x1, local copies, waits for them, and re-layouts, per_device(): jnp.transpose(amplitudes, (0, 2, 1, 3))  1.46 us
    pallas_call x1, Pallas kernels, per_device(): pl.pallas_call(functools.partial(place_kernel, shifts), out_shape=jax.Sha...  0.95 us
  transfers between devices with their start and end apart: 18, of which 6 were waited for; matrix products, arithmetic and copies ran while one was open for 4% of the time, Pallas kernels for 7%

profile of v5, /device:TPU:0, one launch (start us, length us, event | category | flops | bytes accessed | tf_op | source)
XLA Modules:
  0.0 41.1 jit_solution(8241949005022740117)
XLA Ops:
  0.0 0.5 %collective-permute-start.3 = (bf16[1,2,64,512]{3,2,1,0:T(8,128)(2,1)}, bf16[1,2,64,512]{3,2,1,0:T(8,128)(2,1)S(1)}, u32[]{:S(2)}, u32[]{:S(2)}) collective-permute-start(bf16[1,2,64,512]{3,2,1,0:T(8,128)(2,1)} %bitcast.8), channel_id=1, source_target_pairs={{0,1},{1,0},{2,3},{3,2},{4,5},{5,4},{6,7},{7,6},{8,9},{9,8},{10,11... | collective-permute-start | bytes 393224 | tf_op jit(solution)/shard_map/ppermute | solution.py:126
  0.5 0.0 copy-start
  0.5 1.5 %copy.4 = bf16[8,2,64,512]{3,2,1,0:T(8,128)(2,1)S(1)} copy(bf16[8,2,64,512]{3,1,2,0:T(2,128)(2,1)} %bitcast.12) | data formatting | bytes 2097152 | tf_op jit(solution)/shard_map/transpose | solution.py:157
  1.9 0.0 collective-permute-done.3.refs_1_
  1.9 0.0 copy-done
  2.0 4.7 %collective-permute-start.4 = (bf16[2,2,64,512]{3,2,1,0:T(8,128)(2,1)S(1)}, bf16[2,2,64,512]{3,2,1,0:T(8,128)(2,1)S(1)}, u32[]{:S(2)}, u32[]{:S(2)}) collective-permute-start(bf16[2,2,64,512]{3,2,1,0:T(8,128)(2,1)S(1)} %shard_map.38.refs_8_.refs_0_), channel_id=1, source_target_pairs={{0,24},{1,17},{2,26},{3,19},{4,28},{5,21},{6,30},{7,23},{8,16},{9,... | collective-permute-start | bytes 786440 | tf_op jit(solution)/shard_map/ppermute | solution.py:130
  6.7 0.0 copy-start.1
  6.7 0.1 constant_dynamic-slice_fusion
  6.8 1.6 %collective-permute-start.1 = (bf16[1,4,2,64,512]{4,3,2,1,0:T(8,128)(2,1)S(1)}, bf16[1,4,2,64,512]{4,3,2,1,0:T(8,128)(2,1)S(1)}, u32[]{:S(2)}, u32[]{:S(2)}) collective-permute-start(bf16[1,4,2,64,512]{4,3,2,1,0:T(8,128)(2,1)S(1)} %get-tuple-element.22.refs_0_), channel_id=1, source_target_pairs={{0,2},{1,5},{2,0},{3,7},{4,6},{5,1},{6,4},{7,3},{8,10},{9,13},{10,... | collective-permute-start | bytes 1572872 | tf_op jit(solution)/shard_map/ppermute | solution.py:130
  8.4 0.0 collective-permute-start.5
  8.4 0.2 collective-permute-start
  8.6 1.4 %collective-permute-start.2 = (bf16[1,4,2,64,512]{4,3,2,1,0:T(8,128)(2,1)S(1)}, bf16[1,4,2,64,512]{4,3,2,1,0:T(8,128)(2,1)S(1)}, u32[]{:S(2)}, u32[]{:S(2)}) collective-permute-start(bf16[1,4,2,64,512]{4,3,2,1,0:T(8,128)(2,1)S(1)} %get-tuple-element.21), channel_id=1, source_target_pairs={{0,5},{1,2},{2,7},{3,0},{4,1},{5,6},{6,3},{7,4},{8,13},{9,10},{10,... | collective-permute-start | bytes 1572872 | tf_op jit(solution)/shard_map/ppermute | solution.py:130
  10.0 0.0 copy-done.1
  10.0 0.7 %shard_map.37.refs_1_.masks = f32[9,512]{1,0:T(8,128)S(1)} custom-call(s32[8,16]{1,0:T(8,128)S(1)} %copy-done.1), custom_call_target="tpu_custom_call" | custom-call | flops 1 | bytes 1 | tf_op jit(solution)/shard_map/pallas_call | solution.py:148
  10.7 5.0 %collective-permute-done.5.refs_2_.refs_6_.refs_1_ = bf16[1,2,64,512]{3,2,1,0:T(8,128)(2,1)S(1)} collective-permute-done((bf16[1,2,64,512]{3,2,1,0:T(8,128)(2,1)S(1)}, bf16[1,2,64,512]{3,2,1,0:T(8,128)(2,1)S(1)}, u32[]{:S(2)}, u32[]{:S(2)}) %collective-permute-start.5) | collective-permute-done | bytes 131104 | tf_op jit(solution)/shard_map/ppermute | solution.py:130
  15.7 0.0 collective-permute-start.7
  15.7 0.0 collective-permute-done.4.refs_0_
  15.7 1.8 %collective-permute-start.6 = (bf16[2,2,64,512]{3,2,1,0:T(8,128)(2,1)S(1)}, bf16[2,2,64,512]{3,2,1,0:T(8,128)(2,1)S(1)}, u32[]{:S(2)}, u32[]{:S(2)}) collective-permute-start(bf16[2,2,64,512]{3,2,1,0:T(8,128)(2,1)S(1)} %shard_map.39.refs_4_), channel_id=1, source_target_pairs={{0,1},{1,0},{2,3},{3,2},{4,5},{5,4},{6,7},{7,6},{8,9},{9,8},{10,11... | collective-permute-start | bytes 786440 | tf_op jit(solution)/shard_map/ppermute | solution.py:126
  17.5 0.0 collective-permute-done.7.refs_7_.refs_2_
  17.5 1.3 %collective-permute-start.10 = (bf16[2,2,64,512]{3,2,1,0:T(8,128)(2,1)S(1)}, bf16[2,2,64,512]{3,2,1,0:T(8,128)(2,1)S(1)}, u32[]{:S(2)}, u32[]{:S(2)}) collective-permute-start(bf16[2,2,64,512]{3,2,1,0:T(8,128)(2,1)S(1)} %shard_map.39.refs_4_), channel_id=1, source_target_pairs={{0,3},{1,4},{2,1},{3,6},{4,7},{5,0},{6,5},{7,2},{8,11},{9,12},{10,... | collective-permute-start | bytes 786440 | tf_op jit(solution)/shard_map/ppermute | solution.py:130
  18.8 1.7 %collective-permute-done.1.refs_2_.refs_3_ = bf16[1,4,2,64,512]{4,3,2,1,0:T(8,128)(2,1)S(1)} collective-permute-done((bf16[1,4,2,64,512]{4,3,2,1,0:T(8,128)(2,1)S(1)}, bf16[1,4,2,64,512]{4,3,2,1,0:T(8,128)(2,1)S(1)}, u32[]{:S(2)}, u32[]{:S(2)}) %collective-permute-start.1) | collective-permute-done | bytes 524320 | tf_op jit(solution)/shard_map/ppermute | solution.py:130
  20.5 1.7 %collective-permute-start.9 = (bf16[2,2,64,512]{3,2,1,0:T(8,128)(2,1)S(1)}, bf16[2,2,64,512]{3,2,1,0:T(8,128)(2,1)S(1)}, u32[]{:S(2)}, u32[]{:S(2)}) collective-permute-start(bf16[2,2,64,512]{3,2,1,0:T(8,128)(2,1)S(1)} %shard_map.39.refs_4_), channel_id=1, source_target_pairs={{0,4},{1,3},{2,6},{3,1},{4,0},{5,7},{6,2},{7,5},{8,12},{9,11},{10,... | collective-permute-start | bytes 786440 | tf_op jit(solution)/shard_map/ppermute | solution.py:130
  22.3 0.0 collective-permute-done.refs_1_
  22.3 0.3 collective-permute-start.15
  22.7 0.0 collective-permute-done.2.refs_3_
  22.7 0.0 collective-permute-done.6.refs_5_
  22.7 0.7 %shard_map.40 = (bf16[4,64,128]{2,1,0:T(8,128)(2,1)S(1)}, bf16[4,64,128]{2,1,0:T(8,128)(2,1)S(1)}, bf16[4,64,128]{2,1,0:T(8,128)(2,1)S(1)}, bf16[4,64,128]{2,1,0:T(8,128)(2,1)S(1)}) custom-call(f32[9,512]{1,0:T(8,128)S(1)} %shard_map.37.refs_1_.masks, bf16[1,4,2,64,512]{4,3,2,1,0:T(8,128)(2,1)S(1)} %get-tuple-element.22.refs_0_, ...), custom_call_target="tpu_custom_call" | custom-call | flops 1 | bytes 1 | tf_op jit(solution)/shard_map/pallas_call | solution.py:134
  23.4 1.3 %collective-permute-start.12 = (bf16[4,64,128]{2,1,0:T(8,128)(2,1)S(1)}, bf16[4,64,128]{2,1,0:T(8,128)(2,1)S(1)}, u32[]{:S(2)}, u32[]{:S(2)}) collective-permute-start(bf16[4,64,128]{2,1,0:T(8,128)(2,1)S(1)} %get-tuple-element.15), channel_id=1, source_target_pairs={{0,16},{1,25},{2,18},{3,27},{4,20},{5,29},{6,22},{7,31},{8,24},{9,... | collective-permute-start | bytes 196616 | tf_op jit(solution)/shard_map/ppermute | solution.py:130
  24.7 1.1 %collective-permute-start.8 = (bf16[4,64,128]{2,1,0:T(8,128)(2,1)S(1)}, bf16[4,64,128]{2,1,0:T(8,128)(2,1)S(1)}, u32[]{:S(2)}, u32[]{:S(2)}) collective-permute-start(bf16[4,64,128]{2,1,0:T(8,128)(2,1)S(1)} %get-tuple-element.13.refs_6_), channel_id=1, source_target_pairs={{0,24},{1,17},{2,26},{3,19},{4,28},{5,21},{6,30},{7,23},{8,16},{9,... | collective-permute-start | bytes 196616 | tf_op jit(solution)/shard_map/ppermute | solution.py:130
  25.9 0.0 collective-permute-done.10.refs_5_
  25.9 1.0 %collective-permute-done.9.refs_4_ = bf16[2,2,64,512]{3,2,1,0:T(8,128)(2,1)S(1)} collective-permute-done((bf16[2,2,64,512]{3,2,1,0:T(8,128)(2,1)S(1)}, bf16[2,2,64,512]{3,2,1,0:T(8,128)(2,1)S(1)}, u32[]{:S(2)}, u32[]{:S(2)}) %collective-permute-start.9) | collective-permute-done | bytes 262176 | tf_op jit(solution)/shard_map/ppermute | solution.py:130
  26.9 0.8 %shard_map.41 = (bf16[4,64,128]{2,1,0:T(8,128)(2,1)S(1)}, bf16[4,64,128]{2,1,0:T(8,128)(2,1)S(1)}) custom-call(f32[9,512]{1,0:T(8,128)S(1)} %shard_map.37.refs_1_.masks, bf16[1,4,2,64,512]{4,3,2,1,0:T(8,128)(2,1)S(1)} %get-tuple-element.22.refs_0_, bf16[1,4,2,64,512]{4,3,2,1,0:T(8,128)(2,1)S(1)} %collective-permute-done.refs_1_, ...), custom_call_target="tpu_custom_call" | custom-call | flops 6000000000 | bytes 1 | tf_op jit(solution)/shard_map/pallas_call | solution.py:134
  27.7 4.0 %collective-permute-start.11 = (bf16[4,64,128]{2,1,0:T(8,128)(2,1)S(1)}, bf16[4,64,128]{2,1,0:T(8,128)(2,1)S(1)}, u32[]{:S(2)}, u32[]{:S(2)}) collective-permute-start(bf16[4,64,128]{2,1,0:T(8,128)(2,1)S(1)} %get-tuple-element.14.refs_5_), channel_id=1, source_target_pairs={{0,28},{1,19},{2,30},{3,17},{4,24},{5,23},{6,26},{7,21},{8,20},{9,... | collective-permute-start | bytes 196616 | tf_op jit(solution)/shard_map/ppermute | solution.py:130
  31.7 0.0 collective-permute-start.13
  31.7 0.0 collective-permute-done.12.refs_7_.refs_2_
  31.7 1.3 %collective-permute-start.14 = (bf16[4,64,128]{2,1,0:T(8,128)(2,1)S(1)}, bf16[4,64,128]{2,1,0:T(8,128)(2,1)S(1)}, u32[]{:S(2)}, u32[]{:S(2)}) collective-permute-start(bf16[4,64,128]{2,1,0:T(8,128)(2,1)S(1)} %get-tuple-element.17), channel_id=1, source_target_pairs={{0,8},{1,9},{2,10},{3,11},{4,12},{5,13},{6,14},{7,15},{8,0},{9,1},... | collective-permute-start | bytes 196616 | tf_op jit(solution)/shard_map/ppermute | solution.py:130
  33.1 0.0 collective-permute-done.8.refs_6_.refs_0_
  33.1 0.0 collective-permute-done.15.refs_4_
  33.1 0.8 %shard_map.43 = (bf16[4,64,128]{2,1,0:T(8,128)(2,1)S(1)}, bf16[4,64,128]{2,1,0:T(8,128)(2,1)S(1)}) custom-call(f32[9,512]{1,0:T(8,128)S(1)} %shard_map.37.refs_1_.masks, bf16[1,4,2,64,512]{4,3,2,1,0:T(8,128)(2,1)S(1)} %get-tuple-element.22.refs_0_, bf16[1,4,2,64,512]{4,3,2,1,0:T(8,128)(2,1)S(1)} %collective-permute-done.refs_1_, ...), custom_call_target="tpu_custom_call" | custom-call | flops 3000000000 | bytes 1 | tf_op jit(solution)/shard_map/pallas_call | solution.py:134
  33.9 1.7 %collective-permute-start.16 = (bf16[4,64,128]{2,1,0:T(8,128)(2,1)S(1)}, bf16[4,64,128]{2,1,0:T(8,128)(2,1)S(1)}, u32[]{:S(2)}, u32[]{:S(2)}) collective-permute-start(bf16[4,64,128]{2,1,0:T(8,128)(2,1)S(1)} %get-tuple-element.18), channel_id=1, source_target_pairs={{0,12},{1,11},{2,14},{3,9},{4,8},{5,15},{6,10},{7,13},{8,4},{9,3},... | collective-permute-start | bytes 196616 | tf_op jit(solution)/shard_map/ppermute | solution.py:130
  35.6 0.7 %collective-permute-start.17 = (bf16[4,64,128]{2,1,0:T(8,128)(2,1)S(1)}, bf16[4,64,128]{2,1,0:T(8,128)(2,1)S(1)}, u32[]{:S(2)}, u32[]{:S(2)}) collective-permute-start(bf16[4,64,128]{2,1,0:T(8,128)(2,1)S(1)} %get-tuple-element.20), channel_id=1, source_target_pairs={{0,4},{1,3},{2,6},{3,1},{4,0},{5,7},{6,2},{7,5},{8,12},{9,11},{10,... | collective-permute-start | bytes 196616 | tf_op jit(solution)/shard_map/ppermute | solution.py:130
  36.2 0.0 collective-permute-done.11.refs_0_.refs_1_
  36.2 2.3 %collective-permute-done.13.refs_1_.refs_3_ = bf16[4,64,128]{2,1,0:T(8,128)(2,1)S(1)} collective-permute-done((bf16[4,64,128]{2,1,0:T(8,128)(2,1)S(1)}, bf16[4,64,128]{2,1,0:T(8,128)(2,1)S(1)}, u32[]{:S(2)}, u32[]{:S(2)}) %collective-permute-start.13) | collective-permute-done | bytes 65568 | tf_op jit(solution)/shard_map/ppermute | solution.py:130
  38.6 0.0 collective-permute-done.14.refs_4_
  38.6 1.2 %collective-permute-done.16.refs_5_ = bf16[4,64,128]{2,1,0:T(8,128)(2,1)S(1)} collective-permute-done((bf16[4,64,128]{2,1,0:T(8,128)(2,1)S(1)}, bf16[4,64,128]{2,1,0:T(8,128)(2,1)S(1)}, u32[]{:S(2)}, u32[]{:S(2)}) %collective-permute-start.16) | collective-permute-done | bytes 65568 | tf_op jit(solution)/shard_map/ppermute | solution.py:130
  39.8 0.4 collective-permute-done.17.refs_7_
  40.1 1.0 %shard_map.45 = bf16[4,64,1024]{2,1,0:T(8,128)(2,1)} custom-call(bf16[4,64,128]{2,1,0:T(8,128)(2,1)S(1)} %collective-permute-done.8.refs_6_.refs_0_, bf16[4,64,128]{2,1,0:T(8,128)(2,1)S(1)} %collective-permute-done.11.refs_0_.refs_1_, bf16[4,64,128]{2,1,0:T(8,128)(2,1)S(1)} %collective-permute-done.12.refs_7_.refs_2_, ...), custom_call_target="tpu_custom_call" | custom-call | flops 1 | bytes 1 | tf_op jit(solution)/shard_map/pallas_call | solution.py:195
  (4 shorter events, 0.1 us)
Async XLA Ops:
  0.0 1.9 %collective-permute-start.3 = (bf16[1,2,64,512]{3,2,1,0:T(8,128)(2,1)}, bf16[1,2,64,512]{3,2,1,0:T(8,128)(2,1)S(1)}, u32[]{:S(2)}, u32[]{:S(2)}) collective-permute-start(bf16[1,2,64,512]{3,2,1,0:T(8,128)(2,1)} %bitcast.8), channel_id=1, source_target_pairs={{0,1},{1,0},{2,3},{3,2},{4,5},{5,4},{6,7},{7,6},{8,9},{9,8},{10,11... | collective-permute-start | bytes 393224 | tf_op jit(solution)/shard_map/ppermute | solution.py:126
  0.5 1.5 %copy-start = (bf16[2,512,1,64]{1,3,2,0:T(8,128)(2,1)S(1)}, bf16[2,512,1,64]{1,3,2,0:T(8,128)(2,1)}, u32[]{:S(2)}) copy-start(bf16[2,512,1,64]{1,3,2,0:T(8,128)(2,1)} %param.4) | copy-start | bytes 393220
  2.0 13.7 %collective-permute-start.4 = (bf16[2,2,64,512]{3,2,1,0:T(8,128)(2,1)S(1)}, bf16[2,2,64,512]{3,2,1,0:T(8,128)(2,1)S(1)}, u32[]{:S(2)}, u32[]{:S(2)}) collective-permute-start(bf16[2,2,64,512]{3,2,1,0:T(8,128)(2,1)S(1)} %shard_map.38.refs_8_.refs_0_), channel_id=1, source_target_pairs={{0,24},{1,17},{2,26},{3,19},{4,28},{5,21},{6,30},{7,23},{8,16},{9,... | collective-permute-start | bytes 786440 | tf_op jit(solution)/shard_map/ppermute | solution.py:130
  6.7 3.3 %copy-start.1 = (s32[8,16]{1,0:T(8,128)S(1)}, s32[8,16]{1,0:T(8,128)}, u32[]{:S(2)}) copy-start(s32[8,16]{1,0:T(8,128)} %live.1) | copy-start | bytes 1540
  6.8 13.7 %collective-permute-start.1 = (bf16[1,4,2,64,512]{4,3,2,1,0:T(8,128)(2,1)S(1)}, bf16[1,4,2,64,512]{4,3,2,1,0:T(8,128)(2,1)S(1)}, u32[]{:S(2)}, u32[]{:S(2)}) collective-permute-start(bf16[1,4,2,64,512]{4,3,2,1,0:T(8,128)(2,1)S(1)} %get-tuple-element.22.refs_0_), channel_id=1, source_target_pairs={{0,2},{1,5},{2,0},{3,7},{4,6},{5,1},{6,4},{7,3},{8,10},{9,13},{10,... | collective-permute-start | bytes 1572872 | tf_op jit(solution)/shard_map/ppermute | solution.py:130
  8.4 7.3 %collective-permute-start.5 = (bf16[1,2,64,512]{3,2,1,0:T(8,128)(2,1)S(1)}, bf16[1,2,64,512]{3,2,1,0:T(8,128)(2,1)S(1)}, u32[]{:S(2)}, u32[]{:S(2)}) collective-permute-start(bf16[1,2,64,512]{3,2,1,0:T(8,128)(2,1)S(1)} %bitcast.10), channel_id=1, source_target_pairs={{0,8},{1,9},{2,10},{3,11},{4,12},{5,13},{6,14},{7,15},{8,0},{9,1},... | collective-permute-start | bytes 393224 | tf_op jit(solution)/shard_map/ppermute | solution.py:130
  8.4 13.9 %collective-permute-start = (bf16[1,4,2,64,512]{4,3,2,1,0:T(8,128)(2,1)S(1)}, bf16[1,4,2,64,512]{4,3,2,1,0:T(8,128)(2,1)S(1)}, u32[]{:S(2)}, u32[]{:S(2)}) collective-permute-start(bf16[1,4,2,64,512]{4,3,2,1,0:T(8,128)(2,1)S(1)} %get-tuple-element.21), channel_id=1, source_target_pairs={{0,1},{1,0},{2,3},{3,2},{4,5},{5,4},{6,7},{7,6},{8,9},{9,8},{10,11... | collective-permute-start | bytes 1572872 | tf_op jit(solution)/shard_map/ppermute | solution.py:126
  8.6 14.1 %collective-permute-start.2 = (bf16[1,4,2,64,512]{4,3,2,1,0:T(8,128)(2,1)S(1)}, bf16[1,4,2,64,512]{4,3,2,1,0:T(8,128)(2,1)S(1)}, u32[]{:S(2)}, u32[]{:S(2)}) collective-permute-start(bf16[1,4,2,64,512]{4,3,2,1,0:T(8,128)(2,1)S(1)} %get-tuple-element.21), channel_id=1, source_target_pairs={{0,5},{1,2},{2,7},{3,0},{4,1},{5,6},{6,3},{7,4},{8,13},{9,10},{10,... | collective-permute-start | bytes 1572872 | tf_op jit(solution)/shard_map/ppermute | solution.py:130
  15.7 1.8 %collective-permute-start.7 = (bf16[1,2,64,512]{3,2,1,0:T(8,128)(2,1)S(1)}, bf16[1,2,64,512]{3,2,1,0:T(8,128)(2,1)S(1)}, u32[]{:S(2)}, u32[]{:S(2)}) collective-permute-start(bf16[1,2,64,512]{3,2,1,0:T(8,128)(2,1)S(1)} %collective-permute-done.5.refs_2_.refs_6_.refs_1_), channel_id=1, source_target_pairs={{0,1},{1,0},{2,3},{3,2},{4,5},{5,4},{6,7},{7,6},{8,9},{9,8},{10,11... | collective-permute-start | bytes 393224 | tf_op jit(solution)/shard_map/ppermute | solution.py:126
  15.7 7.0 %collective-permute-start.6 = (bf16[2,2,64,512]{3,2,1,0:T(8,128)(2,1)S(1)}, bf16[2,2,64,512]{3,2,1,0:T(8,128)(2,1)S(1)}, u32[]{:S(2)}, u32[]{:S(2)}) collective-permute-start(bf16[2,2,64,512]{3,2,1,0:T(8,128)(2,1)S(1)} %shard_map.39.refs_4_), channel_id=1, source_target_pairs={{0,1},{1,0},{2,3},{3,2},{4,5},{5,4},{6,7},{7,6},{8,9},{9,8},{10,11... | collective-permute-start | bytes 786440 | tf_op jit(solution)/shard_map/ppermute | solution.py:126
  17.5 8.4 %collective-permute-start.10 = (bf16[2,2,64,512]{3,2,1,0:T(8,128)(2,1)S(1)}, bf16[2,2,64,512]{3,2,1,0:T(8,128)(2,1)S(1)}, u32[]{:S(2)}, u32[]{:S(2)}) collective-permute-start(bf16[2,2,64,512]{3,2,1,0:T(8,128)(2,1)S(1)} %shard_map.39.refs_4_), channel_id=1, source_target_pairs={{0,3},{1,4},{2,1},{3,6},{4,7},{5,0},{6,5},{7,2},{8,11},{9,12},{10,... | collective-permute-start | bytes 786440 | tf_op jit(solution)/shard_map/ppermute | solution.py:130
  20.5 6.4 %collective-permute-start.9 = (bf16[2,2,64,512]{3,2,1,0:T(8,128)(2,1)S(1)}, bf16[2,2,64,512]{3,2,1,0:T(8,128)(2,1)S(1)}, u32[]{:S(2)}, u32[]{:S(2)}) collective-permute-start(bf16[2,2,64,512]{3,2,1,0:T(8,128)(2,1)S(1)} %shard_map.39.refs_4_), channel_id=1, source_target_pairs={{0,4},{1,3},{2,6},{3,1},{4,0},{5,7},{6,2},{7,5},{8,12},{9,11},{10,... | collective-permute-start | bytes 786440 | tf_op jit(solution)/shard_map/ppermute | solution.py:130
  22.3 10.8 %collective-permute-start.15 = (bf16[4,2,64,512]{3,2,1,0:T(8,128)(2,1)S(1)}, bf16[4,2,64,512]{3,2,1,0:T(8,128)(2,1)S(1)}, u32[]{:S(2)}, u32[]{:S(2)}) collective-permute-start(bf16[4,2,64,512]{3,2,1,0:T(8,128)(2,1)S(1)} %shard_map.42), channel_id=1, source_target_pairs={{0,4},{1,3},{2,6},{3,1},{4,0},{5,7},{6,2},{7,5},{8,12},{9,11},{10,... | collective-permute-start | bytes 1572872 | tf_op jit(solution)/shard_map/ppermute | solution.py:130
  23.4 8.3 %collective-permute-start.12 = (bf16[4,64,128]{2,1,0:T(8,128)(2,1)S(1)}, bf16[4,64,128]{2,1,0:T(8,128)(2,1)S(1)}, u32[]{:S(2)}, u32[]{:S(2)}) collective-permute-start(bf16[4,64,128]{2,1,0:T(8,128)(2,1)S(1)} %get-tuple-element.15), channel_id=1, source_target_pairs={{0,16},{1,25},{2,18},{3,27},{4,20},{5,29},{6,22},{7,31},{8,24},{9,... | collective-permute-start | bytes 196616 | tf_op jit(solution)/shard_map/ppermute | solution.py:130
  24.7 8.3 %collective-permute-start.8 = (bf16[4,64,128]{2,1,0:T(8,128)(2,1)S(1)}, bf16[4,64,128]{2,1,0:T(8,128)(2,1)S(1)}, u32[]{:S(2)}, u32[]{:S(2)}) collective-permute-start(bf16[4,64,128]{2,1,0:T(8,128)(2,1)S(1)} %get-tuple-element.13.refs_6_), channel_id=1, source_target_pairs={{0,24},{1,17},{2,26},{3,19},{4,28},{5,21},{6,30},{7,23},{8,16},{9,... | collective-permute-start | bytes 196616 | tf_op jit(solution)/shard_map/ppermute | solution.py:130
  27.7 8.5 %collective-permute-start.11 = (bf16[4,64,128]{2,1,0:T(8,128)(2,1)S(1)}, bf16[4,64,128]{2,1,0:T(8,128)(2,1)S(1)}, u32[]{:S(2)}, u32[]{:S(2)}) collective-permute-start(bf16[4,64,128]{2,1,0:T(8,128)(2,1)S(1)} %get-tuple-element.14.refs_5_), channel_id=1, source_target_pairs={{0,28},{1,19},{2,30},{3,17},{4,24},{5,23},{6,26},{7,21},{8,20},{9,... | collective-permute-start | bytes 196616 | tf_op jit(solution)/shard_map/ppermute | solution.py:130
  31.7 6.8 %collective-permute-start.13 = (bf16[4,64,128]{2,1,0:T(8,128)(2,1)S(1)}, bf16[4,64,128]{2,1,0:T(8,128)(2,1)S(1)}, u32[]{:S(2)}, u32[]{:S(2)}) collective-permute-start(bf16[4,64,128]{2,1,0:T(8,128)(2,1)S(1)} %get-tuple-element.16), channel_id=1, source_target_pairs={{0,20},{1,27},{2,22},{3,25},{4,16},{5,31},{6,18},{7,29},{8,28},{9,... | collective-permute-start | bytes 196616 | tf_op jit(solution)/shard_map/ppermute | solution.py:130
  31.7 6.8 %collective-permute-start.14 = (bf16[4,64,128]{2,1,0:T(8,128)(2,1)S(1)}, bf16[4,64,128]{2,1,0:T(8,128)(2,1)S(1)}, u32[]{:S(2)}, u32[]{:S(2)}) collective-permute-start(bf16[4,64,128]{2,1,0:T(8,128)(2,1)S(1)} %get-tuple-element.17), channel_id=1, source_target_pairs={{0,8},{1,9},{2,10},{3,11},{4,12},{5,13},{6,14},{7,15},{8,0},{9,1},... | collective-permute-start | bytes 196616 | tf_op jit(solution)/shard_map/ppermute | solution.py:130
  33.9 5.9 %collective-permute-start.16 = (bf16[4,64,128]{2,1,0:T(8,128)(2,1)S(1)}, bf16[4,64,128]{2,1,0:T(8,128)(2,1)S(1)}, u32[]{:S(2)}, u32[]{:S(2)}) collective-permute-start(bf16[4,64,128]{2,1,0:T(8,128)(2,1)S(1)} %get-tuple-element.18), channel_id=1, source_target_pairs={{0,12},{1,11},{2,14},{3,9},{4,8},{5,15},{6,10},{7,13},{8,4},{9,3},... | collective-permute-start | bytes 196616 | tf_op jit(solution)/shard_map/ppermute | solution.py:130
  35.6 4.6 %collective-permute-start.17 = (bf16[4,64,128]{2,1,0:T(8,128)(2,1)S(1)}, bf16[4,64,128]{2,1,0:T(8,128)(2,1)S(1)}, u32[]{:S(2)}, u32[]{:S(2)}) collective-permute-start(bf16[4,64,128]{2,1,0:T(8,128)(2,1)S(1)} %get-tuple-element.20), channel_id=1, source_target_pairs={{0,4},{1,3},{2,6},{3,1},{4,0},{5,7},{6,2},{7,5},{8,12},{9,11},{10,... | collective-permute-start | bytes 196616 | tf_op jit(solution)/shard_map/ppermute | solution.py:130

commit v6 on v5

--- a/solution.py
+++ b/solution.py
@@ -167,7 +167,7 @@
     whole_side = [over_tr(whole, beside, e) for e in range(n_ct)]
     whole_rest = [over_ct(whole, e) for e in range(1, n_ct)]
     some_rest = [over_ct(some, e) for e in range(1, n_ct)]
-    some_side = over_tr(pack([own_parts, some, *some_rest], their_a[:1]), beside)
+    some_side = over_tr(pack([own_parts, some, *some_rest], their_a[1:]), beside)
 
     n_some = some.shape[0]
     of_group = [[(n, g * n_ct + (e ^ n)) for e in range(n_ct)] for g in range(len(groups)) for n in range(n_ct)]
@@ -184,10 +184,10 @@
     near = blocks(column, [whole, *whole_rest, some, *some_rest, own_parts], [], 0)
     made = near[:1]
     near = [over_tr(b, lambda c, by=by: 4 * by[c]) if any(by) else b for b, by in zip(near, shifts)]
-    side = blocks(of_group, whole_side, made, 6)
+    side = blocks(of_group, whole_side, made, 9)
     made = side[:1]
     side = [over_tr(b, lambda c, by=by: 4 * by[c] + beside(c)) for b, by in zip(side, shifts)]
-    late = blocks(side_near, [some_side], [*made, *near[:2]], 3)
+    late = blocks(side_near, [some_side], [*made, *near[:2]], 8)
     done = call(join_kernel, (8, 128), [], side, 10, F32)
     side += [over_tr(b, lambda c, by=by: 4 * by[c] + beside(c)) for b, by in zip(late, shifts[len(shared) :])]
 

time: 41.2 us -> 41.1 us (level)
  waiting for transfers between devices: 11.7 us -> 10.9 us
  starting transfers between devices: 23.7 us -> 24.4 us
    ppermute x14, starting transfers between devices: 21.2 us -> 22.6 us  [over_tr(): return lax.ppermute(value, ('tr', 'ct'), pairs)]
    ppermute x14, waiting for transfers between devices: 11.7 us -> 10.7 us  [over_tr(): return lax.ppermute(value, ('tr', 'ct'), pairs)]
    ppermute x4, starting transfers between devices: 2.47 us -> 1.78 us  [over_ct(): return lax.ppermute(value, 'ct', [(c, c ^ e) for c in range(n_ct)])]
  transfers between devices with their start and end apart: 18 -> 18, of which waited for: 6 -> 7; matrix products, arithmetic and copies ran while one was open for 4% -> 4% of each run, Pallas kernels for 7% -> 8%
where the time goes in v6:
time: 41.1 us; the launch traced here: 41 us
  starting transfers between devices  24.4 us (59%)
  waiting for transfers between devices  10.9 us (27%)
  Pallas kernels  4.05 us (10%)
  local copies, waits for them, and re-layouts  1.56 us (4%)
    ppermute x14, starting transfers between devices, over_tr(): return lax.ppermute(value, ('tr', 'ct'), pairs)  22.6 us
    ppermute x14, waiting for transfers between devices, over_tr(): return lax.ppermute(value, ('tr', 'ct'), pairs)  10.7 us
    pallas_call x7, Pallas kernels, call(): pl.pallas_call(kernel, out_shape=result if count is None else [result] *...  2.42 us
    ppermute x4, starting transfers between devices, over_ct(): return lax.ppermute(value, 'ct', [(c, c ^ e) for c in range(n_ct)])  1.78 us
    transpose x1, local copies, waits for them, and re-layouts, per_device(): jnp.transpose(amplitudes, (0, 2, 1, 3))  1.46 us
    pallas_call x1, Pallas kernels, per_device(): pl.pallas_call(functools.partial(place_kernel, shifts), out_shape=jax.Sha...  0.95 us
  transfers between devices with their start and end apart: 18, of which 7 were waited for; matrix products, arithmetic and copies ran while one was open for 4% of the time, Pallas kernels for 8%

profile of v6, /device:TPU:0, one launch (start us, length us, event | category | flops | bytes accessed | tf_op | source)
XLA Modules:
  0.0 41.0 jit_solution(15710577058176362013)
XLA Ops:
  0.0 0.5 %collective-permute-start.3 = (bf16[1,2,64,512]{3,2,1,0:T(8,128)(2,1)}, bf16[1,2,64,512]{3,2,1,0:T(8,128)(2,1)S(1)}, u32[]{:S(2)}, u32[]{:S(2)}) collective-permute-start(bf16[1,2,64,512]{3,2,1,0:T(8,128)(2,1)} %bitcast.8), channel_id=1, source_target_pairs={{0,1},{1,0},{2,3},{3,2},{4,5},{5,4},{6,7},{7,6},{8,9},{9,8},{10,11... | collective-permute-start | bytes 393224 | tf_op jit(solution)/shard_map/ppermute | solution.py:126
  0.5 0.0 copy-start
  0.5 1.5 %copy.4 = bf16[8,2,64,512]{3,2,1,0:T(8,128)(2,1)S(1)} copy(bf16[8,2,64,512]{3,1,2,0:T(2,128)(2,1)} %bitcast.12) | data formatting | bytes 2097152 | tf_op jit(solution)/shard_map/transpose | solution.py:157
  1.9 0.0 collective-permute-done.3.refs_1_
  1.9 0.0 copy-done
  2.0 4.7 %collective-permute-start.4 = (bf16[2,2,64,512]{3,2,1,0:T(8,128)(2,1)S(1)}, bf16[2,2,64,512]{3,2,1,0:T(8,128)(2,1)S(1)}, u32[]{:S(2)}, u32[]{:S(2)}) collective-permute-start(bf16[2,2,64,512]{3,2,1,0:T(8,128)(2,1)S(1)} %shard_map.38.refs_8_.refs_0_), channel_id=1, source_target_pairs={{0,24},{1,17},{2,26},{3,19},{4,28},{5,21},{6,30},{7,23},{8,16},{9,... | collective-permute-start | bytes 786440 | tf_op jit(solution)/shard_map/ppermute | solution.py:130
  6.7 0.0 copy-start.1
  6.7 0.1 constant_dynamic-slice_fusion
  6.8 0.3 collective-permute-start.2
  7.1 1.6 %collective-permute-start.5 = (bf16[1,2,64,512]{3,2,1,0:T(8,128)(2,1)S(1)}, bf16[1,2,64,512]{3,2,1,0:T(8,128)(2,1)S(1)}, u32[]{:S(2)}, u32[]{:S(2)}) collective-permute-start(bf16[1,2,64,512]{3,2,1,0:T(8,128)(2,1)S(1)} %bitcast.10), channel_id=1, source_target_pairs={{0,8},{1,9},{2,10},{3,11},{4,12},{5,13},{6,14},{7,15},{8,0},{9,1},... | collective-permute-start | bytes 393224 | tf_op jit(solution)/shard_map/ppermute | solution.py:130
  8.7 0.0 collective-permute-start
  8.7 1.5 %collective-permute-start.1 = (bf16[1,4,2,64,512]{4,3,2,1,0:T(8,128)(2,1)S(1)}, bf16[1,4,2,64,512]{4,3,2,1,0:T(8,128)(2,1)S(1)}, u32[]{:S(2)}, u32[]{:S(2)}) collective-permute-start(bf16[1,4,2,64,512]{4,3,2,1,0:T(8,128)(2,1)S(1)} %get-tuple-element.22.refs_0_), channel_id=1, source_target_pairs={{0,2},{1,5},{2,0},{3,7},{4,6},{5,1},{6,4},{7,3},{8,10},{9,13},{10,... | collective-permute-start | bytes 1572872 | tf_op jit(solution)/shard_map/ppermute | solution.py:130
  10.2 0.0 copy-done.1
  10.2 0.7 %shard_map.37.refs_1_.masks = f32[9,512]{1,0:T(8,128)S(1)} custom-call(s32[8,16]{1,0:T(8,128)S(1)} %copy-done.1), custom_call_target="tpu_custom_call" | custom-call | flops 1 | bytes 1 | tf_op jit(solution)/shard_map/pallas_call | solution.py:148
  10.9 5.3 %collective-permute-done.5.refs_2_.refs_6_.refs_1_ = bf16[1,2,64,512]{3,2,1,0:T(8,128)(2,1)S(1)} collective-permute-done((bf16[1,2,64,512]{3,2,1,0:T(8,128)(2,1)S(1)}, bf16[1,2,64,512]{3,2,1,0:T(8,128)(2,1)S(1)}, u32[]{:S(2)}, u32[]{:S(2)}) %collective-permute-start.5) | collective-permute-done | bytes 131104 | tf_op jit(solution)/shard_map/ppermute | solution.py:130
  16.1 0.5 %collective-permute-start.7 = (bf16[1,2,64,512]{3,2,1,0:T(8,128)(2,1)S(1)}, bf16[1,2,64,512]{3,2,1,0:T(8,128)(2,1)S(1)}, u32[]{:S(2)}, u32[]{:S(2)}) collective-permute-start(bf16[1,2,64,512]{3,2,1,0:T(8,128)(2,1)S(1)} %collective-permute-done.5.refs_2_.refs_6_.refs_1_), channel_id=1, source_target_pairs={{0,1},{1,0},{2,3},{3,2},{4,5},{5,4},{6,7},{7,6},{8,9},{9,8},{10,11... | collective-permute-start | bytes 393224 | tf_op jit(solution)/shard_map/ppermute | solution.py:126
  16.6 0.0 collective-permute-done.4.refs_0_
  16.6 0.9 %collective-permute-start.6 = (bf16[2,2,64,512]{3,2,1,0:T(8,128)(2,1)S(1)}, bf16[2,2,64,512]{3,2,1,0:T(8,128)(2,1)S(1)}, u32[]{:S(2)}, u32[]{:S(2)}) collective-permute-start(bf16[2,2,64,512]{3,2,1,0:T(8,128)(2,1)S(1)} %shard_map.39.refs_4_), channel_id=1, source_target_pairs={{0,1},{1,0},{2,3},{3,2},{4,5},{5,4},{6,7},{7,6},{8,9},{9,8},{10,11... | collective-permute-start | bytes 786440 | tf_op jit(solution)/shard_map/ppermute | solution.py:126
  17.5 0.1 collective-permute-done.7.refs_7_.refs_2_
  17.6 1.2 %collective-permute-start.10 = (bf16[2,2,64,512]{3,2,1,0:T(8,128)(2,1)S(1)}, bf16[2,2,64,512]{3,2,1,0:T(8,128)(2,1)S(1)}, u32[]{:S(2)}, u32[]{:S(2)}) collective-permute-start(bf16[2,2,64,512]{3,2,1,0:T(8,128)(2,1)S(1)} %shard_map.39.refs_4_), channel_id=1, source_target_pairs={{0,3},{1,4},{2,1},{3,6},{4,7},{5,0},{6,5},{7,2},{8,11},{9,12},{10,... | collective-permute-start | bytes 786440 | tf_op jit(solution)/shard_map/ppermute | solution.py:130
  18.8 0.0 collective-permute-done.2.refs_3_
  18.8 1.6 %collective-permute-start.9 = (bf16[2,2,64,512]{3,2,1,0:T(8,128)(2,1)S(1)}, bf16[2,2,64,512]{3,2,1,0:T(8,128)(2,1)S(1)}, u32[]{:S(2)}, u32[]{:S(2)}) collective-permute-start(bf16[2,2,64,512]{3,2,1,0:T(8,128)(2,1)S(1)} %shard_map.39.refs_4_), channel_id=1, source_target_pairs={{0,4},{1,3},{2,6},{3,1},{4,0},{5,7},{6,2},{7,5},{8,12},{9,11},{10,... | collective-permute-start | bytes 786440 | tf_op jit(solution)/shard_map/ppermute | solution.py:130
  20.4 0.7 %collective-permute-done.1.refs_2_ = bf16[1,4,2,64,512]{4,3,2,1,0:T(8,128)(2,1)S(1)} collective-permute-done((bf16[1,4,2,64,512]{4,3,2,1,0:T(8,128)(2,1)S(1)}, bf16[1,4,2,64,512]{4,3,2,1,0:T(8,128)(2,1)S(1)}, u32[]{:S(2)}, u32[]{:S(2)}) %collective-permute-start.1) | collective-permute-done | bytes 524320 | tf_op jit(solution)/shard_map/ppermute | solution.py:130
  21.1 1.5 %collective-permute-start.15 = (bf16[4,2,64,512]{3,2,1,0:T(8,128)(2,1)S(1)}, bf16[4,2,64,512]{3,2,1,0:T(8,128)(2,1)S(1)}, u32[]{:S(2)}, u32[]{:S(2)}) collective-permute-start(bf16[4,2,64,512]{3,2,1,0:T(8,128)(2,1)S(1)} %shard_map.42), channel_id=1, source_target_pairs={{0,4},{1,3},{2,6},{3,1},{4,0},{5,7},{6,2},{7,5},{8,12},{9,11},{10,... | collective-permute-start | bytes 1572872 | tf_op jit(solution)/shard_map/ppermute | solution.py:130
  22.6 0.0 collective-permute-done.refs_1_
  22.6 0.0 collective-permute-done.6.refs_5_
  22.6 0.7 %shard_map.40 = (bf16[4,64,128]{2,1,0:T(8,128)(2,1)S(1)}, bf16[4,64,128]{2,1,0:T(8,128)(2,1)S(1)}, bf16[4,64,128]{2,1,0:T(8,128)(2,1)S(1)}, bf16[4,64,128]{2,1,0:T(8,128)(2,1)S(1)}) custom-call(f32[9,512]{1,0:T(8,128)S(1)} %shard_map.37.refs_1_.masks, bf16[1,4,2,64,512]{4,3,2,1,0:T(8,128)(2,1)S(1)} %get-tuple-element.22.refs_0_, ...), custom_call_target="tpu_custom_call" | custom-call | flops 1 | bytes 1 | tf_op jit(solution)/shard_map/pallas_call | solution.py:134
  23.3 1.4 %collective-permute-start.12 = (bf16[4,64,128]{2,1,0:T(8,128)(2,1)S(1)}, bf16[4,64,128]{2,1,0:T(8,128)(2,1)S(1)}, u32[]{:S(2)}, u32[]{:S(2)}) collective-permute-start(bf16[4,64,128]{2,1,0:T(8,128)(2,1)S(1)} %get-tuple-element.15), channel_id=1, source_target_pairs={{0,16},{1,25},{2,18},{3,27},{4,20},{5,29},{6,22},{7,31},{8,24},{9,... | collective-permute-start | bytes 196616 | tf_op jit(solution)/shard_map/ppermute | solution.py:130
  24.7 1.1 %collective-permute-start.8 = (bf16[4,64,128]{2,1,0:T(8,128)(2,1)S(1)}, bf16[4,64,128]{2,1,0:T(8,128)(2,1)S(1)}, u32[]{:S(2)}, u32[]{:S(2)}) collective-permute-start(bf16[4,64,128]{2,1,0:T(8,128)(2,1)S(1)} %get-tuple-element.13.refs_6_), channel_id=1, source_target_pairs={{0,24},{1,17},{2,26},{3,19},{4,28},{5,21},{6,30},{7,23},{8,16},{9,... | collective-permute-start | bytes 196616 | tf_op jit(solution)/shard_map/ppermute | solution.py:130
  25.9 0.0 collective-permute-done.10.refs_5_
  25.9 0.9 %collective-permute-done.9.refs_4_ = bf16[2,2,64,512]{3,2,1,0:T(8,128)(2,1)S(1)} collective-permute-done((bf16[2,2,64,512]{3,2,1,0:T(8,128)(2,1)S(1)}, bf16[2,2,64,512]{3,2,1,0:T(8,128)(2,1)S(1)}, u32[]{:S(2)}, u32[]{:S(2)}) %collective-permute-start.9) | collective-permute-done | bytes 262176 | tf_op jit(solution)/shard_map/ppermute | solution.py:130
  26.8 0.8 %shard_map.41 = (bf16[4,64,128]{2,1,0:T(8,128)(2,1)S(1)}, bf16[4,64,128]{2,1,0:T(8,128)(2,1)S(1)}) custom-call(f32[9,512]{1,0:T(8,128)S(1)} %shard_map.37.refs_1_.masks, bf16[1,4,2,64,512]{4,3,2,1,0:T(8,128)(2,1)S(1)} %get-tuple-element.22.refs_0_, bf16[1,4,2,64,512]{4,3,2,1,0:T(8,128)(2,1)S(1)} %collective-permute-done.refs_1_, ...), custom_call_target="tpu_custom_call" | custom-call | flops 9000000512 | bytes 1 | tf_op jit(solution)/shard_map/pallas_call | solution.py:134
  27.6 4.2 %collective-permute-start.11 = (bf16[4,64,128]{2,1,0:T(8,128)(2,1)S(1)}, bf16[4,64,128]{2,1,0:T(8,128)(2,1)S(1)}, u32[]{:S(2)}, u32[]{:S(2)}) collective-permute-start(bf16[4,64,128]{2,1,0:T(8,128)(2,1)S(1)} %get-tuple-element.14.refs_5_), channel_id=1, source_target_pairs={{0,28},{1,19},{2,30},{3,17},{4,24},{5,23},{6,26},{7,21},{8,20},{9,... | collective-permute-start | bytes 196616 | tf_op jit(solution)/shard_map/ppermute | solution.py:130
  31.7 0.0 collective-permute-start.13
  31.7 0.0 collective-permute-done.12.refs_7_.refs_2_
  31.7 1.2 %collective-permute-start.14 = (bf16[4,64,128]{2,1,0:T(8,128)(2,1)S(1)}, bf16[4,64,128]{2,1,0:T(8,128)(2,1)S(1)}, u32[]{:S(2)}, u32[]{:S(2)}) collective-permute-start(bf16[4,64,128]{2,1,0:T(8,128)(2,1)S(1)} %get-tuple-element.17), channel_id=1, source_target_pairs={{0,8},{1,9},{2,10},{3,11},{4,12},{5,13},{6,14},{7,15},{8,0},{9,1},... | collective-permute-start | bytes 196616 | tf_op jit(solution)/shard_map/ppermute | solution.py:130
  32.9 0.0 collective-permute-done.8.refs_6_.refs_0_
  32.9 0.0 collective-permute-done.15.refs_4_
  32.9 0.8 %shard_map.43 = (bf16[4,64,128]{2,1,0:T(8,128)(2,1)S(1)}, bf16[4,64,128]{2,1,0:T(8,128)(2,1)S(1)}) custom-call(f32[9,512]{1,0:T(8,128)S(1)} %shard_map.37.refs_1_.masks, bf16[1,4,2,64,512]{4,3,2,1,0:T(8,128)(2,1)S(1)} %get-tuple-element.22.refs_0_, bf16[1,4,2,64,512]{4,3,2,1,0:T(8,128)(2,1)S(1)} %collective-permute-done.refs_1_, ...), custom_call_target="tpu_custom_call" | custom-call | flops 8000000000 | bytes 1 | tf_op jit(solution)/shard_map/pallas_call | solution.py:134
  33.8 1.5 %collective-permute-start.16 = (bf16[4,64,128]{2,1,0:T(8,128)(2,1)S(1)}, bf16[4,64,128]{2,1,0:T(8,128)(2,1)S(1)}, u32[]{:S(2)}, u32[]{:S(2)}) collective-permute-start(bf16[4,64,128]{2,1,0:T(8,128)(2,1)S(1)} %get-tuple-element.18), channel_id=1, source_target_pairs={{0,12},{1,11},{2,14},{3,9},{4,8},{5,15},{6,10},{7,13},{8,4},{9,3},... | collective-permute-start | bytes 196616 | tf_op jit(solution)/shard_map/ppermute | solution.py:130
  35.3 0.8 %collective-permute-start.17 = (bf16[4,64,128]{2,1,0:T(8,128)(2,1)S(1)}, bf16[4,64,128]{2,1,0:T(8,128)(2,1)S(1)}, u32[]{:S(2)}, u32[]{:S(2)}) collective-permute-start(bf16[4,64,128]{2,1,0:T(8,128)(2,1)S(1)} %get-tuple-element.20), channel_id=1, source_target_pairs={{0,4},{1,3},{2,6},{3,1},{4,0},{5,7},{6,2},{7,5},{8,12},{9,11},{10,... | collective-permute-start | bytes 196616 | tf_op jit(solution)/shard_map/ppermute | solution.py:130
  36.1 0.0 collective-permute-done.11.refs_0_.refs_1_
  36.1 2.2 %collective-permute-done.13.refs_1_.refs_3_ = bf16[4,64,128]{2,1,0:T(8,128)(2,1)S(1)} collective-permute-done((bf16[4,64,128]{2,1,0:T(8,128)(2,1)S(1)}, bf16[4,64,128]{2,1,0:T(8,128)(2,1)S(1)}, u32[]{:S(2)}, u32[]{:S(2)}) %collective-permute-start.13) | collective-permute-done | bytes 65568 | tf_op jit(solution)/shard_map/ppermute | solution.py:130
  38.4 0.0 collective-permute-done.14.refs_4_
  38.4 1.5 %collective-permute-done.16.refs_5_ = bf16[4,64,128]{2,1,0:T(8,128)(2,1)S(1)} collective-permute-done((bf16[4,64,128]{2,1,0:T(8,128)(2,1)S(1)}, bf16[4,64,128]{2,1,0:T(8,128)(2,1)S(1)}, u32[]{:S(2)}, u32[]{:S(2)}) %collective-permute-start.16) | collective-permute-done | bytes 65568 | tf_op jit(solution)/shard_map/ppermute | solution.py:130
  39.8 0.2 collective-permute-done.17.refs_7_
  40.0 1.0 %shard_map.45 = bf16[4,64,1024]{2,1,0:T(8,128)(2,1)} custom-call(bf16[4,64,128]{2,1,0:T(8,128)(2,1)S(1)} %collective-permute-done.8.refs_6_.refs_0_, bf16[4,64,128]{2,1,0:T(8,128)(2,1)S(1)} %collective-permute-done.11.refs_0_.refs_1_, bf16[4,64,128]{2,1,0:T(8,128)(2,1)S(1)} %collective-permute-done.12.refs_7_.refs_2_, ...), custom_call_target="tpu_custom_call" | custom-call | flops 1 | bytes 1 | tf_op jit(solution)/shard_map/pallas_call | solution.py:195
  (4 shorter events, 0.1 us)
Async XLA Ops:
  0.0 1.9 %collective-permute-start.3 = (bf16[1,2,64,512]{3,2,1,0:T(8,128)(2,1)}, bf16[1,2,64,512]{3,2,1,0:T(8,128)(2,1)S(1)}, u32[]{:S(2)}, u32[]{:S(2)}) collective-permute-start(bf16[1,2,64,512]{3,2,1,0:T(8,128)(2,1)} %bitcast.8), channel_id=1, source_target_pairs={{0,1},{1,0},{2,3},{3,2},{4,5},{5,4},{6,7},{7,6},{8,9},{9,8},{10,11... | collective-permute-start | bytes 393224 | tf_op jit(solution)/shard_map/ppermute | solution.py:126
  0.5 1.5 %copy-start = (bf16[2,512,1,64]{1,3,2,0:T(8,128)(2,1)S(1)}, bf16[2,512,1,64]{1,3,2,0:T(8,128)(2,1)}, u32[]{:S(2)}) copy-start(bf16[2,512,1,64]{1,3,2,0:T(8,128)(2,1)} %param.4) | copy-start | bytes 393220
  2.0 14.6 %collective-permute-start.4 = (bf16[2,2,64,512]{3,2,1,0:T(8,128)(2,1)S(1)}, bf16[2,2,64,512]{3,2,1,0:T(8,128)(2,1)S(1)}, u32[]{:S(2)}, u32[]{:S(2)}) collective-permute-start(bf16[2,2,64,512]{3,2,1,0:T(8,128)(2,1)S(1)} %shard_map.38.refs_8_.refs_0_), channel_id=1, source_target_pairs={{0,24},{1,17},{2,26},{3,19},{4,28},{5,21},{6,30},{7,23},{8,16},{9,... | collective-permute-start | bytes 786440 | tf_op jit(solution)/shard_map/ppermute | solution.py:130
  6.7 3.5 %copy-start.1 = (s32[8,16]{1,0:T(8,128)S(1)}, s32[8,16]{1,0:T(8,128)}, u32[]{:S(2)}) copy-start(s32[8,16]{1,0:T(8,128)} %live.1) | copy-start | bytes 1540
  6.8 12.0 %collective-permute-start.2 = (bf16[1,4,2,64,512]{4,3,2,1,0:T(8,128)(2,1)S(1)}, bf16[1,4,2,64,512]{4,3,2,1,0:T(8,128)(2,1)S(1)}, u32[]{:S(2)}, u32[]{:S(2)}) collective-permute-start(bf16[1,4,2,64,512]{4,3,2,1,0:T(8,128)(2,1)S(1)} %get-tuple-element.21), channel_id=1, source_target_pairs={{0,5},{1,2},{2,7},{3,0},{4,1},{5,6},{6,3},{7,4},{8,13},{9,10},{10,... | collective-permute-start | bytes 1572872 | tf_op jit(solution)/shard_map/ppermute | solution.py:130
  7.1 9.0 %collective-permute-start.5 = (bf16[1,2,64,512]{3,2,1,0:T(8,128)(2,1)S(1)}, bf16[1,2,64,512]{3,2,1,0:T(8,128)(2,1)S(1)}, u32[]{:S(2)}, u32[]{:S(2)}) collective-permute-start(bf16[1,2,64,512]{3,2,1,0:T(8,128)(2,1)S(1)} %bitcast.10), channel_id=1, source_target_pairs={{0,8},{1,9},{2,10},{3,11},{4,12},{5,13},{6,14},{7,15},{8,0},{9,1},... | collective-permute-start | bytes 393224 | tf_op jit(solution)/shard_map/ppermute | solution.py:130
  8.7 13.9 %collective-permute-start = (bf16[1,4,2,64,512]{4,3,2,1,0:T(8,128)(2,1)S(1)}, bf16[1,4,2,64,512]{4,3,2,1,0:T(8,128)(2,1)S(1)}, u32[]{:S(2)}, u32[]{:S(2)}) collective-permute-start(bf16[1,4,2,64,512]{4,3,2,1,0:T(8,128)(2,1)S(1)} %get-tuple-element.21), channel_id=1, source_target_pairs={{0,1},{1,0},{2,3},{3,2},{4,5},{5,4},{6,7},{7,6},{8,9},{9,8},{10,11... | collective-permute-start | bytes 1572872 | tf_op jit(solution)/shard_map/ppermute | solution.py:126
  8.7 12.4 %collective-permute-start.1 = (bf16[1,4,2,64,512]{4,3,2,1,0:T(8,128)(2,1)S(1)}, bf16[1,4,2,64,512]{4,3,2,1,0:T(8,128)(2,1)S(1)}, u32[]{:S(2)}, u32[]{:S(2)}) collective-permute-start(bf16[1,4,2,64,512]{4,3,2,1,0:T(8,128)(2,1)S(1)} %get-tuple-element.22.refs_0_), channel_id=1, source_target_pairs={{0,2},{1,5},{2,0},{3,7},{4,6},{5,1},{6,4},{7,3},{8,10},{9,13},{10,... | collective-permute-start | bytes 1572872 | tf_op jit(solution)/shard_map/ppermute | solution.py:130
  16.1 1.5 %collective-permute-start.7 = (bf16[1,2,64,512]{3,2,1,0:T(8,128)(2,1)S(1)}, bf16[1,2,64,512]{3,2,1,0:T(8,128)(2,1)S(1)}, u32[]{:S(2)}, u32[]{:S(2)}) collective-permute-start(bf16[1,2,64,512]{3,2,1,0:T(8,128)(2,1)S(1)} %collective-permute-done.5.refs_2_.refs_6_.refs_1_), channel_id=1, source_target_pairs={{0,1},{1,0},{2,3},{3,2},{4,5},{5,4},{6,7},{7,6},{8,9},{9,8},{10,11... | collective-permute-start | bytes 393224 | tf_op jit(solution)/shard_map/ppermute | solution.py:126
  16.6 6.0 %collective-permute-start.6 = (bf16[2,2,64,512]{3,2,1,0:T(8,128)(2,1)S(1)}, bf16[2,2,64,512]{3,2,1,0:T(8,128)(2,1)S(1)}, u32[]{:S(2)}, u32[]{:S(2)}) collective-permute-start(bf16[2,2,64,512]{3,2,1,0:T(8,128)(2,1)S(1)} %shard_map.39.refs_4_), channel_id=1, source_target_pairs={{0,1},{1,0},{2,3},{3,2},{4,5},{5,4},{6,7},{7,6},{8,9},{9,8},{10,11... | collective-permute-start | bytes 786440 | tf_op jit(solution)/shard_map/ppermute | solution.py:126
  17.6 8.3 %collective-permute-start.10 = (bf16[2,2,64,512]{3,2,1,0:T(8,128)(2,1)S(1)}, bf16[2,2,64,512]{3,2,1,0:T(8,128)(2,1)S(1)}, u32[]{:S(2)}, u32[]{:S(2)}) collective-permute-start(bf16[2,2,64,512]{3,2,1,0:T(8,128)(2,1)S(1)} %shard_map.39.refs_4_), channel_id=1, source_target_pairs={{0,3},{1,4},{2,1},{3,6},{4,7},{5,0},{6,5},{7,2},{8,11},{9,12},{10,... | collective-permute-start | bytes 786440 | tf_op jit(solution)/shard_map/ppermute | solution.py:130
  18.8 8.0 %collective-permute-start.9 = (bf16[2,2,64,512]{3,2,1,0:T(8,128)(2,1)S(1)}, bf16[2,2,64,512]{3,2,1,0:T(8,128)(2,1)S(1)}, u32[]{:S(2)}, u32[]{:S(2)}) collective-permute-start(bf16[2,2,64,512]{3,2,1,0:T(8,128)(2,1)S(1)} %shard_map.39.refs_4_), channel_id=1, source_target_pairs={{0,4},{1,3},{2,6},{3,1},{4,0},{5,7},{6,2},{7,5},{8,12},{9,11},{10,... | collective-permute-start | bytes 786440 | tf_op jit(solution)/shard_map/ppermute | solution.py:130
  21.1 11.9 %collective-permute-start.15 = (bf16[4,2,64,512]{3,2,1,0:T(8,128)(2,1)S(1)}, bf16[4,2,64,512]{3,2,1,0:T(8,128)(2,1)S(1)}, u32[]{:S(2)}, u32[]{:S(2)}) collective-permute-start(bf16[4,2,64,512]{3,2,1,0:T(8,128)(2,1)S(1)} %shard_map.42), channel_id=1, source_target_pairs={{0,4},{1,3},{2,6},{3,1},{4,0},{5,7},{6,2},{7,5},{8,12},{9,11},{10,... | collective-permute-start | bytes 1572872 | tf_op jit(solution)/shard_map/ppermute | solution.py:130
  23.3 8.4 %collective-permute-start.12 = (bf16[4,64,128]{2,1,0:T(8,128)(2,1)S(1)}, bf16[4,64,128]{2,1,0:T(8,128)(2,1)S(1)}, u32[]{:S(2)}, u32[]{:S(2)}) collective-permute-start(bf16[4,64,128]{2,1,0:T(8,128)(2,1)S(1)} %get-tuple-element.15), channel_id=1, source_target_pairs={{0,16},{1,25},{2,18},{3,27},{4,20},{5,29},{6,22},{7,31},{8,24},{9,... | collective-permute-start | bytes 196616 | tf_op jit(solution)/shard_map/ppermute | solution.py:130
  24.7 8.2 %collective-permute-start.8 = (bf16[4,64,128]{2,1,0:T(8,128)(2,1)S(1)}, bf16[4,64,128]{2,1,0:T(8,128)(2,1)S(1)}, u32[]{:S(2)}, u32[]{:S(2)}) collective-permute-start(bf16[4,64,128]{2,1,0:T(8,128)(2,1)S(1)} %get-tuple-element.13.refs_6_), channel_id=1, source_target_pairs={{0,24},{1,17},{2,26},{3,19},{4,28},{5,21},{6,30},{7,23},{8,16},{9,... | collective-permute-start | bytes 196616 | tf_op jit(solution)/shard_map/ppermute | solution.py:130
  27.6 8.5 %collective-permute-start.11 = (bf16[4,64,128]{2,1,0:T(8,128)(2,1)S(1)}, bf16[4,64,128]{2,1,0:T(8,128)(2,1)S(1)}, u32[]{:S(2)}, u32[]{:S(2)}) collective-permute-start(bf16[4,64,128]{2,1,0:T(8,128)(2,1)S(1)} %get-tuple-element.14.refs_5_), channel_id=1, source_target_pairs={{0,28},{1,19},{2,30},{3,17},{4,24},{5,23},{6,26},{7,21},{8,20},{9,... | collective-permute-start | bytes 196616 | tf_op jit(solution)/shard_map/ppermute | solution.py:130
  31.7 6.6 %collective-permute-start.13 = (bf16[4,64,128]{2,1,0:T(8,128)(2,1)S(1)}, bf16[4,64,128]{2,1,0:T(8,128)(2,1)S(1)}, u32[]{:S(2)}, u32[]{:S(2)}) collective-permute-start(bf16[4,64,128]{2,1,0:T(8,128)(2,1)S(1)} %get-tuple-element.16), channel_id=1, source_target_pairs={{0,20},{1,27},{2,22},{3,25},{4,16},{5,31},{6,18},{7,29},{8,28},{9,... | collective-permute-start | bytes 196616 | tf_op jit(solution)/shard_map/ppermute | solution.py:130
  31.7 6.6 %collective-permute-start.14 = (bf16[4,64,128]{2,1,0:T(8,128)(2,1)S(1)}, bf16[4,64,128]{2,1,0:T(8,128)(2,1)S(1)}, u32[]{:S(2)}, u32[]{:S(2)}) collective-permute-start(bf16[4,64,128]{2,1,0:T(8,128)(2,1)S(1)} %get-tuple-element.17), channel_id=1, source_target_pairs={{0,8},{1,9},{2,10},{3,11},{4,12},{5,13},{6,14},{7,15},{8,0},{9,1},... | collective-permute-start | bytes 196616 | tf_op jit(solution)/shard_map/ppermute | solution.py:130
  33.8 6.1 %collective-permute-start.16 = (bf16[4,64,128]{2,1,0:T(8,128)(2,1)S(1)}, bf16[4,64,128]{2,1,0:T(8,128)(2,1)S(1)}, u32[]{:S(2)}, u32[]{:S(2)}) collective-permute-start(bf16[4,64,128]{2,1,0:T(8,128)(2,1)S(1)} %get-tuple-element.18), channel_id=1, source_target_pairs={{0,12},{1,11},{2,14},{3,9},{4,8},{5,15},{6,10},{7,13},{8,4},{9,3},... | collective-permute-start | bytes 196616 | tf_op jit(solution)/shard_map/ppermute | solution.py:130
  35.3 4.7 %collective-permute-start.17 = (bf16[4,64,128]{2,1,0:T(8,128)(2,1)S(1)}, bf16[4,64,128]{2,1,0:T(8,128)(2,1)S(1)}, u32[]{:S(2)}, u32[]{:S(2)}) collective-permute-start(bf16[4,64,128]{2,1,0:T(8,128)(2,1)S(1)} %get-tuple-element.20), channel_id=1, source_target_pairs={{0,4},{1,3},{2,6},{3,1},{4,0},{5,7},{6,2},{7,5},{8,12},{9,11},{10,... | collective-permute-start | bytes 196616 | tf_op jit(solution)/shard_map/ppermute | solution.py:130

commit v7 on v6

--- a/solution.py
+++ b/solution.py
@@ -91,20 +91,38 @@
     half = lax.broadcasted_iota(jnp.int32, (1, wide), 1) < wide // 2
     straight = pair_bit(ct) == 1
     own_first = (tr & (3 - pair_bit(ct))) == 0
-    copies = []
-    for n, by_core in enumerate(shifts):
+    places = []
+    for by_core in shifts:
         shift = sum(jnp.where(ct == c, z, 0) for c, z in enumerate(by_core))
-        at = pl.multiple_of(((tr // 4) ^ shift) * 2 * wide, 2 * wide)
-        for i in range(out.shape[0]):
-            a, b = parts[2 * n][i], parts[2 * n + 1][i]
-            lo, hi = jnp.where(own_first, a, b), jnp.where(own_first, b, a)
-            across = pltpu.roll(jnp.where(half, hi, lo).astype(F32), wide // 2, 1).astype(lo.dtype)
-            stage[n, i, :, pl.ds(0, wide)] = jnp.where(straight, lo, jnp.where(half, lo, hi))
-            stage[n, i, :, pl.ds(wide, wide)] = jnp.where(straight, hi, across)
-        copies.append(pltpu.make_async_copy(stage.at[n], out.at[:, :, pl.ds(at, 2 * wide)], sems.at[n]))
-        copies[-1].start()
-    for copy in copies:
-        copy.wait()
+        places.append(pl.multiple_of(((tr // 4) ^ shift) * 2 * wide, 2 * wide))
+
+    @pl.when(straight)
+    def _():
+        copies = []
+        for n, at in enumerate(places):
+            for m in range(2):
+                lane = pl.multiple_of(at + jnp.where(own_first, m, 1 - m) * wide, wide)
+                copies.append(
+                    pltpu.make_async_copy(parts[2 * n + m], out.at[:, :, pl.ds(lane, wide)], sems.at[2 * n + m])
+                )
+                copies[-1].start()
+        for copy in copies:
+            copy.wait()
+
+    @pl.when(jnp.logical_not(straight))
+    def _():
+        copies = []
+        for n, at in enumerate(places):
+            for i in range(out.shape[0]):
+                a, b = parts[2 * n][i], parts[2 * n + 1][i]
+                lo, hi = jnp.where(own_first, a, b), jnp.where(own_first, b, a)
+                across = pltpu.roll(jnp.where(half, hi, lo).astype(F32), wide // 2, 1).astype(lo.dtype)
+                stage[n, i, :, pl.ds(0, wide)] = jnp.where(half, lo, hi)
+                stage[n, i, :, pl.ds(wide, wide)] = across
+            copies.append(pltpu.make_async_copy(stage.at[n], out.at[:, :, pl.ds(at, 2 * wide)], sems.at[2 * n]))
+            copies[-1].start()
+        for copy in copies:
+            copy.wait()
 
 
 def per_device(n_tr, n_ct, amplitudes, cycle_integrals, pair_live):
@@ -199,7 +217,7 @@
         out_specs=ANY,
         scratch_shapes=[
             pltpu.VMEM((n_z, n_local, vt, 4 * vt), jnp.bfloat16),
-            pltpu.SemaphoreType.DMA((n_z,)),
+            pltpu.SemaphoreType.DMA((2 * n_z,)),
         ],
         compiler_params=PARAMS,
         cost_estimate=cost(),

time: 41.1 us -> 41 us (level)
  no operation moved by 1% of the time
where the time goes in v7:
time: 41 us; the launch traced here: 40.9 us
  starting transfers between devices  24.4 us (60%)
  waiting for transfers between devices  10.9 us (27%)
  Pallas kernels  3.95 us (10%)
  local copies, waits for them, and re-layouts  1.56 us (4%)
    ppermute x14, starting transfers between devices, over_tr(): return lax.ppermute(value, ('tr', 'ct'), pairs)  22.6 us
    ppermute x14, waiting for transfers between devices, over_tr(): return lax.ppermute(value, ('tr', 'ct'), pairs)  10.7 us
    pallas_call x7, Pallas kernels, call(): pl.pallas_call(kernel, out_shape=result if count is None else [result] *...  2.42 us
    ppermute x4, starting transfers between devices, over_ct(): return lax.ppermute(value, 'ct', [(c, c ^ e) for c in range(n_ct)])  1.78 us
    transpose x1, local copies, waits for them, and re-layouts, per_device(): jnp.transpose(amplitudes, (0, 2, 1, 3))  1.46 us
    pallas_call x1, Pallas kernels, per_device(): pl.pallas_call(functools.partial(place_kernel, shifts), out_shape=jax.Sha...  0.85 us
  transfers between devices with their start and end apart: 18, of which 7 were waited for; matrix products, arithmetic and copies ran while one was open for 4% of the time, Pallas kernels for 8%

profile of v7, /device:TPU:0, one launch (start us, length us, event | category | flops | bytes accessed | tf_op | source)
XLA Modules:
  0.0 40.9 jit_solution(1174296633551929706)
XLA Ops:
  0.0 0.5 %collective-permute-start.3 = (bf16[1,2,64,512]{3,2,1,0:T(8,128)(2,1)}, bf16[1,2,64,512]{3,2,1,0:T(8,128)(2,1)S(1)}, u32[]{:S(2)}, u32[]{:S(2)}) collective-permute-start(bf16[1,2,64,512]{3,2,1,0:T(8,128)(2,1)} %bitcast.8), channel_id=1, source_target_pairs={{0,1},{1,0},{2,3},{3,2},{4,5},{5,4},{6,7},{7,6},{8,9},{9,8},{10,11... | collective-permute-start | bytes 393224 | tf_op jit(solution)/shard_map/ppermute | solution.py:144
  0.5 0.0 copy-start
  0.5 1.5 %copy.4 = bf16[8,2,64,512]{3,2,1,0:T(8,128)(2,1)S(1)} copy(bf16[8,2,64,512]{3,1,2,0:T(2,128)(2,1)} %bitcast.12) | data formatting | bytes 2097152 | tf_op jit(solution)/shard_map/transpose | solution.py:175
  1.9 0.0 collective-permute-done.3.refs_1_
  1.9 0.0 copy-done
  2.0 4.7 %collective-permute-start.4 = (bf16[2,2,64,512]{3,2,1,0:T(8,128)(2,1)S(1)}, bf16[2,2,64,512]{3,2,1,0:T(8,128)(2,1)S(1)}, u32[]{:S(2)}, u32[]{:S(2)}) collective-permute-start(bf16[2,2,64,512]{3,2,1,0:T(8,128)(2,1)S(1)} %shard_map.38.refs_8_.refs_0_), channel_id=1, source_target_pairs={{0,24},{1,17},{2,26},{3,19},{4,28},{5,21},{6,30},{7,23},{8,16},{9,... | collective-permute-start | bytes 786440 | tf_op jit(solution)/shard_map/ppermute | solution.py:148
  6.7 0.0 copy-start.1
  6.7 0.1 constant_dynamic-slice_fusion
  6.8 0.3 collective-permute-start.2
  7.1 1.6 %collective-permute-start.5 = (bf16[1,2,64,512]{3,2,1,0:T(8,128)(2,1)S(1)}, bf16[1,2,64,512]{3,2,1,0:T(8,128)(2,1)S(1)}, u32[]{:S(2)}, u32[]{:S(2)}) collective-permute-start(bf16[1,2,64,512]{3,2,1,0:T(8,128)(2,1)S(1)} %bitcast.10), channel_id=1, source_target_pairs={{0,8},{1,9},{2,10},{3,11},{4,12},{5,13},{6,14},{7,15},{8,0},{9,1},... | collective-permute-start | bytes 393224 | tf_op jit(solution)/shard_map/ppermute | solution.py:148
  8.7 0.0 collective-permute-start
  8.7 1.5 %collective-permute-start.1 = (bf16[1,4,2,64,512]{4,3,2,1,0:T(8,128)(2,1)S(1)}, bf16[1,4,2,64,512]{4,3,2,1,0:T(8,128)(2,1)S(1)}, u32[]{:S(2)}, u32[]{:S(2)}) collective-permute-start(bf16[1,4,2,64,512]{4,3,2,1,0:T(8,128)(2,1)S(1)} %get-tuple-element.22.refs_0_), channel_id=1, source_target_pairs={{0,2},{1,5},{2,0},{3,7},{4,6},{5,1},{6,4},{7,3},{8,10},{9,13},{10,... | collective-permute-start | bytes 1572872 | tf_op jit(solution)/shard_map/ppermute | solution.py:148
  10.2 0.0 copy-done.1
  10.2 0.7 %shard_map.37.refs_1_.masks = f32[9,512]{1,0:T(8,128)S(1)} custom-call(s32[8,16]{1,0:T(8,128)S(1)} %copy-done.1), custom_call_target="tpu_custom_call" | custom-call | flops 1 | bytes 1 | tf_op jit(solution)/shard_map/pallas_call | solution.py:166
  10.9 5.3 %collective-permute-done.5.refs_2_.refs_6_.refs_1_ = bf16[1,2,64,512]{3,2,1,0:T(8,128)(2,1)S(1)} collective-permute-done((bf16[1,2,64,512]{3,2,1,0:T(8,128)(2,1)S(1)}, bf16[1,2,64,512]{3,2,1,0:T(8,128)(2,1)S(1)}, u32[]{:S(2)}, u32[]{:S(2)}) %collective-permute-start.5) | collective-permute-done | bytes 131104 | tf_op jit(solution)/shard_map/ppermute | solution.py:148
  16.1 0.5 %collective-permute-start.7 = (bf16[1,2,64,512]{3,2,1,0:T(8,128)(2,1)S(1)}, bf16[1,2,64,512]{3,2,1,0:T(8,128)(2,1)S(1)}, u32[]{:S(2)}, u32[]{:S(2)}) collective-permute-start(bf16[1,2,64,512]{3,2,1,0:T(8,128)(2,1)S(1)} %collective-permute-done.5.refs_2_.refs_6_.refs_1_), channel_id=1, source_target_pairs={{0,1},{1,0},{2,3},{3,2},{4,5},{5,4},{6,7},{7,6},{8,9},{9,8},{10,11... | collective-permute-start | bytes 393224 | tf_op jit(solution)/shard_map/ppermute | solution.py:144
  16.6 0.0 collective-permute-done.4.refs_0_
  16.6 0.9 %collective-permute-start.6 = (bf16[2,2,64,512]{3,2,1,0:T(8,128)(2,1)S(1)}, bf16[2,2,64,512]{3,2,1,0:T(8,128)(2,1)S(1)}, u32[]{:S(2)}, u32[]{:S(2)}) collective-permute-start(bf16[2,2,64,512]{3,2,1,0:T(8,128)(2,1)S(1)} %shard_map.39.refs_4_), channel_id=1, source_target_pairs={{0,1},{1,0},{2,3},{3,2},{4,5},{5,4},{6,7},{7,6},{8,9},{9,8},{10,11... | collective-permute-start | bytes 786440 | tf_op jit(solution)/shard_map/ppermute | solution.py:144
  17.5 0.1 collective-permute-done.7.refs_7_.refs_2_
  17.6 1.2 %collective-permute-start.10 = (bf16[2,2,64,512]{3,2,1,0:T(8,128)(2,1)S(1)}, bf16[2,2,64,512]{3,2,1,0:T(8,128)(2,1)S(1)}, u32[]{:S(2)}, u32[]{:S(2)}) collective-permute-start(bf16[2,2,64,512]{3,2,1,0:T(8,128)(2,1)S(1)} %shard_map.39.refs_4_), channel_id=1, source_target_pairs={{0,3},{1,4},{2,1},{3,6},{4,7},{5,0},{6,5},{7,2},{8,11},{9,12},{10,... | collective-permute-start | bytes 786440 | tf_op jit(solution)/shard_map/ppermute | solution.py:148
  18.8 0.0 collective-permute-done.2.refs_3_
  18.8 1.6 %collective-permute-start.9 = (bf16[2,2,64,512]{3,2,1,0:T(8,128)(2,1)S(1)}, bf16[2,2,64,512]{3,2,1,0:T(8,128)(2,1)S(1)}, u32[]{:S(2)}, u32[]{:S(2)}) collective-permute-start(bf16[2,2,64,512]{3,2,1,0:T(8,128)(2,1)S(1)} %shard_map.39.refs_4_), channel_id=1, source_target_pairs={{0,4},{1,3},{2,6},{3,1},{4,0},{5,7},{6,2},{7,5},{8,12},{9,11},{10,... | collective-permute-start | bytes 786440 | tf_op jit(solution)/shard_map/ppermute | solution.py:148
  20.4 0.7 %collective-permute-done.1.refs_2_ = bf16[1,4,2,64,512]{4,3,2,1,0:T(8,128)(2,1)S(1)} collective-permute-done((bf16[1,4,2,64,512]{4,3,2,1,0:T(8,128)(2,1)S(1)}, bf16[1,4,2,64,512]{4,3,2,1,0:T(8,128)(2,1)S(1)}, u32[]{:S(2)}, u32[]{:S(2)}) %collective-permute-start.1) | collective-permute-done | bytes 524320 | tf_op jit(solution)/shard_map/ppermute | solution.py:148
  21.1 1.5 %collective-permute-start.15 = (bf16[4,2,64,512]{3,2,1,0:T(8,128)(2,1)S(1)}, bf16[4,2,64,512]{3,2,1,0:T(8,128)(2,1)S(1)}, u32[]{:S(2)}, u32[]{:S(2)}) collective-permute-start(bf16[4,2,64,512]{3,2,1,0:T(8,128)(2,1)S(1)} %shard_map.42), channel_id=1, source_target_pairs={{0,4},{1,3},{2,6},{3,1},{4,0},{5,7},{6,2},{7,5},{8,12},{9,11},{10,... | collective-permute-start | bytes 1572872 | tf_op jit(solution)/shard_map/ppermute | solution.py:148
  22.6 0.0 collective-permute-done.refs_1_
  22.6 0.0 collective-permute-done.6.refs_5_
  22.6 0.7 %shard_map.40 = (bf16[4,64,128]{2,1,0:T(8,128)(2,1)S(1)}, bf16[4,64,128]{2,1,0:T(8,128)(2,1)S(1)}, bf16[4,64,128]{2,1,0:T(8,128)(2,1)S(1)}, bf16[4,64,128]{2,1,0:T(8,128)(2,1)S(1)}) custom-call(f32[9,512]{1,0:T(8,128)S(1)} %shard_map.37.refs_1_.masks, bf16[1,4,2,64,512]{4,3,2,1,0:T(8,128)(2,1)S(1)} %get-tuple-element.22.refs_0_, ...), custom_call_target="tpu_custom_call" | custom-call | flops 1 | bytes 1 | tf_op jit(solution)/shard_map/pallas_call | solution.py:152
  23.3 1.4 %collective-permute-start.12 = (bf16[4,64,128]{2,1,0:T(8,128)(2,1)S(1)}, bf16[4,64,128]{2,1,0:T(8,128)(2,1)S(1)}, u32[]{:S(2)}, u32[]{:S(2)}) collective-permute-start(bf16[4,64,128]{2,1,0:T(8,128)(2,1)S(1)} %get-tuple-element.15), channel_id=1, source_target_pairs={{0,16},{1,25},{2,18},{3,27},{4,20},{5,29},{6,22},{7,31},{8,24},{9,... | collective-permute-start | bytes 196616 | tf_op jit(solution)/shard_map/ppermute | solution.py:148
  24.7 1.1 %collective-permute-start.8 = (bf16[4,64,128]{2,1,0:T(8,128)(2,1)S(1)}, bf16[4,64,128]{2,1,0:T(8,128)(2,1)S(1)}, u32[]{:S(2)}, u32[]{:S(2)}) collective-permute-start(bf16[4,64,128]{2,1,0:T(8,128)(2,1)S(1)} %get-tuple-element.13.refs_6_), channel_id=1, source_target_pairs={{0,24},{1,17},{2,26},{3,19},{4,28},{5,21},{6,30},{7,23},{8,16},{9,... | collective-permute-start | bytes 196616 | tf_op jit(solution)/shard_map/ppermute | solution.py:148
  25.9 0.0 collective-permute-done.10.refs_5_
  25.9 0.9 %collective-permute-done.9.refs_4_ = bf16[2,2,64,512]{3,2,1,0:T(8,128)(2,1)S(1)} collective-permute-done((bf16[2,2,64,512]{3,2,1,0:T(8,128)(2,1)S(1)}, bf16[2,2,64,512]{3,2,1,0:T(8,128)(2,1)S(1)}, u32[]{:S(2)}, u32[]{:S(2)}) %collective-permute-start.9) | collective-permute-done | bytes 262176 | tf_op jit(solution)/shard_map/ppermute | solution.py:148
  26.8 0.8 %shard_map.41 = (bf16[4,64,128]{2,1,0:T(8,128)(2,1)S(1)}, bf16[4,64,128]{2,1,0:T(8,128)(2,1)S(1)}) custom-call(f32[9,512]{1,0:T(8,128)S(1)} %shard_map.37.refs_1_.masks, bf16[1,4,2,64,512]{4,3,2,1,0:T(8,128)(2,1)S(1)} %get-tuple-element.22.refs_0_, bf16[1,4,2,64,512]{4,3,2,1,0:T(8,128)(2,1)S(1)} %collective-permute-done.refs_1_, ...), custom_call_target="tpu_custom_call" | custom-call | flops 9000000512 | bytes 1 | tf_op jit(solution)/shard_map/pallas_call | solution.py:152
  27.6 4.2 %collective-permute-start.11 = (bf16[4,64,128]{2,1,0:T(8,128)(2,1)S(1)}, bf16[4,64,128]{2,1,0:T(8,128)(2,1)S(1)}, u32[]{:S(2)}, u32[]{:S(2)}) collective-permute-start(bf16[4,64,128]{2,1,0:T(8,128)(2,1)S(1)} %get-tuple-element.14.refs_5_), channel_id=1, source_target_pairs={{0,28},{1,19},{2,30},{3,17},{4,24},{5,23},{6,26},{7,21},{8,20},{9,... | collective-permute-start | bytes 196616 | tf_op jit(solution)/shard_map/ppermute | solution.py:148
  31.7 0.0 collective-permute-start.13
  31.7 0.0 collective-permute-done.12.refs_7_.refs_2_
  31.7 1.2 %collective-permute-start.14 = (bf16[4,64,128]{2,1,0:T(8,128)(2,1)S(1)}, bf16[4,64,128]{2,1,0:T(8,128)(2,1)S(1)}, u32[]{:S(2)}, u32[]{:S(2)}) collective-permute-start(bf16[4,64,128]{2,1,0:T(8,128)(2,1)S(1)} %get-tuple-element.17), channel_id=1, source_target_pairs={{0,8},{1,9},{2,10},{3,11},{4,12},{5,13},{6,14},{7,15},{8,0},{9,1},... | collective-permute-start | bytes 196616 | tf_op jit(solution)/shard_map/ppermute | solution.py:148
  32.9 0.0 collective-permute-done.8.refs_6_.refs_0_
  32.9 0.0 collective-permute-done.15.refs_4_
  32.9 0.8 %shard_map.43 = (bf16[4,64,128]{2,1,0:T(8,128)(2,1)S(1)}, bf16[4,64,128]{2,1,0:T(8,128)(2,1)S(1)}) custom-call(f32[9,512]{1,0:T(8,128)S(1)} %shard_map.37.refs_1_.masks, bf16[1,4,2,64,512]{4,3,2,1,0:T(8,128)(2,1)S(1)} %get-tuple-element.22.refs_0_, bf16[1,4,2,64,512]{4,3,2,1,0:T(8,128)(2,1)S(1)} %collective-permute-done.refs_1_, ...), custom_call_target="tpu_custom_call" | custom-call | flops 8000000000 | bytes 1 | tf_op jit(solution)/shard_map/pallas_call | solution.py:152
  33.8 1.5 %collective-permute-start.16 = (bf16[4,64,128]{2,1,0:T(8,128)(2,1)S(1)}, bf16[4,64,128]{2,1,0:T(8,128)(2,1)S(1)}, u32[]{:S(2)}, u32[]{:S(2)}) collective-permute-start(bf16[4,64,128]{2,1,0:T(8,128)(2,1)S(1)} %get-tuple-element.18), channel_id=1, source_target_pairs={{0,12},{1,11},{2,14},{3,9},{4,8},{5,15},{6,10},{7,13},{8,4},{9,3},... | collective-permute-start | bytes 196616 | tf_op jit(solution)/shard_map/ppermute | solution.py:148
  35.3 0.8 %collective-permute-start.17 = (bf16[4,64,128]{2,1,0:T(8,128)(2,1)S(1)}, bf16[4,64,128]{2,1,0:T(8,128)(2,1)S(1)}, u32[]{:S(2)}, u32[]{:S(2)}) collective-permute-start(bf16[4,64,128]{2,1,0:T(8,128)(2,1)S(1)} %get-tuple-element.20), channel_id=1, source_target_pairs={{0,4},{1,3},{2,6},{3,1},{4,0},{5,7},{6,2},{7,5},{8,12},{9,11},{10,... | collective-permute-start | bytes 196616 | tf_op jit(solution)/shard_map/ppermute | solution.py:148
  36.1 0.0 collective-permute-done.11.refs_0_.refs_1_
  36.1 2.2 %collective-permute-done.13.refs_1_.refs_3_ = bf16[4,64,128]{2,1,0:T(8,128)(2,1)S(1)} collective-permute-done((bf16[4,64,128]{2,1,0:T(8,128)(2,1)S(1)}, bf16[4,64,128]{2,1,0:T(8,128)(2,1)S(1)}, u32[]{:S(2)}, u32[]{:S(2)}) %collective-permute-start.13) | collective-permute-done | bytes 65568 | tf_op jit(solution)/shard_map/ppermute | solution.py:148
  38.4 0.0 collective-permute-done.14.refs_4_
  38.4 1.5 %collective-permute-done.16.refs_5_ = bf16[4,64,128]{2,1,0:T(8,128)(2,1)S(1)} collective-permute-done((bf16[4,64,128]{2,1,0:T(8,128)(2,1)S(1)}, bf16[4,64,128]{2,1,0:T(8,128)(2,1)S(1)}, u32[]{:S(2)}, u32[]{:S(2)}) %collective-permute-start.16) | collective-permute-done | bytes 65568 | tf_op jit(solution)/shard_map/ppermute | solution.py:148
  39.8 0.2 collective-permute-done.17.refs_7_
  40.0 0.8 %shard_map.45 = bf16[4,64,1024]{2,1,0:T(8,128)(2,1)} custom-call(bf16[4,64,128]{2,1,0:T(8,128)(2,1)S(1)} %collective-permute-done.8.refs_6_.refs_0_, bf16[4,64,128]{2,1,0:T(8,128)(2,1)S(1)} %collective-permute-done.11.refs_0_.refs_1_, bf16[4,64,128]{2,1,0:T(8,128)(2,1)S(1)} %collective-permute-done.12.refs_7_.refs_2_, ...), custom_call_target="tpu_custom_call" | custom-call | flops 1 | bytes 1 | tf_op jit(solution)/shard_map/pallas_call | solution.py:213
  (4 shorter events, 0.1 us)
Async XLA Ops:
  0.0 1.9 %collective-permute-start.3 = (bf16[1,2,64,512]{3,2,1,0:T(8,128)(2,1)}, bf16[1,2,64,512]{3,2,1,0:T(8,128)(2,1)S(1)}, u32[]{:S(2)}, u32[]{:S(2)}) collective-permute-start(bf16[1,2,64,512]{3,2,1,0:T(8,128)(2,1)} %bitcast.8), channel_id=1, source_target_pairs={{0,1},{1,0},{2,3},{3,2},{4,5},{5,4},{6,7},{7,6},{8,9},{9,8},{10,11... | collective-permute-start | bytes 393224 | tf_op jit(solution)/shard_map/ppermute | solution.py:144
  0.5 1.5 %copy-start = (bf16[2,512,1,64]{1,3,2,0:T(8,128)(2,1)S(1)}, bf16[2,512,1,64]{1,3,2,0:T(8,128)(2,1)}, u32[]{:S(2)}) copy-start(bf16[2,512,1,64]{1,3,2,0:T(8,128)(2,1)} %param.4) | copy-start | bytes 393220
  2.0 14.6 %collective-permute-start.4 = (bf16[2,2,64,512]{3,2,1,0:T(8,128)(2,1)S(1)}, bf16[2,2,64,512]{3,2,1,0:T(8,128)(2,1)S(1)}, u32[]{:S(2)}, u32[]{:S(2)}) collective-permute-start(bf16[2,2,64,512]{3,2,1,0:T(8,128)(2,1)S(1)} %shard_map.38.refs_8_.refs_0_), channel_id=1, source_target_pairs={{0,24},{1,17},{2,26},{3,19},{4,28},{5,21},{6,30},{7,23},{8,16},{9,... | collective-permute-start | bytes 786440 | tf_op jit(solution)/shard_map/ppermute | solution.py:148
  6.7 3.5 %copy-start.1 = (s32[8,16]{1,0:T(8,128)S(1)}, s32[8,16]{1,0:T(8,128)}, u32[]{:S(2)}) copy-start(s32[8,16]{1,0:T(8,128)} %live.1) | copy-start | bytes 1540
  6.8 12.0 %collective-permute-start.2 = (bf16[1,4,2,64,512]{4,3,2,1,0:T(8,128)(2,1)S(1)}, bf16[1,4,2,64,512]{4,3,2,1,0:T(8,128)(2,1)S(1)}, u32[]{:S(2)}, u32[]{:S(2)}) collective-permute-start(bf16[1,4,2,64,512]{4,3,2,1,0:T(8,128)(2,1)S(1)} %get-tuple-element.21), channel_id=1, source_target_pairs={{0,5},{1,2},{2,7},{3,0},{4,1},{5,6},{6,3},{7,4},{8,13},{9,10},{10,... | collective-permute-start | bytes 1572872 | tf_op jit(solution)/shard_map/ppermute | solution.py:148
  7.1 9.0 %collective-permute-start.5 = (bf16[1,2,64,512]{3,2,1,0:T(8,128)(2,1)S(1)}, bf16[1,2,64,512]{3,2,1,0:T(8,128)(2,1)S(1)}, u32[]{:S(2)}, u32[]{:S(2)}) collective-permute-start(bf16[1,2,64,512]{3,2,1,0:T(8,128)(2,1)S(1)} %bitcast.10), channel_id=1, source_target_pairs={{0,8},{1,9},{2,10},{3,11},{4,12},{5,13},{6,14},{7,15},{8,0},{9,1},... | collective-permute-start | bytes 393224 | tf_op jit(solution)/shard_map/ppermute | solution.py:148
  8.7 13.9 %collective-permute-start = (bf16[1,4,2,64,512]{4,3,2,1,0:T(8,128)(2,1)S(1)}, bf16[1,4,2,64,512]{4,3,2,1,0:T(8,128)(2,1)S(1)}, u32[]{:S(2)}, u32[]{:S(2)}) collective-permute-start(bf16[1,4,2,64,512]{4,3,2,1,0:T(8,128)(2,1)S(1)} %get-tuple-element.21), channel_id=1, source_target_pairs={{0,1},{1,0},{2,3},{3,2},{4,5},{5,4},{6,7},{7,6},{8,9},{9,8},{10,11... | collective-permute-start | bytes 1572872 | tf_op jit(solution)/shard_map/ppermute | solution.py:144
  8.7 12.4 %collective-permute-start.1 = (bf16[1,4,2,64,512]{4,3,2,1,0:T(8,128)(2,1)S(1)}, bf16[1,4,2,64,512]{4,3,2,1,0:T(8,128)(2,1)S(1)}, u32[]{:S(2)}, u32[]{:S(2)}) collective-permute-start(bf16[1,4,2,64,512]{4,3,2,1,0:T(8,128)(2,1)S(1)} %get-tuple-element.22.refs_0_), channel_id=1, source_target_pairs={{0,2},{1,5},{2,0},{3,7},{4,6},{5,1},{6,4},{7,3},{8,10},{9,13},{10,... | collective-permute-start | bytes 1572872 | tf_op jit(solution)/shard_map/ppermute | solution.py:148
  16.1 1.5 %collective-permute-start.7 = (bf16[1,2,64,512]{3,2,1,0:T(8,128)(2,1)S(1)}, bf16[1,2,64,512]{3,2,1,0:T(8,128)(2,1)S(1)}, u32[]{:S(2)}, u32[]{:S(2)}) collective-permute-start(bf16[1,2,64,512]{3,2,1,0:T(8,128)(2,1)S(1)} %collective-permute-done.5.refs_2_.refs_6_.refs_1_), channel_id=1, source_target_pairs={{0,1},{1,0},{2,3},{3,2},{4,5},{5,4},{6,7},{7,6},{8,9},{9,8},{10,11... | collective-permute-start | bytes 393224 | tf_op jit(solution)/shard_map/ppermute | solution.py:144
  16.6 6.0 %collective-permute-start.6 = (bf16[2,2,64,512]{3,2,1,0:T(8,128)(2,1)S(1)}, bf16[2,2,64,512]{3,2,1,0:T(8,128)(2,1)S(1)}, u32[]{:S(2)}, u32[]{:S(2)}) collective-permute-start(bf16[2,2,64,512]{3,2,1,0:T(8,128)(2,1)S(1)} %shard_map.39.refs_4_), channel_id=1, source_target_pairs={{0,1},{1,0},{2,3},{3,2},{4,5},{5,4},{6,7},{7,6},{8,9},{9,8},{10,11... | collective-permute-start | bytes 786440 | tf_op jit(solution)/shard_map/ppermute | solution.py:144
  17.6 8.3 %collective-permute-start.10 = (bf16[2,2,64,512]{3,2,1,0:T(8,128)(2,1)S(1)}, bf16[2,2,64,512]{3,2,1,0:T(8,128)(2,1)S(1)}, u32[]{:S(2)}, u32[]{:S(2)}) collective-permute-start(bf16[2,2,64,512]{3,2,1,0:T(8,128)(2,1)S(1)} %shard_map.39.refs_4_), channel_id=1, source_target_pairs={{0,3},{1,4},{2,1},{3,6},{4,7},{5,0},{6,5},{7,2},{8,11},{9,12},{10,... | collective-permute-start | bytes 786440 | tf_op jit(solution)/shard_map/ppermute | solution.py:148
  18.8 8.0 %collective-permute-start.9 = (bf16[2,2,64,512]{3,2,1,0:T(8,128)(2,1)S(1)}, bf16[2,2,64,512]{3,2,1,0:T(8,128)(2,1)S(1)}, u32[]{:S(2)}, u32[]{:S(2)}) collective-permute-start(bf16[2,2,64,512]{3,2,1,0:T(8,128)(2,1)S(1)} %shard_map.39.refs_4_), channel_id=1, source_target_pairs={{0,4},{1,3},{2,6},{3,1},{4,0},{5,7},{6,2},{7,5},{8,12},{9,11},{10,... | collective-permute-start | bytes 786440 | tf_op jit(solution)/shard_map/ppermute | solution.py:148
  21.1 11.9 %collective-permute-start.15 = (bf16[4,2,64,512]{3,2,1,0:T(8,128)(2,1)S(1)}, bf16[4,2,64,512]{3,2,1,0:T(8,128)(2,1)S(1)}, u32[]{:S(2)}, u32[]{:S(2)}) collective-permute-start(bf16[4,2,64,512]{3,2,1,0:T(8,128)(2,1)S(1)} %shard_map.42), channel_id=1, source_target_pairs={{0,4},{1,3},{2,6},{3,1},{4,0},{5,7},{6,2},{7,5},{8,12},{9,11},{10,... | collective-permute-start | bytes 1572872 | tf_op jit(solution)/shard_map/ppermute | solution.py:148
  23.3 8.4 %collective-permute-start.12 = (bf16[4,64,128]{2,1,0:T(8,128)(2,1)S(1)}, bf16[4,64,128]{2,1,0:T(8,128)(2,1)S(1)}, u32[]{:S(2)}, u32[]{:S(2)}) collective-permute-start(bf16[4,64,128]{2,1,0:T(8,128)(2,1)S(1)} %get-tuple-element.15), channel_id=1, source_target_pairs={{0,16},{1,25},{2,18},{3,27},{4,20},{5,29},{6,22},{7,31},{8,24},{9,... | collective-permute-start | bytes 196616 | tf_op jit(solution)/shard_map/ppermute | solution.py:148
  24.7 8.2 %collective-permute-start.8 = (bf16[4,64,128]{2,1,0:T(8,128)(2,1)S(1)}, bf16[4,64,128]{2,1,0:T(8,128)(2,1)S(1)}, u32[]{:S(2)}, u32[]{:S(2)}) collective-permute-start(bf16[4,64,128]{2,1,0:T(8,128)(2,1)S(1)} %get-tuple-element.13.refs_6_), channel_id=1, source_target_pairs={{0,24},{1,17},{2,26},{3,19},{4,28},{5,21},{6,30},{7,23},{8,16},{9,... | collective-permute-start | bytes 196616 | tf_op jit(solution)/shard_map/ppermute | solution.py:148
  27.6 8.5 %collective-permute-start.11 = (bf16[4,64,128]{2,1,0:T(8,128)(2,1)S(1)}, bf16[4,64,128]{2,1,0:T(8,128)(2,1)S(1)}, u32[]{:S(2)}, u32[]{:S(2)}) collective-permute-start(bf16[4,64,128]{2,1,0:T(8,128)(2,1)S(1)} %get-tuple-element.14.refs_5_), channel_id=1, source_target_pairs={{0,28},{1,19},{2,30},{3,17},{4,24},{5,23},{6,26},{7,21},{8,20},{9,... | collective-permute-start | bytes 196616 | tf_op jit(solution)/shard_map/ppermute | solution.py:148
  31.7 6.6 %collective-permute-start.13 = (bf16[4,64,128]{2,1,0:T(8,128)(2,1)S(1)}, bf16[4,64,128]{2,1,0:T(8,128)(2,1)S(1)}, u32[]{:S(2)}, u32[]{:S(2)}) collective-permute-start(bf16[4,64,128]{2,1,0:T(8,128)(2,1)S(1)} %get-tuple-element.16), channel_id=1, source_target_pairs={{0,20},{1,27},{2,22},{3,25},{4,16},{5,31},{6,18},{7,29},{8,28},{9,... | collective-permute-start | bytes 196616 | tf_op jit(solution)/shard_map/ppermute | solution.py:148
  31.7 6.6 %collective-permute-start.14 = (bf16[4,64,128]{2,1,0:T(8,128)(2,1)S(1)}, bf16[4,64,128]{2,1,0:T(8,128)(2,1)S(1)}, u32[]{:S(2)}, u32[]{:S(2)}) collective-permute-start(bf16[4,64,128]{2,1,0:T(8,128)(2,1)S(1)} %get-tuple-element.17), channel_id=1, source_target_pairs={{0,8},{1,9},{2,10},{3,11},{4,12},{5,13},{6,14},{7,15},{8,0},{9,1},... | collective-permute-start | bytes 196616 | tf_op jit(solution)/shard_map/ppermute | solution.py:148
  33.8 6.1 %collective-permute-start.16 = (bf16[4,64,128]{2,1,0:T(8,128)(2,1)S(1)}, bf16[4,64,128]{2,1,0:T(8,128)(2,1)S(1)}, u32[]{:S(2)}, u32[]{:S(2)}) collective-permute-start(bf16[4,64,128]{2,1,0:T(8,128)(2,1)S(1)} %get-tuple-element.18), channel_id=1, source_target_pairs={{0,12},{1,11},{2,14},{3,9},{4,8},{5,15},{6,10},{7,13},{8,4},{9,3},... | collective-permute-start | bytes 196616 | tf_op jit(solution)/shard_map/ppermute | solution.py:148
  35.3 4.7 %collective-permute-start.17 = (bf16[4,64,128]{2,1,0:T(8,128)(2,1)S(1)}, bf16[4,64,128]{2,1,0:T(8,128)(2,1)S(1)}, u32[]{:S(2)}, u32[]{:S(2)}) collective-permute-start(bf16[4,64,128]{2,1,0:T(8,128)(2,1)S(1)} %get-tuple-element.20), channel_id=1, source_target_pairs={{0,4},{1,3},{2,6},{3,1},{4,0},{5,7},{6,2},{7,5},{8,12},{9,11},{10,... | collective-permute-start | bytes 196616 | tf_op jit(solution)/shard_map/ppermute | solution.py:148

commit v8 on v7

--- a/solution.py
+++ b/solution.py
@@ -180,7 +180,7 @@
     some = [over_tr(own_w, lambda c, z=z: 4 * z) for z in split]
     whole = [over_tr(own_parts, lambda c, group=group: 4 * group[c]) for group in groups]
     their_a = [over_tr(value, pair_bit, e) for e, value in enumerate(given)]
-    whole = pack(whole, [masks, *some], 3)
+    whole = pack(whole, [masks], 3)
     some = some[0] if len(some) == 1 else pack(some)
     whole_side = [over_tr(whole, beside, e) for e in range(n_ct)]
     whole_rest = [over_ct(whole, e) for e in range(1, n_ct)]

time: 41 us -> 41 us (level)
  no operation moved by 1% of the time
where the time goes in v8:
time: 41 us; the launch traced here: 40.9 us
  starting transfers between devices  24.4 us (60%)
  waiting for transfers between devices  10.9 us (27%)
  Pallas kernels  3.95 us (10%)
  local copies, waits for them, and re-layouts  1.56 us (4%)
    ppermute x14, starting transfers between devices, over_tr(): return lax.ppermute(value, ('tr', 'ct'), pairs)  22.6 us
    ppermute x14, waiting for transfers between devices, over_tr(): return lax.ppermute(value, ('tr', 'ct'), pairs)  10.7 us
    pallas_call x7, Pallas kernels, call(): pl.pallas_call(kernel, out_shape=result if count is None else [result] *...  2.42 us
    ppermute x4, starting transfers between devices, over_ct(): return lax.ppermute(value, 'ct', [(c, c ^ e) for c in range(n_ct)])  1.78 us
    transpose x1, local copies, waits for them, and re-layouts, per_device(): jnp.transpose(amplitudes, (0, 2, 1, 3))  1.46 us
    pallas_call x1, Pallas kernels, per_device(): pl.pallas_call(functools.partial(place_kernel, shifts), out_shape=jax.Sha...  0.85 us
  transfers between devices with their start and end apart: 18, of which 7 were waited for; matrix products, arithmetic and copies ran while one was open for 4% of the time, Pallas kernels for 8%

profile of v8, /device:TPU:0, one launch (start us, length us, event | category | flops | bytes accessed | tf_op | source)
XLA Modules:
  0.0 40.9 jit_solution(10884192548650439331)
XLA Ops:
  0.0 0.5 %collective-permute-start.3 = (bf16[1,2,64,512]{3,2,1,0:T(8,128)(2,1)}, bf16[1,2,64,512]{3,2,1,0:T(8,128)(2,1)S(1)}, u32[]{:S(2)}, u32[]{:S(2)}) collective-permute-start(bf16[1,2,64,512]{3,2,1,0:T(8,128)(2,1)} %bitcast.8), channel_id=1, source_target_pairs={{0,1},{1,0},{2,3},{3,2},{4,5},{5,4},{6,7},{7,6},{8,9},{9,8},{10,11... | collective-permute-start | bytes 393224 | tf_op jit(solution)/shard_map/ppermute | solution.py:144
  0.5 0.0 copy-start
  0.5 1.5 %copy.4 = bf16[8,2,64,512]{3,2,1,0:T(8,128)(2,1)S(1)} copy(bf16[8,2,64,512]{3,1,2,0:T(2,128)(2,1)} %bitcast.12) | data formatting | bytes 2097152 | tf_op jit(solution)/shard_map/transpose | solution.py:175
  1.9 0.0 collective-permute-done.3.refs_1_
  1.9 0.0 copy-done
  2.0 4.7 %collective-permute-start.4 = (bf16[2,2,64,512]{3,2,1,0:T(8,128)(2,1)S(1)}, bf16[2,2,64,512]{3,2,1,0:T(8,128)(2,1)S(1)}, u32[]{:S(2)}, u32[]{:S(2)}) collective-permute-start(bf16[2,2,64,512]{3,2,1,0:T(8,128)(2,1)S(1)} %shard_map.38.refs_8_.refs_0_), channel_id=1, source_target_pairs={{0,24},{1,17},{2,26},{3,19},{4,28},{5,21},{6,30},{7,23},{8,16},{9,... | collective-permute-start | bytes 786440 | tf_op jit(solution)/shard_map/ppermute | solution.py:148
  6.7 0.0 copy-start.1
  6.7 0.1 constant_dynamic-slice_fusion
  6.8 0.3 collective-permute-start.2
  7.1 1.6 %collective-permute-start.6 = (bf16[1,2,64,512]{3,2,1,0:T(8,128)(2,1)S(1)}, bf16[1,2,64,512]{3,2,1,0:T(8,128)(2,1)S(1)}, u32[]{:S(2)}, u32[]{:S(2)}) collective-permute-start(bf16[1,2,64,512]{3,2,1,0:T(8,128)(2,1)S(1)} %bitcast.10), channel_id=1, source_target_pairs={{0,8},{1,9},{2,10},{3,11},{4,12},{5,13},{6,14},{7,15},{8,0},{9,1},... | collective-permute-start | bytes 393224 | tf_op jit(solution)/shard_map/ppermute | solution.py:148
  8.7 0.0 collective-permute-start
  8.7 1.5 %collective-permute-start.1 = (bf16[1,4,2,64,512]{4,3,2,1,0:T(8,128)(2,1)S(1)}, bf16[1,4,2,64,512]{4,3,2,1,0:T(8,128)(2,1)S(1)}, u32[]{:S(2)}, u32[]{:S(2)}) collective-permute-start(bf16[1,4,2,64,512]{4,3,2,1,0:T(8,128)(2,1)S(1)} %get-tuple-element.22.refs_0_), channel_id=1, source_target_pairs={{0,2},{1,5},{2,0},{3,7},{4,6},{5,1},{6,4},{7,3},{8,10},{9,13},{10,... | collective-permute-start | bytes 1572872 | tf_op jit(solution)/shard_map/ppermute | solution.py:148
  10.2 0.0 copy-done.1
  10.2 0.7 %shard_map.37.refs_1_.masks = f32[9,512]{1,0:T(8,128)S(1)} custom-call(s32[8,16]{1,0:T(8,128)S(1)} %copy-done.1), custom_call_target="tpu_custom_call" | custom-call | flops 1 | bytes 1 | tf_op jit(solution)/shard_map/pallas_call | solution.py:166
  10.9 5.3 %collective-permute-done.6.refs_6_.refs_1_ = bf16[1,2,64,512]{3,2,1,0:T(8,128)(2,1)S(1)} collective-permute-done((bf16[1,2,64,512]{3,2,1,0:T(8,128)(2,1)S(1)}, bf16[1,2,64,512]{3,2,1,0:T(8,128)(2,1)S(1)}, u32[]{:S(2)}, u32[]{:S(2)}) %collective-permute-start.6) | collective-permute-done | bytes 131104 | tf_op jit(solution)/shard_map/ppermute | solution.py:148
  16.1 0.5 %collective-permute-start.7 = (bf16[1,2,64,512]{3,2,1,0:T(8,128)(2,1)S(1)}, bf16[1,2,64,512]{3,2,1,0:T(8,128)(2,1)S(1)}, u32[]{:S(2)}, u32[]{:S(2)}) collective-permute-start(bf16[1,2,64,512]{3,2,1,0:T(8,128)(2,1)S(1)} %collective-permute-done.6.refs_6_.refs_1_), channel_id=1, source_target_pairs={{0,1},{1,0},{2,3},{3,2},{4,5},{5,4},{6,7},{7,6},{8,9},{9,8},{10,11... | collective-permute-start | bytes 393224 | tf_op jit(solution)/shard_map/ppermute | solution.py:144
  16.6 0.0 collective-permute-done.4.refs_0_
  16.6 0.9 %collective-permute-start.5 = (bf16[2,2,64,512]{3,2,1,0:T(8,128)(2,1)S(1)}, bf16[2,2,64,512]{3,2,1,0:T(8,128)(2,1)S(1)}, u32[]{:S(2)}, u32[]{:S(2)}) collective-permute-start(bf16[2,2,64,512]{3,2,1,0:T(8,128)(2,1)S(1)} %shard_map.39.refs_4_), channel_id=1, source_target_pairs={{0,1},{1,0},{2,3},{3,2},{4,5},{5,4},{6,7},{7,6},{8,9},{9,8},{10,11... | collective-permute-start | bytes 786440 | tf_op jit(solution)/shard_map/ppermute | solution.py:144
  17.5 0.1 collective-permute-done.7.refs_7_.refs_2_
  17.6 1.2 %collective-permute-start.10 = (bf16[2,2,64,512]{3,2,1,0:T(8,128)(2,1)S(1)}, bf16[2,2,64,512]{3,2,1,0:T(8,128)(2,1)S(1)}, u32[]{:S(2)}, u32[]{:S(2)}) collective-permute-start(bf16[2,2,64,512]{3,2,1,0:T(8,128)(2,1)S(1)} %shard_map.39.refs_4_), channel_id=1, source_target_pairs={{0,3},{1,4},{2,1},{3,6},{4,7},{5,0},{6,5},{7,2},{8,11},{9,12},{10,... | collective-permute-start | bytes 786440 | tf_op jit(solution)/shard_map/ppermute | solution.py:148
  18.8 0.0 collective-permute-done.2.refs_3_
  18.8 1.6 %collective-permute-start.9 = (bf16[2,2,64,512]{3,2,1,0:T(8,128)(2,1)S(1)}, bf16[2,2,64,512]{3,2,1,0:T(8,128)(2,1)S(1)}, u32[]{:S(2)}, u32[]{:S(2)}) collective-permute-start(bf16[2,2,64,512]{3,2,1,0:T(8,128)(2,1)S(1)} %shard_map.39.refs_4_), channel_id=1, source_target_pairs={{0,4},{1,3},{2,6},{3,1},{4,0},{5,7},{6,2},{7,5},{8,12},{9,11},{10,... | collective-permute-start | bytes 786440 | tf_op jit(solution)/shard_map/ppermute | solution.py:148
  20.4 0.7 %collective-permute-done.1.refs_2_ = bf16[1,4,2,64,512]{4,3,2,1,0:T(8,128)(2,1)S(1)} collective-permute-done((bf16[1,4,2,64,512]{4,3,2,1,0:T(8,128)(2,1)S(1)}, bf16[1,4,2,64,512]{4,3,2,1,0:T(8,128)(2,1)S(1)}, u32[]{:S(2)}, u32[]{:S(2)}) %collective-permute-start.1) | collective-permute-done | bytes 524320 | tf_op jit(solution)/shard_map/ppermute | solution.py:148
  21.1 1.5 %collective-permute-start.15 = (bf16[4,2,64,512]{3,2,1,0:T(8,128)(2,1)S(1)}, bf16[4,2,64,512]{3,2,1,0:T(8,128)(2,1)S(1)}, u32[]{:S(2)}, u32[]{:S(2)}) collective-permute-start(bf16[4,2,64,512]{3,2,1,0:T(8,128)(2,1)S(1)} %shard_map.42), channel_id=1, source_target_pairs={{0,4},{1,3},{2,6},{3,1},{4,0},{5,7},{6,2},{7,5},{8,12},{9,11},{10,... | collective-permute-start | bytes 1572872 | tf_op jit(solution)/shard_map/ppermute | solution.py:148
  22.6 0.0 collective-permute-done.refs_1_
  22.6 0.0 collective-permute-done.5.refs_5_
  22.6 0.7 %shard_map.40 = (bf16[4,64,128]{2,1,0:T(8,128)(2,1)S(1)}, bf16[4,64,128]{2,1,0:T(8,128)(2,1)S(1)}, bf16[4,64,128]{2,1,0:T(8,128)(2,1)S(1)}, bf16[4,64,128]{2,1,0:T(8,128)(2,1)S(1)}) custom-call(f32[9,512]{1,0:T(8,128)S(1)} %shard_map.37.refs_1_.masks, bf16[1,4,2,64,512]{4,3,2,1,0:T(8,128)(2,1)S(1)} %get-tuple-element.22.refs_0_, ...), custom_call_target="tpu_custom_call" | custom-call | flops 1 | bytes 1 | tf_op jit(solution)/shard_map/pallas_call | solution.py:152
  23.3 1.4 %collective-permute-start.12 = (bf16[4,64,128]{2,1,0:T(8,128)(2,1)S(1)}, bf16[4,64,128]{2,1,0:T(8,128)(2,1)S(1)}, u32[]{:S(2)}, u32[]{:S(2)}) collective-permute-start(bf16[4,64,128]{2,1,0:T(8,128)(2,1)S(1)} %get-tuple-element.15), channel_id=1, source_target_pairs={{0,16},{1,25},{2,18},{3,27},{4,20},{5,29},{6,22},{7,31},{8,24},{9,... | collective-permute-start | bytes 196616 | tf_op jit(solution)/shard_map/ppermute | solution.py:148
  24.7 1.1 %collective-permute-start.8 = (bf16[4,64,128]{2,1,0:T(8,128)(2,1)S(1)}, bf16[4,64,128]{2,1,0:T(8,128)(2,1)S(1)}, u32[]{:S(2)}, u32[]{:S(2)}) collective-permute-start(bf16[4,64,128]{2,1,0:T(8,128)(2,1)S(1)} %get-tuple-element.13.refs_6_), channel_id=1, source_target_pairs={{0,24},{1,17},{2,26},{3,19},{4,28},{5,21},{6,30},{7,23},{8,16},{9,... | collective-permute-start | bytes 196616 | tf_op jit(solution)/shard_map/ppermute | solution.py:148
  25.9 0.0 collective-permute-done.10.refs_5_
  25.9 0.9 %collective-permute-done.9.refs_4_ = bf16[2,2,64,512]{3,2,1,0:T(8,128)(2,1)S(1)} collective-permute-done((bf16[2,2,64,512]{3,2,1,0:T(8,128)(2,1)S(1)}, bf16[2,2,64,512]{3,2,1,0:T(8,128)(2,1)S(1)}, u32[]{:S(2)}, u32[]{:S(2)}) %collective-permute-start.9) | collective-permute-done | bytes 262176 | tf_op jit(solution)/shard_map/ppermute | solution.py:148
  26.8 0.8 %shard_map.41 = (bf16[4,64,128]{2,1,0:T(8,128)(2,1)S(1)}, bf16[4,64,128]{2,1,0:T(8,128)(2,1)S(1)}) custom-call(f32[9,512]{1,0:T(8,128)S(1)} %shard_map.37.refs_1_.masks, bf16[1,4,2,64,512]{4,3,2,1,0:T(8,128)(2,1)S(1)} %get-tuple-element.22.refs_0_, bf16[1,4,2,64,512]{4,3,2,1,0:T(8,128)(2,1)S(1)} %collective-permute-done.refs_1_, ...), custom_call_target="tpu_custom_call" | custom-call | flops 9000000512 | bytes 1 | tf_op jit(solution)/shard_map/pallas_call | solution.py:152
  27.6 4.2 %collective-permute-start.11 = (bf16[4,64,128]{2,1,0:T(8,128)(2,1)S(1)}, bf16[4,64,128]{2,1,0:T(8,128)(2,1)S(1)}, u32[]{:S(2)}, u32[]{:S(2)}) collective-permute-start(bf16[4,64,128]{2,1,0:T(8,128)(2,1)S(1)} %get-tuple-element.14.refs_5_), channel_id=1, source_target_pairs={{0,28},{1,19},{2,30},{3,17},{4,24},{5,23},{6,26},{7,21},{8,20},{9,... | collective-permute-start | bytes 196616 | tf_op jit(solution)/shard_map/ppermute | solution.py:148
  31.7 0.0 collective-permute-start.13
  31.7 0.0 collective-permute-done.12.refs_7_.refs_2_
  31.7 1.2 %collective-permute-start.14 = (bf16[4,64,128]{2,1,0:T(8,128)(2,1)S(1)}, bf16[4,64,128]{2,1,0:T(8,128)(2,1)S(1)}, u32[]{:S(2)}, u32[]{:S(2)}) collective-permute-start(bf16[4,64,128]{2,1,0:T(8,128)(2,1)S(1)} %get-tuple-element.17), channel_id=1, source_target_pairs={{0,8},{1,9},{2,10},{3,11},{4,12},{5,13},{6,14},{7,15},{8,0},{9,1},... | collective-permute-start | bytes 196616 | tf_op jit(solution)/shard_map/ppermute | solution.py:148
  32.9 0.0 collective-permute-done.8.refs_6_.refs_0_
  32.9 0.0 collective-permute-done.15.refs_4_
  32.9 0.8 %shard_map.43 = (bf16[4,64,128]{2,1,0:T(8,128)(2,1)S(1)}, bf16[4,64,128]{2,1,0:T(8,128)(2,1)S(1)}) custom-call(f32[9,512]{1,0:T(8,128)S(1)} %shard_map.37.refs_1_.masks, bf16[1,4,2,64,512]{4,3,2,1,0:T(8,128)(2,1)S(1)} %get-tuple-element.22.refs_0_, bf16[1,4,2,64,512]{4,3,2,1,0:T(8,128)(2,1)S(1)} %collective-permute-done.refs_1_, ...), custom_call_target="tpu_custom_call" | custom-call | flops 8000000000 | bytes 1 | tf_op jit(solution)/shard_map/pallas_call | solution.py:152
  33.8 1.5 %collective-permute-start.16 = (bf16[4,64,128]{2,1,0:T(8,128)(2,1)S(1)}, bf16[4,64,128]{2,1,0:T(8,128)(2,1)S(1)}, u32[]{:S(2)}, u32[]{:S(2)}) collective-permute-start(bf16[4,64,128]{2,1,0:T(8,128)(2,1)S(1)} %get-tuple-element.18), channel_id=1, source_target_pairs={{0,12},{1,11},{2,14},{3,9},{4,8},{5,15},{6,10},{7,13},{8,4},{9,3},... | collective-permute-start | bytes 196616 | tf_op jit(solution)/shard_map/ppermute | solution.py:148
  35.3 0.8 %collective-permute-start.17 = (bf16[4,64,128]{2,1,0:T(8,128)(2,1)S(1)}, bf16[4,64,128]{2,1,0:T(8,128)(2,1)S(1)}, u32[]{:S(2)}, u32[]{:S(2)}) collective-permute-start(bf16[4,64,128]{2,1,0:T(8,128)(2,1)S(1)} %get-tuple-element.20), channel_id=1, source_target_pairs={{0,4},{1,3},{2,6},{3,1},{4,0},{5,7},{6,2},{7,5},{8,12},{9,11},{10,... | collective-permute-start | bytes 196616 | tf_op jit(solution)/shard_map/ppermute | solution.py:148
  36.1 0.0 collective-permute-done.11.refs_0_.refs_1_
  36.1 2.2 %collective-permute-done.13.refs_1_.refs_3_ = bf16[4,64,128]{2,1,0:T(8,128)(2,1)S(1)} collective-permute-done((bf16[4,64,128]{2,1,0:T(8,128)(2,1)S(1)}, bf16[4,64,128]{2,1,0:T(8,128)(2,1)S(1)}, u32[]{:S(2)}, u32[]{:S(2)}) %collective-permute-start.13) | collective-permute-done | bytes 65568 | tf_op jit(solution)/shard_map/ppermute | solution.py:148
  38.4 0.0 collective-permute-done.14.refs_4_
  38.4 1.5 %collective-permute-done.16.refs_5_ = bf16[4,64,128]{2,1,0:T(8,128)(2,1)S(1)} collective-permute-done((bf16[4,64,128]{2,1,0:T(8,128)(2,1)S(1)}, bf16[4,64,128]{2,1,0:T(8,128)(2,1)S(1)}, u32[]{:S(2)}, u32[]{:S(2)}) %collective-permute-start.16) | collective-permute-done | bytes 65568 | tf_op jit(solution)/shard_map/ppermute | solution.py:148
  39.8 0.2 collective-permute-done.17.refs_7_
  40.0 0.8 %shard_map.45 = bf16[4,64,1024]{2,1,0:T(8,128)(2,1)} custom-call(bf16[4,64,128]{2,1,0:T(8,128)(2,1)S(1)} %collective-permute-done.8.refs_6_.refs_0_, bf16[4,64,128]{2,1,0:T(8,128)(2,1)S(1)} %collective-permute-done.11.refs_0_.refs_1_, bf16[4,64,128]{2,1,0:T(8,128)(2,1)S(1)} %collective-permute-done.12.refs_7_.refs_2_, ...), custom_call_target="tpu_custom_call" | custom-call | flops 1 | bytes 1 | tf_op jit(solution)/shard_map/pallas_call | solution.py:213
  (4 shorter events, 0.1 us)
Async XLA Ops:
  0.0 1.9 %collective-permute-start.3 = (bf16[1,2,64,512]{3,2,1,0:T(8,128)(2,1)}, bf16[1,2,64,512]{3,2,1,0:T(8,128)(2,1)S(1)}, u32[]{:S(2)}, u32[]{:S(2)}) collective-permute-start(bf16[1,2,64,512]{3,2,1,0:T(8,128)(2,1)} %bitcast.8), channel_id=1, source_target_pairs={{0,1},{1,0},{2,3},{3,2},{4,5},{5,4},{6,7},{7,6},{8,9},{9,8},{10,11... | collective-permute-start | bytes 393224 | tf_op jit(solution)/shard_map/ppermute | solution.py:144
  0.5 1.5 %copy-start = (bf16[2,512,1,64]{1,3,2,0:T(8,128)(2,1)S(1)}, bf16[2,512,1,64]{1,3,2,0:T(8,128)(2,1)}, u32[]{:S(2)}) copy-start(bf16[2,512,1,64]{1,3,2,0:T(8,128)(2,1)} %param.4) | copy-start | bytes 393220
  2.0 14.6 %collective-permute-start.4 = (bf16[2,2,64,512]{3,2,1,0:T(8,128)(2,1)S(1)}, bf16[2,2,64,512]{3,2,1,0:T(8,128)(2,1)S(1)}, u32[]{:S(2)}, u32[]{:S(2)}) collective-permute-start(bf16[2,2,64,512]{3,2,1,0:T(8,128)(2,1)S(1)} %shard_map.38.refs_8_.refs_0_), channel_id=1, source_target_pairs={{0,24},{1,17},{2,26},{3,19},{4,28},{5,21},{6,30},{7,23},{8,16},{9,... | collective-permute-start | bytes 786440 | tf_op jit(solution)/shard_map/ppermute | solution.py:148
  6.7 3.5 %copy-start.1 = (s32[8,16]{1,0:T(8,128)S(1)}, s32[8,16]{1,0:T(8,128)}, u32[]{:S(2)}) copy-start(s32[8,16]{1,0:T(8,128)} %live.1) | copy-start | bytes 1540
  6.8 12.0 %collective-permute-start.2 = (bf16[1,4,2,64,512]{4,3,2,1,0:T(8,128)(2,1)S(1)}, bf16[1,4,2,64,512]{4,3,2,1,0:T(8,128)(2,1)S(1)}, u32[]{:S(2)}, u32[]{:S(2)}) collective-permute-start(bf16[1,4,2,64,512]{4,3,2,1,0:T(8,128)(2,1)S(1)} %get-tuple-element.21), channel_id=1, source_target_pairs={{0,5},{1,2},{2,7},{3,0},{4,1},{5,6},{6,3},{7,4},{8,13},{9,10},{10,... | collective-permute-start | bytes 1572872 | tf_op jit(solution)/shard_map/ppermute | solution.py:148
  7.1 9.0 %collective-permute-start.6 = (bf16[1,2,64,512]{3,2,1,0:T(8,128)(2,1)S(1)}, bf16[1,2,64,512]{3,2,1,0:T(8,128)(2,1)S(1)}, u32[]{:S(2)}, u32[]{:S(2)}) collective-permute-start(bf16[1,2,64,512]{3,2,1,0:T(8,128)(2,1)S(1)} %bitcast.10), channel_id=1, source_target_pairs={{0,8},{1,9},{2,10},{3,11},{4,12},{5,13},{6,14},{7,15},{8,0},{9,1},... | collective-permute-start | bytes 393224 | tf_op jit(solution)/shard_map/ppermute | solution.py:148
  8.7 13.9 %collective-permute-start = (bf16[1,4,2,64,512]{4,3,2,1,0:T(8,128)(2,1)S(1)}, bf16[1,4,2,64,512]{4,3,2,1,0:T(8,128)(2,1)S(1)}, u32[]{:S(2)}, u32[]{:S(2)}) collective-permute-start(bf16[1,4,2,64,512]{4,3,2,1,0:T(8,128)(2,1)S(1)} %get-tuple-element.21), channel_id=1, source_target_pairs={{0,1},{1,0},{2,3},{3,2},{4,5},{5,4},{6,7},{7,6},{8,9},{9,8},{10,11... | collective-permute-start | bytes 1572872 | tf_op jit(solution)/shard_map/ppermute | solution.py:144
  8.7 12.4 %collective-permute-start.1 = (bf16[1,4,2,64,512]{4,3,2,1,0:T(8,128)(2,1)S(1)}, bf16[1,4,2,64,512]{4,3,2,1,0:T(8,128)(2,1)S(1)}, u32[]{:S(2)}, u32[]{:S(2)}) collective-permute-start(bf16[1,4,2,64,512]{4,3,2,1,0:T(8,128)(2,1)S(1)} %get-tuple-element.22.refs_0_), channel_id=1, source_target_pairs={{0,2},{1,5},{2,0},{3,7},{4,6},{5,1},{6,4},{7,3},{8,10},{9,13},{10,... | collective-permute-start | bytes 1572872 | tf_op jit(solution)/shard_map/ppermute | solution.py:148
  16.1 1.5 %collective-permute-start.7 = (bf16[1,2,64,512]{3,2,1,0:T(8,128)(2,1)S(1)}, bf16[1,2,64,512]{3,2,1,0:T(8,128)(2,1)S(1)}, u32[]{:S(2)}, u32[]{:S(2)}) collective-permute-start(bf16[1,2,64,512]{3,2,1,0:T(8,128)(2,1)S(1)} %collective-permute-done.6.refs_6_.refs_1_), channel_id=1, source_target_pairs={{0,1},{1,0},{2,3},{3,2},{4,5},{5,4},{6,7},{7,6},{8,9},{9,8},{10,11... | collective-permute-start | bytes 393224 | tf_op jit(solution)/shard_map/ppermute | solution.py:144
  16.6 6.0 %collective-permute-start.5 = (bf16[2,2,64,512]{3,2,1,0:T(8,128)(2,1)S(1)}, bf16[2,2,64,512]{3,2,1,0:T(8,128)(2,1)S(1)}, u32[]{:S(2)}, u32[]{:S(2)}) collective-permute-start(bf16[2,2,64,512]{3,2,1,0:T(8,128)(2,1)S(1)} %shard_map.39.refs_4_), channel_id=1, source_target_pairs={{0,1},{1,0},{2,3},{3,2},{4,5},{5,4},{6,7},{7,6},{8,9},{9,8},{10,11... | collective-permute-start | bytes 786440 | tf_op jit(solution)/shard_map/ppermute | solution.py:144
  17.6 8.3 %collective-permute-start.10 = (bf16[2,2,64,512]{3,2,1,0:T(8,128)(2,1)S(1)}, bf16[2,2,64,512]{3,2,1,0:T(8,128)(2,1)S(1)}, u32[]{:S(2)}, u32[]{:S(2)}) collective-permute-start(bf16[2,2,64,512]{3,2,1,0:T(8,128)(2,1)S(1)} %shard_map.39.refs_4_), channel_id=1, source_target_pairs={{0,3},{1,4},{2,1},{3,6},{4,7},{5,0},{6,5},{7,2},{8,11},{9,12},{10,... | collective-permute-start | bytes 786440 | tf_op jit(solution)/shard_map/ppermute | solution.py:148
  18.8 8.0 %collective-permute-start.9 = (bf16[2,2,64,512]{3,2,1,0:T(8,128)(2,1)S(1)}, bf16[2,2,64,512]{3,2,1,0:T(8,128)(2,1)S(1)}, u32[]{:S(2)}, u32[]{:S(2)}) collective-permute-start(bf16[2,2,64,512]{3,2,1,0:T(8,128)(2,1)S(1)} %shard_map.39.refs_4_), channel_id=1, source_target_pairs={{0,4},{1,3},{2,6},{3,1},{4,0},{5,7},{6,2},{7,5},{8,12},{9,11},{10,... | collective-permute-start | bytes 786440 | tf_op jit(solution)/shard_map/ppermute | solution.py:148
  21.1 11.9 %collective-permute-start.15 = (bf16[4,2,64,512]{3,2,1,0:T(8,128)(2,1)S(1)}, bf16[4,2,64,512]{3,2,1,0:T(8,128)(2,1)S(1)}, u32[]{:S(2)}, u32[]{:S(2)}) collective-permute-start(bf16[4,2,64,512]{3,2,1,0:T(8,128)(2,1)S(1)} %shard_map.42), channel_id=1, source_target_pairs={{0,4},{1,3},{2,6},{3,1},{4,0},{5,7},{6,2},{7,5},{8,12},{9,11},{10,... | collective-permute-start | bytes 1572872 | tf_op jit(solution)/shard_map/ppermute | solution.py:148
  23.3 8.4 %collective-permute-start.12 = (bf16[4,64,128]{2,1,0:T(8,128)(2,1)S(1)}, bf16[4,64,128]{2,1,0:T(8,128)(2,1)S(1)}, u32[]{:S(2)}, u32[]{:S(2)}) collective-permute-start(bf16[4,64,128]{2,1,0:T(8,128)(2,1)S(1)} %get-tuple-element.15), channel_id=1, source_target_pairs={{0,16},{1,25},{2,18},{3,27},{4,20},{5,29},{6,22},{7,31},{8,24},{9,... | collective-permute-start | bytes 196616 | tf_op jit(solution)/shard_map/ppermute | solution.py:148
  24.7 8.2 %collective-permute-start.8 = (bf16[4,64,128]{2,1,0:T(8,128)(2,1)S(1)}, bf16[4,64,128]{2,1,0:T(8,128)(2,1)S(1)}, u32[]{:S(2)}, u32[]{:S(2)}) collective-permute-start(bf16[4,64,128]{2,1,0:T(8,128)(2,1)S(1)} %get-tuple-element.13.refs_6_), channel_id=1, source_target_pairs={{0,24},{1,17},{2,26},{3,19},{4,28},{5,21},{6,30},{7,23},{8,16},{9,... | collective-permute-start | bytes 196616 | tf_op jit(solution)/shard_map/ppermute | solution.py:148
  27.6 8.5 %collective-permute-start.11 = (bf16[4,64,128]{2,1,0:T(8,128)(2,1)S(1)}, bf16[4,64,128]{2,1,0:T(8,128)(2,1)S(1)}, u32[]{:S(2)}, u32[]{:S(2)}) collective-permute-start(bf16[4,64,128]{2,1,0:T(8,128)(2,1)S(1)} %get-tuple-element.14.refs_5_), channel_id=1, source_target_pairs={{0,28},{1,19},{2,30},{3,17},{4,24},{5,23},{6,26},{7,21},{8,20},{9,... | collective-permute-start | bytes 196616 | tf_op jit(solution)/shard_map/ppermute | solution.py:148
  31.7 6.6 %collective-permute-start.13 = (bf16[4,64,128]{2,1,0:T(8,128)(2,1)S(1)}, bf16[4,64,128]{2,1,0:T(8,128)(2,1)S(1)}, u32[]{:S(2)}, u32[]{:S(2)}) collective-permute-start(bf16[4,64,128]{2,1,0:T(8,128)(2,1)S(1)} %get-tuple-element.16), channel_id=1, source_target_pairs={{0,20},{1,27},{2,22},{3,25},{4,16},{5,31},{6,18},{7,29},{8,28},{9,... | collective-permute-start | bytes 196616 | tf_op jit(solution)/shard_map/ppermute | solution.py:148
  31.7 6.6 %collective-permute-start.14 = (bf16[4,64,128]{2,1,0:T(8,128)(2,1)S(1)}, bf16[4,64,128]{2,1,0:T(8,128)(2,1)S(1)}, u32[]{:S(2)}, u32[]{:S(2)}) collective-permute-start(bf16[4,64,128]{2,1,0:T(8,128)(2,1)S(1)} %get-tuple-element.17), channel_id=1, source_target_pairs={{0,8},{1,9},{2,10},{3,11},{4,12},{5,13},{6,14},{7,15},{8,0},{9,1},... | collective-permute-start | bytes 196616 | tf_op jit(solution)/shard_map/ppermute | solution.py:148
  33.8 6.1 %collective-permute-start.16 = (bf16[4,64,128]{2,1,0:T(8,128)(2,1)S(1)}, bf16[4,64,128]{2,1,0:T(8,128)(2,1)S(1)}, u32[]{:S(2)}, u32[]{:S(2)}) collective-permute-start(bf16[4,64,128]{2,1,0:T(8,128)(2,1)S(1)} %get-tuple-element.18), channel_id=1, source_target_pairs={{0,12},{1,11},{2,14},{3,9},{4,8},{5,15},{6,10},{7,13},{8,4},{9,3},... | collective-permute-start | bytes 196616 | tf_op jit(solution)/shard_map/ppermute | solution.py:148
  35.3 4.7 %collective-permute-start.17 = (bf16[4,64,128]{2,1,0:T(8,128)(2,1)S(1)}, bf16[4,64,128]{2,1,0:T(8,128)(2,1)S(1)}, u32[]{:S(2)}, u32[]{:S(2)}) collective-permute-start(bf16[4,64,128]{2,1,0:T(8,128)(2,1)S(1)} %get-tuple-element.20), channel_id=1, source_target_pairs={{0,4},{1,3},{2,6},{3,1},{4,0},{5,7},{6,2},{7,5},{8,12},{9,11},{10,... | collective-permute-start | bytes 196616 | tf_op jit(solution)/shard_map/ppermute | solution.py:148
